TPU v7x, 1024 devices: a whole 4x8x16 slice. The times are simulated.
1024 devices in a mesh: inner: 16 (over z), outer: 16 (over y, core), tensor: 4 (over x).
Axes of the slice: x: 4, y: 8, z: 16, core: 2. Of those that a mesh axis runs over, the one named last changes fastest.
Arguments:
- activations: bfloat16 [98304, 14848], P(('inner', 'outer'), 'tensor'), may hold values from -6 to 6
- out_grad: bfloat16 [98304, 1024], P(('inner', 'outer', 'tensor')), may hold values from -0.078125 to 0.078125
Outputs:
- weight_grad: float32 [1024, 14848], P(('inner', 'outer'), 'tensor')
All inputs are finite; a program needn't handle non-finite values.
Results may differ from a plain program's by a relative error of at most 0.012.
Values may be sent and summed in bfloat16 or wider, within the bound.
No kernel may reach another device: no remote copies, remote signals or barrier semaphores. Data moves between devices by JAX's collectives and lax.ppermute only.
A program may use at most 32 MiB of HBM per device.

v0:
```python
import jax
import jax.numpy as jnp
from jax import lax
from jax.sharding import PartitionSpec as P


def add_sources(received):
    return jnp.sum(received, axis=0, dtype=jnp.float32)


def on_device(activations, out_grad):
    width = activations.shape[1]
    columns = out_grad.shape[1]
    partial_sum = lax.dot_general(
        lax.all_gather(out_grad, "tensor", axis=0, tiled=True),
        activations,
        (((0,), (0,)), ((), ())),
        preferred_element_type=jnp.float32,
    )
    inner_count = lax.axis_size("inner")
    outer_count = lax.axis_size("outer")
    packed = partial_sum.astype(jnp.bfloat16).reshape(inner_count, columns // inner_count, width)
    first = add_sources(lax.all_to_all(packed, "inner", split_axis=0, concat_axis=0, tiled=True))
    block_cols = first.shape[0]
    packed_two = first.astype(jnp.bfloat16).reshape(outer_count, block_cols // outer_count, width)
    second = add_sources(
        lax.all_to_all(packed_two, "outer", split_axis=0, concat_axis=0, tiled=True)
    )
    return second


def solution(mesh):
    in_specs = (P(("inner", "outer"), "tensor"), P(("inner", "outer", "tensor"), None))
    out_specs = P(("inner", "outer"), "tensor")
    return jax.shard_map(
        on_device, mesh=mesh, in_specs=in_specs, out_specs=out_specs, check_vma=False
    )
```

profile of v0, /device:TPU:6, one launch (start us, length us, event | category | flops | bytes accessed | tf_op | source)
XLA Modules:
  0.0 395.6 jit_solution(681229685632920097)
XLA Ops:
  0.0 0.0 copy-start
  0.0 23.6 %all_gather.3 = bf16[384,1024]{1,0:T(8,128)(2,1)S(1)} all-gather(bf16[96,1024]{1,0:T(8,128)(2,1)} %param.3), channel_id=1, replica_groups=mesh['inner'=16,'outer'=16,'tensor'=4] {'tensor'}, dimensions={0}, use_global_device_ids=true | all-gather | bytes 983040 | tf_op jit(solution)/shard_map/all_gather | solution.py:15
  23.6 0.0 copy-done
  23.6 4.5 %convolution_convert_fusion = bf16[1024,3712]{1,0:T(8,128)(2,1)S(1)} fusion(bf16[384,1024]{1,0:T(8,128)(2,1)S(1)} %all_gather.3, bf16[384,3712]{1,0:T(8,128)(2,1)S(1)} %copy-done), kind=kOutput, calls=%fused_computation | convolution fusion | flops 2923036672 | bytes 11239424 | tf_op jit(solution)/shard_map/dot_general | solution.py:14
  28.1 338.4 %all_to_all.10 = bf16[16,64,3712]{2,1,0:T(8,128)(2,1)} all-to-all(bf16[16,64,3712]{2,1,0:T(8,128)(2,1)S(1)} %bitcast.3), channel_id=1, replica_groups=mesh['inner'=16,'outer'=16,'tensor'=4] {'inner'}, dimensions={0} | all-to-all | bytes 15204352 | tf_op jit(solution)/shard_map/all_to_all | solution.py:23
  366.5 5.1 %reduce_sum.21 = bf16[64,3712]{1,0:T(8,128)(2,1)} reduce(bf16[16,64,3712]{2,1,0:T(8,128)(2,1)} %all_to_all.10, bf16[]{:T(256)} %constant.2.clone.1), dimensions={0}, to_apply=%region_0.0 | reduce | flops 3563520 | bytes 8077314 | tf_op jit(solution)/shard_map/reduce_sum | solution.py:8
  371.6 1.1 reshape.7
  372.7 22.1 %all_to_all.11 = bf16[16,4,3712]{2,1,0:T(4,128)(2,1)S(1)} all-to-all(bf16[16,4,3712]{2,1,0:T(4,128)(2,1)S(1)} %reshape.7), channel_id=1, replica_groups=mesh['inner'=16,'outer'=16,'tensor'=4] {'outer'}, dimensions={0} | all-to-all | bytes 950272 | tf_op jit(solution)/shard_map/all_to_all | solution.py:27
  394.8 0.8 convert_reduce_fusion
Async XLA Ops:
  0.0 23.6 %copy-start = (bf16[384,3712]{1,0:T(8,128)(2,1)S(1)}, bf16[384,3712]{1,0:T(8,128)(2,1)}, u32[]{:S(2)}) copy-start(bf16[384,3712]{1,0:T(8,128)(2,1)} %param.2) | copy-start | bytes 8552452
where the time goes:
time: 401 us; the launch traced here: 396 us
  blocking collectives  384 us (96%)
  other arithmetic  5.91 us (1%)
  matrix products  4.49 us (1%)
    all_to_all x1, blocking collectives, on_device(): lax.all_to_all(packed, 'inner', split_axis=0, concat_axis=0, tiled=True)  338 us
    all_gather x1, blocking collectives, on_device(): lax.all_gather(out_grad, 'tensor', axis=0, tiled=True)  23.6 us
    all_to_all x1, blocking collectives, on_device(): lax.all_to_all(packed_two, 'outer', split_axis=0, concat_axis=0, tiled=True)  22.1 us

commit v1 on v0

v1 whole, which is shorter than its diff:
```python
import jax
import jax.numpy as jnp
from jax import lax
from jax.sharding import PartitionSpec as P

LANES = 128


def on_device(activations, out_grad):
    width = activations.shape[1]
    columns = out_grad.shape[1]
    owners = lax.axis_size("inner") * lax.axis_size("outer")
    rows = columns // owners
    groups = width // LANES
    partial_sum = lax.dot_general(
        lax.all_gather(out_grad, "tensor", axis=0, tiled=True),
        activations,
        (((0,), (0,)), ((), ())),
        preferred_element_type=jnp.float32,
    ).astype(jnp.bfloat16)
    packed = partial_sum.reshape(owners, rows, groups, LANES).transpose(0, 2, 1, 3)
    packed = packed.reshape(owners, groups * rows, LANES)
    total = lax.psum_scatter(packed, ("inner", "outer"), scatter_dimension=0, tiled=True)
    total = total.reshape(groups, rows, LANES).transpose(1, 0, 2)
    return total.reshape(rows, width).astype(jnp.float32)


def solution(mesh):
    in_specs = (P(("inner", "outer"), "tensor"), P(("inner", "outer", "tensor"), None))
    out_specs = P(("inner", "outer"), "tensor")
    return jax.shard_map(
        on_device, mesh=mesh, in_specs=in_specs, out_specs=out_specs, check_vma=False
    )
```

time: 401 us -> 450 us (1.12)
  waiting for transfers between devices: 0 us -> 368 us
  blocking collectives: 384 us -> 23.6 us
  local copies, waits for them, and re-layouts: 1.14 us -> 37.1 us
  between operations: 0.02 us -> 13.4 us
  other arithmetic: 5.91 us -> 0 us
    unnamed x0 -> x2, waiting for transfers between devices: none -> 368 us
    all_to_all x2 -> x0, blocking collectives: 360 us -> none  [the longest x1 338 us: on_device(): lax.all_to_all(packed, 'inner', split_axis=0, concat_axis=0, tiled=True)]
    reshape x1 -> x2, local copies, waits for them, and re-layouts: 1.14 us -> 24.2 us  [the longest x1 13 us: on_device(): partial_sum.reshape(owners, rows, groups, LANES).transpose(0, 2, 1, 3)]
    transpose x0 -> x1, local copies, waits for them, and re-layouts: none -> 11.5 us  [on_device(): partial_sum.reshape(owners, rows, groups, LANES).transpose(0, 2, 1, 3)]
    reduce_sum x2 -> x0, other arithmetic: 5.91 us -> none  [add_sources(): return jnp.sum(received, axis=0, dtype=jnp.float32)]
  transfers between devices with their start and end apart: 0 -> 1, of which waited for: 0 -> 1; matrix products, arithmetic and copies ran while one was open for 0% -> 0% of each run, Pallas kernels for 0% -> 0%
where the time goes in v1:
time: 450 us; the launch traced here: 449 us
  waiting for transfers between devices  368 us (82%)
  local copies, waits for them, and re-layouts  37.1 us (8%)
  blocking collectives  23.6 us (5%)
  between operations  13.4 us (3%)
  matrix products  6.36 us (1%)
    unnamed x2, waiting for transfers between devices  368 us
    all_gather x1, blocking collectives, on_device(): lax.all_gather(out_grad, 'tensor', axis=0, tiled=True)  23.6 us
    reshape x1, local copies, waits for them, and re-layouts, on_device(): partial_sum.reshape(owners, rows, groups, LANES).transpose(0, 2, 1, 3)  13 us
    transpose x1, local copies, waits for them, and re-layouts, on_device(): partial_sum.reshape(owners, rows, groups, LANES).transpose(0, 2, 1, 3)  11.5 us
    reshape x1, local copies, waits for them, and re-layouts, on_device(): packed = packed.reshape(owners, groups * rows, LANES)  11.2 us
  transfers between devices with their start and end apart: 1, of which 1 were waited for; matrix products, arithmetic and copies ran while one was open for 0% of the time, Pallas kernels for 0%

profile of v1, /device:TPU:6, one launch (start us, length us, event | category | flops | bytes accessed | tf_op | source)
XLA Modules:
  0.0 448.8 jit_solution(3361415370450352891)
XLA Ops:
  6.5 0.0 copy-start
  6.5 0.0 reduce-scatter.4.cloned.1.call-start
  6.5 23.6 %all_gather.3 = bf16[384,1024]{1,0:T(8,128)(2,1)S(1)} all-gather(bf16[96,1024]{1,0:T(8,128)(2,1)} %param.3), channel_id=1, replica_groups=mesh['inner'=16,'outer'=16,'tensor'=4] {'tensor'}, dimensions={0}, use_global_device_ids=true | all-gather | bytes 983040 | tf_op jit(solution)/shard_map/all_gather | solution.py:16
  30.1 0.0 copy-done
  30.1 6.4 %convolution_convert_fusion = bf16[1024,3712]{1,0:T(8,128)(2,1)} fusion(bf16[384,1024]{1,0:T(8,128)(2,1)S(1)} %all_gather.3, bf16[384,3712]{1,0:T(8,128)(2,1)S(1)} %copy-done), kind=kOutput, calls=%fused_computation | convolution fusion | flops 2923036672 | bytes 11239424 | tf_op jit(solution)/shard_map/dot_general | solution.py:15
  36.5 13.0 %reshape.12 = bf16[256,4,29,128]{3,2,1,0:T(8,128)(2,1)} reshape(bf16[1024,3712]{1,0:T(8,128)(2,1)} %convolution_convert_fusion) | data formatting | bytes 15204352 | tf_op jit(solution)/shard_map/reshape | solution.py:21
  49.5 11.5 %copy.4 = bf16[256,29,4,128]{3,0,2,1:T(8,128)(2,1)} copy(bf16[256,29,4,128]{3,1,2,0:T(8,128)(2,1)} %bitcast.8) | data formatting | bytes 15204352 | tf_op jit(solution)/shard_map/transpose | solution.py:21
  61.0 11.2 %copy.5 = bf16[256,116,128]{2,1,0:T(8,128)(2,1)} copy(bf16[256,116,128]{2,0,1:T(8,128)(2,1)} %bitcast.9) | data formatting | bytes 15204352 | tf_op jit(solution)/shard_map/reshape | solution.py:22
  72.1 0.0 reduce-scatter.4.cloned.1.call-update
  72.2 368.4 %reduce-scatter.4.cloned.1.call-done = bf16[1,116,128]{2,1,0:T(8,128)(2,1)} async-done(((bf16[256,116,128]{2,1,0:T(8,128)(2,1)}), bf16[1,116,128]{2,1,0:T(8,128)(2,1)}) %reduce-scatter.4.cloned.1.call-update) | async-done | bytes 29712
  440.6 1.4 reshape.15
Async XLA Ops:
  6.5 23.6 %copy-start = (bf16[384,3712]{1,0:T(8,128)(2,1)S(1)}, bf16[384,3712]{1,0:T(8,128)(2,1)}, u32[]{:S(2)}) copy-start(bf16[384,3712]{1,0:T(8,128)(2,1)} %param.2) | copy-start | bytes 8552452
  6.5 434.0 %reduce-scatter.4.cloned.1.call-start = ((), (), s32[]{:S(2)}) async-start(), calls=%async_computation.1 | async-start | bytes 7895040
Sparse Core Ops, SparseCore 0:
  72.3 368.2 reduce-scatter.3

commit v2 on v1

v2 whole, which is shorter than its diff:
```python
import jax
import jax.numpy as jnp
from jax import lax
from jax.sharding import Mesh, PartitionSpec as P

LANES = 128


def pairs(count):
    return [(i, i ^ 1) for i in range(count)]


def on_device(activations, out_grad):
    tokens, width = activations.shape
    core = lax.axis_index("core")
    first = core == 0
    half = -(-(width // LANES) // 2) * LANES
    low, high = activations[:, :half], activations[:, width - half :]
    received = lax.ppermute(jnp.where(first, high, low), "core", pairs(2))
    kept = jnp.where(first, low, high)
    grads = lax.all_gather(out_grad, "x", axis=0, tiled=True)
    grads_other = lax.ppermute(grads, "core", pairs(2))
    contract = (((0,), (0,)), ((), ()))
    partial_sum = lax.dot_general(
        jnp.concatenate([grads, grads_other], axis=0),
        jnp.concatenate([kept, received], axis=0),
        contract,
        preferred_element_type=jnp.float32,
    ).astype(jnp.bfloat16)
    over_inner = lax.psum_scatter(partial_sum, "inner", scatter_dimension=0, tiled=True)
    count = lax.axis_size("y")
    rows = over_inner.shape[0] // count
    blocks = lax.all_to_all(
        over_inner.reshape(count, rows, half), "y", split_axis=0, concat_axis=0, tiled=True
    )
    total = jnp.sum(blocks, axis=0, dtype=jnp.float32)
    mine = rows // 2
    top, bottom = total[:mine], total[mine:]
    own = jnp.where(first, top, bottom)
    other = lax.ppermute(jnp.where(first, bottom, top), "core", pairs(2))
    overlap = 2 * half - width
    left = jnp.where(first, own, other)
    right = jnp.where(first, other, own)
    return jnp.concatenate([left, right[:, overlap:]], axis=1)


def solution(mesh):
    inner, outer, tensor = (mesh.shape[name] for name in ("inner", "outer", "tensor"))
    fine = Mesh(
        mesh.devices.reshape(inner, outer // 2, 2, tensor), ("inner", "y", "core", "x")
    )
    in_specs = (P(("inner", "y", "core"), "x"), P(("inner", "y", "core", "x"), None))
    out_specs = P(("inner", "y", "core"), "x")
    return jax.shard_map(
        on_device, mesh=fine, in_specs=in_specs, out_specs=out_specs, check_vma=False
    )
```

time: 450 us -> 154 us (0.34)
  waiting for transfers between devices: 368 us -> 84.7 us
  local copies, waits for them, and re-layouts: 37.1 us -> 0.01 us
  blocking collectives: 23.6 us -> 41.4 us
  starting transfers between devices: 0.01 us -> 5.75 us
    unnamed x2 -> x1, waiting for transfers between devices: 368 us -> 0.02 us
    reduce_scatter x0 -> x1, waiting for transfers between devices: none -> 81.2 us  [on_device(): lax.psum_scatter(partial_sum, 'inner', scatter_dimension=0, tiled=True)]
    reshape x2 -> x0, local copies, waits for them, and re-layouts: 24.2 us -> none  [the longest x1 13 us: on_device(): partial_sum.reshape(owners, rows, groups, LANES).transpose(0, 2, 1, 3)]
    all_to_all x0 -> x1, blocking collectives: none -> 17.3 us  [on_device(): lax.all_to_all(over_inner.reshape(count, rows, half), 'y', split_axis=0,...]
    transpose x1 -> x0, local copies, waits for them, and re-layouts: 11.5 us -> none  [on_device(): partial_sum.reshape(owners, rows, groups, LANES).transpose(0, 2, 1, 3)]
    ppermute x0 -> x3, starting transfers between devices: none -> 5.75 us  [the longest x1 1.92 us: on_device(): received = lax.ppermute(jnp.where(first, high, low), 'core', pairs(2))]
  transfers between devices with their start and end apart: 1 -> 4, of which waited for: 1 -> 3; matrix products, arithmetic and copies ran while one was open for 0% -> 0% of each run, Pallas kernels for 0% -> 0%
where the time goes in v2:
time: 154 us; the launch traced here: 153 us
  waiting for transfers between devices  84.7 us (55%)
  blocking collectives  41.4 us (27%)
  between operations  13.4 us (9%)
  starting transfers between devices  5.75 us (4%)
  matrix products  5.01 us (3%)
  other arithmetic  2.83 us (2%)
    reduce_scatter x1, waiting for transfers between devices, on_device(): lax.psum_scatter(partial_sum, 'inner', scatter_dimension=0, tiled=True)  81.2 us
    all_gather x1, blocking collectives, on_device(): grads = lax.all_gather(out_grad, 'x', axis=0, tiled=True)  24.1 us
    all_to_all x1, blocking collectives, on_device(): lax.all_to_all(over_inner.reshape(count, rows, half), 'y', split_axis=0,...  17.3 us
    dot_general x1, matrix products, on_device(): lax.dot_general(jnp.concatenate([grads, grads_other], axis=0), jnp.concat...  5.01 us
  transfers between devices with their start and end apart: 4, of which 3 were waited for; matrix products, arithmetic and copies ran while one was open for 0% of the time, Pallas kernels for 0%

profile of v2, /device:TPU:6, one launch (start us, length us, event | category | flops | bytes accessed | tf_op | source)
XLA Modules:
  0.0 153.1 jit_solution(2504053751339963876)
XLA Ops:
  6.5 0.0 reduce-scatter.2.cloned.1.call-start
  6.5 0.0 copy-start
  6.5 2.1 %broadcast_select_fusion.1 = (bf16[384,1920]{1,0:T(8,128)(2,1)S(1)}, bf16[384,1920]{1,0:T(8,128)(2,1)S(1)}) fusion(pred[]{:T(512)S(6)} %eq.3, bf16[384,3712]{1,0:T(8,128)(2,1)} %param.2), kind=kLoop, calls=%fused_computation.8 | loop fusion | flops 1474560 | bytes 5898241 | tf_op jit(solution)/shard_map/jit(_where)/select_n | solution.py:20
  8.7 1.9 %collective-permute-start.1 = (bf16[384,1920]{1,0:T(8,128)(2,1)S(1)}, bf16[384,1920]{1,0:T(8,128)(2,1)S(1)}, u32[]{:S(2)}, u32[]{:S(2)}) collective-permute-start(bf16[384,1920]{1,0:T(8,128)(2,1)S(1)} %get-tuple-element.8), channel_id=1, source_target_pairs={{0,4},{4,0},{1,5},{5,1},{2,6},{6,2},{3,7},{7,3},{8,12},{12,8},{9,1... | collective-permute-start | bytes 4423688 | tf_op jit(solution)/shard_map/ppermute | solution.py:19
  10.6 0.0 copy-done
  10.6 24.1 %all_gather.3 = bf16[384,1024]{1,0:T(8,128)(2,1)S(1)} all-gather(bf16[96,1024]{1,0:T(8,128)(2,1)S(1)} %copy-done), channel_id=1, replica_groups=mesh['inner'=16,'y'=8,'core'=2,'x'=4] {'x'}, dimensions={0}, use_global_device_ids=true | all-gather | bytes 983040 | tf_op jit(solution)/shard_map/all_gather | solution.py:21
  34.7 1.9 %collective-permute-start = (bf16[384,1024]{1,0:T(8,128)(2,1)S(1)}, bf16[384,1024]{1,0:T(8,128)(2,1)S(1)}, u32[]{:S(2)}, u32[]{:S(2)}) collective-permute-start(bf16[384,1024]{1,0:T(8,128)(2,1)S(1)} %all_gather.3), channel_id=1, source_target_pairs={{0,4},{4,0},{1,5},{5,1},{2,6},{6,2},{3,7},{7,3},{8,12},{12,8},{9,1... | collective-permute-start | bytes 2359304 | tf_op jit(solution)/shard_map/ppermute | solution.py:22
  36.6 2.3 %collective-permute-done = bf16[384,1024]{1,0:T(8,128)(2,1)S(1)} collective-permute-done((bf16[384,1024]{1,0:T(8,128)(2,1)S(1)}, bf16[384,1024]{1,0:T(8,128)(2,1)S(1)}, u32[]{:S(2)}, u32[]{:S(2)}) %collective-permute-start) | collective-permute-done | bytes 786464 | tf_op jit(solution)/shard_map/ppermute | solution.py:22
  38.9 0.0 collective-permute-done.1
  38.9 5.0 %convolution_convert_fusion = bf16[1024,1920]{1,0:T(8,128)(2,1)} fusion(bf16[384,1920]{1,0:T(8,128)(2,1)S(1)} %collective-permute-done.1, bf16[384,1920]{1,0:T(8,128)(2,1)S(1)} %get-tuple-element.7, bf16[384,1024]{1,0:T(8,128)(2,1)S(1)} %collective-permute-done, bf16[384,1024]{1,0:T(8,128)(2,1)S(1)} %all_gather.3), kind=kOutput, calls=%fused_computation | convolution fusion | flops 3030908928 | bytes 8454144 | tf_op jit(solution)/shard_map/dot_general | solution.py:24
  43.9 0.0 reduce-scatter.2.cloned.1.call-update
  43.9 81.2 %reduce-scatter.2.cloned.1.call-done = bf16[64,1920]{1,0:T(8,128)(2,1)} async-done(((bf16[1024,1920]{1,0:T(8,128)(2,1)}), bf16[64,1920]{1,0:T(8,128)(2,1)}) %reduce-scatter.2.cloned.1.call-update) | async-done | bytes 245776 | tf_op jit(solution)/shard_map/reduce_scatter | solution.py:30
  125.1 17.3 %all_to_all.5 = bf16[8,8,1920]{2,1,0:T(8,128)(2,1)S(1)} all-to-all(bf16[8,8,1920]{2,1,0:T(8,128)(2,1)} %bitcast.1), channel_id=1, replica_groups=mesh['inner'=16,'y'=8,'core'=2,'x'=4] {'y'}, dimensions={0} | all-to-all | bytes 491520 | tf_op jit(solution)/shard_map/all_to_all | solution.py:33
  142.5 1.9 %collective-permute-start.2 = (f32[4,1920]{1,0:T(4,128)S(1)}, f32[4,1920]{1,0:T(4,128)S(1)}, u32[]{:S(2)}, u32[]{:S(2)}) collective-permute-start(f32[4,1920]{1,0:T(4,128)S(1)} %slice_select_fusion.1), channel_id=1, source_target_pairs={{0,4},{4,0},{1,5},{5,1},{2,6},{6,2},{3,7},{7,3},{8,12},{12,8},{9,1... | collective-permute-start | bytes 92168 | tf_op jit(solution)/shard_map/ppermute | solution.py:40
  144.4 1.2 collective-permute-done.2
  145.6 0.6 pad_maximum_fusion
  (4 shorter events, 0.1 us)
Async XLA Ops:
  6.5 118.6 %reduce-scatter.2.cloned.1.call-start = ((), (), s32[]{:S(2)}) async-start(), calls=%async_computation.2 | async-start | bytes 4177920 | tf_op jit(solution)/shard_map/reduce_scatter | solution.py:30
  6.5 4.1 %copy-start = (bf16[96,1024]{1,0:T(8,128)(2,1)S(1)}, bf16[96,1024]{1,0:T(8,128)(2,1)}, u32[]{:S(2)}) copy-start(bf16[96,1024]{1,0:T(8,128)(2,1)} %param.3) | copy-start | bytes 589828
  8.7 30.2 %collective-permute-start.1 = (bf16[384,1920]{1,0:T(8,128)(2,1)S(1)}, bf16[384,1920]{1,0:T(8,128)(2,1)S(1)}, u32[]{:S(2)}, u32[]{:S(2)}) collective-permute-start(bf16[384,1920]{1,0:T(8,128)(2,1)S(1)} %get-tuple-element.8), channel_id=1, source_target_pairs={{0,4},{4,0},{1,5},{5,1},{2,6},{6,2},{3,7},{7,3},{8,12},{12,8},{9,1... | collective-permute-start | bytes 4423688 | tf_op jit(solution)/shard_map/ppermute | solution.py:19
  34.7 4.2 %collective-permute-start = (bf16[384,1024]{1,0:T(8,128)(2,1)S(1)}, bf16[384,1024]{1,0:T(8,128)(2,1)S(1)}, u32[]{:S(2)}, u32[]{:S(2)}) collective-permute-start(bf16[384,1024]{1,0:T(8,128)(2,1)S(1)} %all_gather.3), channel_id=1, source_target_pairs={{0,4},{4,0},{1,5},{5,1},{2,6},{6,2},{3,7},{7,3},{8,12},{12,8},{9,1... | collective-permute-start | bytes 2359304 | tf_op jit(solution)/shard_map/ppermute | solution.py:22
  142.5 3.1 %collective-permute-start.2 = (f32[4,1920]{1,0:T(4,128)S(1)}, f32[4,1920]{1,0:T(4,128)S(1)}, u32[]{:S(2)}, u32[]{:S(2)}) collective-permute-start(f32[4,1920]{1,0:T(4,128)S(1)} %slice_select_fusion.1), channel_id=1, source_target_pairs={{0,4},{4,0},{1,5},{5,1},{2,6},{6,2},{3,7},{7,3},{8,12},{12,8},{9,1... | collective-permute-start | bytes 92168 | tf_op jit(solution)/shard_map/ppermute | solution.py:40
Sparse Core Ops, SparseCore 0:
  44.0 81.0 reduce-scatter.1

commit v3 on v1

v3 whole, which is shorter than its diff:
```python
import jax
import jax.numpy as jnp
from jax import lax
from jax.sharding import Mesh, PartitionSpec as P

LANES = 128
SWAP = [(0, 1), (1, 0)]


def in_owner_order(out_grad, inner, outer):
    columns = out_grad.shape[1]
    rows = columns // (inner * outer * 2)
    new = lax.broadcasted_iota(jnp.int32, (columns, columns), 1)
    old = lax.broadcasted_iota(jnp.int32, (columns, columns), 0)
    row, rest = new % rows, new // rows
    i, rest = rest % inner, rest // inner
    y, core = rest % outer, rest // outer
    source = ((i * outer + y) * 2 + core) * rows + row
    one_hot = (source == old).astype(out_grad.dtype)
    moved = lax.dot_general(
        out_grad, one_hot, (((1,), (0,)), ((), ())), preferred_element_type=jnp.float32
    )
    return moved.astype(out_grad.dtype)


def add(left, right):
    return (left.astype(jnp.float32) + right.astype(jnp.float32)).astype(jnp.bfloat16)


def on_device(activations, out_grad):
    inner, outer = lax.axis_size("inner"), lax.axis_size("y")
    core, me = lax.axis_index("core"), lax.axis_index("y")
    width = activations.shape[1]
    activations_other = lax.ppermute(activations, "core", SWAP)
    grads = lax.all_gather(in_owner_order(out_grad, inner, outer), "x", axis=0, tiled=True)
    columns = grads.shape[1] // 2
    grads_own = lax.dynamic_slice_in_dim(grads, core * columns, columns, 1, allow_negative_indices=False)
    grads_sent = lax.dynamic_slice_in_dim(
        grads, (1 - core) * columns, columns, 1, allow_negative_indices=False
    )
    grads_other = lax.ppermute(grads_sent, "core", SWAP)
    all_grads = jnp.concatenate([grads_own, grads_other], axis=0)
    cut = -(-(width // LANES) // 2) * LANES

    def partial_sum(low, high):
        tokens = jnp.concatenate([activations[:, low:high], activations_other[:, low:high]], axis=0)
        product = lax.dot_general(
            all_grads, tokens, (((0,), (0,)), ((), ())), preferred_element_type=jnp.float32
        )
        return product.astype(jnp.bfloat16).reshape(outer, columns // outer, high - low)

    pieces = (partial_sum(0, cut), partial_sum(cut, width))

    def of(piece, distance):
        owner = lax.rem(me + (distance + outer), outer)
        return lax.dynamic_index_in_dim(piece, owner, 0, keepdims=False, allow_negative_indices=False)

    far = outer // 2
    streams = [(p, sign, far if (sign > 0) == (p == 0) else far - 1) for sign in (1, -1) for p in (0, 1)]
    moving = {}
    for distance in range(far, 0, -1):
        for p, sign, hops in streams:
            if distance > hops:
                continue
            own = of(pieces[p], sign * distance)
            block = own if distance == hops else add(moving[p, sign], own)
            moving[p, sign] = lax.ppermute(
                block, "y", [(s, (s + sign) % outer) for s in range(outer)]
            )
    sums = [
        (
            of(pieces[p], 0).astype(jnp.float32)
            + moving[p, 1].astype(jnp.float32)
            + moving[p, -1].astype(jnp.float32)
        ).astype(jnp.bfloat16)
        for p in (0, 1)
    ]
    first = jnp.concatenate(sums, axis=1).reshape(inner, columns // outer // inner, width)
    blocks = lax.all_to_all(first, "inner", split_axis=0, concat_axis=0, tiled=True)
    return jnp.sum(blocks, axis=0, dtype=jnp.float32)


def solution(mesh):
    inner, outer, tensor = (mesh.shape[name] for name in ("inner", "outer", "tensor"))
    fine = Mesh(
        mesh.devices.reshape(inner, outer // 2, 2, tensor), ("inner", "y", "core", "x")
    )
    in_specs = (P(("inner", "y", "core"), "x"), P(("inner", "y", "core", "x"), None))
    out_specs = P(("inner", "y", "core"), "x")
    return jax.shard_map(
        on_device, mesh=fine, in_specs=in_specs, out_specs=out_specs, check_vma=False
    )
```

time: 450 us -> 134 us (0.30)
  waiting for transfers between devices: 368 us -> 13 us
  starting transfers between devices: 0.01 us -> 50.1 us
  blocking collectives: 23.6 us -> 54.5 us
  local copies, waits for them, and re-layouts: 37.1 us -> 6.4 us
  between operations: 13.4 us -> 0.38 us
    unnamed x2 -> x0, waiting for transfers between devices: 368 us -> none
    ppermute x0 -> x16, starting transfers between devices: none -> 50.1 us  [the longest x14 46.2 us: on_device(): lax.ppermute(block, 'y', [(s, (s + sign) % outer) for s in range(outer)])]
    all_to_all x0 -> x1, blocking collectives: none -> 30.4 us  [on_device(): lax.all_to_all(first, 'inner', split_axis=0, concat_axis=0, tiled=True)]
    reshape x2 -> x1, local copies, waits for them, and re-layouts: 24.2 us -> 0.11 us  [on_device(): jnp.concatenate(sums, axis=1)]
    ppermute x0 -> x16, waiting for transfers between devices: none -> 13 us  [the longest x14 13 us: on_device(): lax.ppermute(block, 'y', [(s, (s + sign) % outer) for s in range(outer)])]
    transpose x1 -> x0, local copies, waits for them, and re-layouts: 11.5 us -> none  [on_device(): partial_sum.reshape(owners, rows, groups, LANES).transpose(0, 2, 1, 3)]
    slice x0 -> x4, local copies, waits for them, and re-layouts: none -> 5.34 us  [the longest x2 2.91 us: partial_sum(): activations_other[:, low:high]]
  transfers between devices with their start and end apart: 1 -> 16, of which waited for: 1 -> 4; matrix products, arithmetic and copies ran while one was open for 0% -> 8% of each run, Pallas kernels for 0% -> 0%
where the time goes in v3:
time: 134 us; the launch traced here: 133 us
  blocking collectives  54.5 us (41%)
  starting transfers between devices  50.1 us (37%)
  waiting for transfers between devices  13 us (10%)
  matrix products  7.4 us (6%)
  local copies, waits for them, and re-layouts  6.4 us (5%)
  other arithmetic  1.68 us (1%)
    ppermute x14, starting transfers between devices, on_device(): lax.ppermute(block, 'y', [(s, (s + sign) % outer) for s in range(outer)])  46.2 us
    all_to_all x1, blocking collectives, on_device(): lax.all_to_all(first, 'inner', split_axis=0, concat_axis=0, tiled=True)  30.4 us
    all_gather x1, blocking collectives, on_device(): lax.all_gather(in_owner_order(out_grad, inner, outer), 'x', axis=0, tiled...  24.1 us
    ppermute x14, waiting for transfers between devices, on_device(): lax.ppermute(block, 'y', [(s, (s + sign) % outer) for s in range(outer)])  13 us
    dot_general x2, matrix products, partial_sum(): lax.dot_general(all_grads, tokens, (((0,), (0,)), ((), ())), preferred_el...  5.96 us
    slice x2, local copies, waits for them, and re-layouts, partial_sum(): activations_other[:, low:high]  2.91 us
  transfers between devices with their start and end apart: 16, of which 4 were waited for; matrix products, arithmetic and copies ran while one was open for 8% of the time, Pallas kernels for 0%

profile of v3, /device:TPU:6, one launch (start us, length us, event | category | flops | bytes accessed | tf_op | source)
XLA Modules:
  0.0 133.5 jit_solution(10417374136079559977)
XLA Ops:
  0.0 2.0 %collective-permute-start.1 = (bf16[384,3712]{1,0:T(8,128)(2,1)}, bf16[384,3712]{1,0:T(8,128)(2,1)}, u32[]{:S(2)}, u32[]{:S(2)}) collective-permute-start(bf16[384,3712]{1,0:T(8,128)(2,1)} %param.2), channel_id=1, source_target_pairs={{0,4},{4,0},{1,5},{5,1},{2,6},{6,2},{3,7},{7,3},{8,12},{12,8},{9,1... | collective-permute-start | bytes 8552456 | tf_op jit(solution)/shard_map/ppermute | solution.py:34
  2.1 0.0 copy-start.1
  2.1 1.4 %fusion.42 = bf16[96,1024]{1,0:T(8,128)(2,1)S(1)} fusion(bf16[96,1024]{1,0:T(8,128)(2,1)S(1)} %copy-done, s32[1024]{0:T(1024)S(1)} %get-tuple-element.22, s32[1024]{0:T(1024)S(1)} %get-tuple-element.23, s32[1024]{0:T(1024)S(1)} %get-tuple-element.21, s32[1024]{0:T(1024)S(1)} %get-tuple-element.24, pred[1024]{0:T(1024)(128)(4,1)S(1)} %get-tuple-element.19, ...), kind=kOutput, calls=%fused_computation.55 | convolution fusion | flops 250707968 | bytes 411648 | tf_op jit(solution)/shard_map/dot_general | solution.py:20
  3.6 24.1 %all_gather.3 = bf16[384,1024]{1,0:T(8,128)(2,1)S(1)} all-gather(bf16[96,1024]{1,0:T(8,128)(2,1)S(1)} %fusion.42), channel_id=1, replica_groups=mesh['inner'=16,'y'=8,'core'=2,'x'=4] {'x'}, dimensions={0}, use_global_device_ids=true | all-gather | bytes 983040 | tf_op jit(solution)/shard_map/all_gather | solution.py:35
  27.7 0.8 constant_dynamic-slice_fusion.1
  28.5 1.9 %collective-permute-start = (bf16[384,512]{1,0:T(8,128)(2,1)}, bf16[384,512]{1,0:T(8,128)(2,1)}, u32[]{:S(2)}, u32[]{:S(2)}) collective-permute-start(bf16[384,512]{1,0:T(8,128)(2,1)} %get-tuple-element.18), channel_id=1, source_target_pairs={{0,4},{4,0},{1,5},{5,1},{2,6},{6,2},{3,7},{7,3},{8,12},{12,8},{9,1... | collective-permute-start | bytes 1179656 | tf_op jit(solution)/shard_map/ppermute | solution.py:41
  30.4 1.2 slice.14
  31.6 1.2 slice.12
  32.9 0.0 collective-permute-done.1
  32.9 1.4 %slice.17 = bf16[384,1792]{1,0:T(8,128)(2,1)S(1)} slice(bf16[384,3712]{1,0:T(8,128)(2,1)} %collective-permute-done.1), slice={[0:384], [1920:3712]} | slice | bytes 2752512 | tf_op jit(solution)/shard_map/slice | solution.py:46
  34.3 3.1 %convolution_convert_fusion = bf16[512,1792]{1,0:T(8,128)(2,1)S(1)} fusion(bf16[384,1792]{1,0:T(8,128)(2,1)S(1)} %slice.17, bf16[384,1792]{1,0:T(8,128)(2,1)} %slice.14, bf16[384,512]{1,0:T(8,128)(2,1)} %collective-permute-done, bf16[384,512]{1,0:T(8,128)(2,1)S(1)} %get-tuple-element.17), kind=kOutput, calls=%fused_computation.30 | convolution fusion | flops 1417281536 | bytes 5373952 | tf_op jit(solution)/shard_map/dot_general | solution.py:47
  37.5 2.1 %collective-permute-start.9 = (bf16[64,1792]{1,0:T(8,128)(2,1)S(1)}, bf16[64,1792]{1,0:T(8,128)(2,1)S(1)}, u32[]{:S(2)}, u32[]{:S(2)}) collective-permute-start(bf16[64,1792]{1,0:T(8,128)(2,1)S(1)} %get-tuple-element.15), channel_id=1, source_target_pairs={{0,8},{8,16},{16,24},{24,32},{32,40},{40,48},{48,56},{56,0},{1,9},... | collective-permute-start | bytes 688136 | tf_op jit(solution)/shard_map/ppermute | solution.py:67
  39.5 5.1 %collective-permute-start.12 = (bf16[64,1792]{1,0:T(8,128)(2,1)S(1)}, bf16[64,1792]{1,0:T(8,128)(2,1)S(1)}, u32[]{:S(2)}, u32[]{:S(2)}) collective-permute-start(bf16[64,1792]{1,0:T(8,128)(2,1)S(1)} %get-tuple-element.16), channel_id=1, source_target_pairs={{0,56},{8,0},{16,8},{24,16},{32,24},{40,32},{48,40},{56,48},{1,57}... | collective-permute-start | bytes 688136 | tf_op jit(solution)/shard_map/ppermute | solution.py:67
  44.7 1.5 %slice.16 = bf16[384,1920]{1,0:T(8,128)(2,1)S(1)} slice(bf16[384,3712]{1,0:T(8,128)(2,1)} %collective-permute-done.1), slice={[0:384], [0:1920]} | slice | bytes 2949120 | tf_op jit(solution)/shard_map/slice | solution.py:46
  46.2 2.9 %convolution_convert_fusion.1 = bf16[512,1920]{1,0:T(8,128)(2,1)S(1)} fusion(bf16[384,1920]{1,0:T(8,128)(2,1)S(1)} %slice.16, bf16[384,1920]{1,0:T(8,128)(2,1)S(1)} %copy-done.2, bf16[384,512]{1,0:T(8,128)(2,1)} %collective-permute-done, bf16[384,512]{1,0:T(8,128)(2,1)S(1)} %get-tuple-element.17), kind=kOutput, calls=%fused_computation.31 | convolution fusion | flops 1518403584 | bytes 5701632 | tf_op jit(solution)/shard_map/dot_general | solution.py:47
  49.1 1.9 %collective-permute-start.2 = (bf16[64,1920]{1,0:T(8,128)(2,1)S(1)}, bf16[64,1920]{1,0:T(8,128)(2,1)S(1)}, u32[]{:S(2)}, u32[]{:S(2)}) collective-permute-start(bf16[64,1920]{1,0:T(8,128)(2,1)S(1)} %get-tuple-element.9), channel_id=1, source_target_pairs={{0,8},{8,16},{16,24},{24,32},{32,40},{40,48},{48,56},{56,0},{1,9},... | collective-permute-start | bytes 737288 | tf_op jit(solution)/shard_map/ppermute | solution.py:67
  51.0 5.1 %collective-permute-start.6 = (bf16[64,1920]{1,0:T(8,128)(2,1)S(1)}, bf16[64,1920]{1,0:T(8,128)(2,1)S(1)}, u32[]{:S(2)}, u32[]{:S(2)}) collective-permute-start(bf16[64,1920]{1,0:T(8,128)(2,1)S(1)} %get-tuple-element.10), channel_id=1, source_target_pairs={{0,56},{8,0},{16,8},{24,16},{32,24},{40,32},{48,40},{56,48},{1,57}... | collective-permute-start | bytes 737288 | tf_op jit(solution)/shard_map/ppermute | solution.py:67
  56.2 0.1 fusion.54
  56.2 1.9 %collective-permute-start.13 = (bf16[64,1792]{1,0:T(8,128)(2,1)S(1)}, bf16[64,1792]{1,0:T(8,128)(2,1)S(1)}, u32[]{:S(2)}, u32[]{:S(2)}) collective-permute-start(bf16[64,1792]{1,0:T(8,128)(2,1)S(1)} %fusion.54), channel_id=1, source_target_pairs={{0,56},{8,0},{16,8},{24,16},{32,24},{40,32},{48,40},{56,48},{1,57}... | collective-permute-start | bytes 688136 | tf_op jit(solution)/shard_map/ppermute | solution.py:67
  58.2 1.8 %collective-permute-done.2 = bf16[64,1920]{1,0:T(8,128)(2,1)S(1)} collective-permute-done((bf16[64,1920]{1,0:T(8,128)(2,1)S(1)}, bf16[64,1920]{1,0:T(8,128)(2,1)S(1)}, u32[]{:S(2)}, u32[]{:S(2)}) %collective-permute-start.2) | collective-permute-done | bytes 245792 | tf_op jit(solution)/shard_map/ppermute | solution.py:67
  60.0 0.1 fusion.49
  60.1 2.1 %collective-permute-start.3 = (bf16[64,1920]{1,0:T(8,128)(2,1)S(1)}, bf16[64,1920]{1,0:T(8,128)(2,1)S(1)}, u32[]{:S(2)}, u32[]{:S(2)}) collective-permute-start(bf16[64,1920]{1,0:T(8,128)(2,1)S(1)} %fusion.49), channel_id=1, source_target_pairs={{0,8},{8,16},{16,24},{24,32},{32,40},{40,48},{48,56},{56,0},{1,9},... | collective-permute-start | bytes 737288 | tf_op jit(solution)/shard_map/ppermute | solution.py:67
  62.2 0.0 collective-permute-done.9
  62.2 3.9 %collective-permute-done.13 = bf16[64,1792]{1,0:T(8,128)(2,1)S(1)} collective-permute-done((bf16[64,1792]{1,0:T(8,128)(2,1)S(1)}, bf16[64,1792]{1,0:T(8,128)(2,1)S(1)}, u32[]{:S(2)}, u32[]{:S(2)}) %collective-permute-start.13) | collective-permute-done | bytes 229408 | tf_op jit(solution)/shard_map/ppermute | solution.py:67
  66.1 0.1 fusion.56
  66.2 1.9 %collective-permute-start.10 = (bf16[64,1792]{1,0:T(8,128)(2,1)S(1)}, bf16[64,1792]{1,0:T(8,128)(2,1)S(1)}, u32[]{:S(2)}, u32[]{:S(2)}) collective-permute-start(bf16[64,1792]{1,0:T(8,128)(2,1)S(1)} %get-tuple-element.13), channel_id=1, source_target_pairs={{0,8},{8,16},{16,24},{24,32},{32,40},{40,48},{48,56},{56,0},{1,9},... | collective-permute-start | bytes 688136 | tf_op jit(solution)/shard_map/ppermute | solution.py:67
  68.1 5.6 %collective-permute-start.14 = (bf16[64,1792]{1,0:T(8,128)(2,1)S(1)}, bf16[64,1792]{1,0:T(8,128)(2,1)S(1)}, u32[]{:S(2)}, u32[]{:S(2)}) collective-permute-start(bf16[64,1792]{1,0:T(8,128)(2,1)S(1)} %get-tuple-element.14), channel_id=1, source_target_pairs={{0,56},{8,0},{16,8},{24,16},{32,24},{40,32},{48,40},{56,48},{1,57}... | collective-permute-start | bytes 688136 | tf_op jit(solution)/shard_map/ppermute | solution.py:67
  73.7 0.0 collective-permute-done.6
  73.8 0.1 fusion.48
  73.9 1.9 %collective-permute-start.4 = (bf16[64,1920]{1,0:T(8,128)(2,1)S(1)}, bf16[64,1920]{1,0:T(8,128)(2,1)S(1)}, u32[]{:S(2)}, u32[]{:S(2)}) collective-permute-start(bf16[64,1920]{1,0:T(8,128)(2,1)S(1)} %get-tuple-element.7), channel_id=1, source_target_pairs={{0,8},{8,16},{16,24},{24,32},{32,40},{40,48},{48,56},{56,0},{1,9},... | collective-permute-start | bytes 737288 | tf_op jit(solution)/shard_map/ppermute | solution.py:67
  75.8 5.1 %collective-permute-start.7 = (bf16[64,1920]{1,0:T(8,128)(2,1)S(1)}, bf16[64,1920]{1,0:T(8,128)(2,1)S(1)}, u32[]{:S(2)}, u32[]{:S(2)}) collective-permute-start(bf16[64,1920]{1,0:T(8,128)(2,1)S(1)} %get-tuple-element.8), channel_id=1, source_target_pairs={{0,56},{8,0},{16,8},{24,16},{32,24},{40,32},{48,40},{56,48},{1,57}... | collective-permute-start | bytes 737288 | tf_op jit(solution)/shard_map/ppermute | solution.py:67
  81.0 0.0 collective-permute-done.10
  81.0 0.0 collective-permute-done.14
  81.0 0.1 fusion.55
  81.1 2.7 %collective-permute-start.15 = (bf16[64,1792]{1,0:T(8,128)(2,1)S(1)}, bf16[64,1792]{1,0:T(8,128)(2,1)S(1)}, u32[]{:S(2)}, u32[]{:S(2)}) collective-permute-start(bf16[64,1792]{1,0:T(8,128)(2,1)S(1)} %get-tuple-element.12), channel_id=1, source_target_pairs={{0,56},{8,0},{16,8},{24,16},{32,24},{40,32},{48,40},{56,48},{1,57}... | collective-permute-start | bytes 688136 | tf_op jit(solution)/shard_map/ppermute | solution.py:67
  83.8 3.1 %collective-permute-start.11 = (bf16[64,1792]{1,0:T(8,128)(2,1)S(1)}, bf16[64,1792]{1,0:T(8,128)(2,1)S(1)}, u32[]{:S(2)}, u32[]{:S(2)}) collective-permute-start(bf16[64,1792]{1,0:T(8,128)(2,1)S(1)} %get-tuple-element.11), channel_id=1, source_target_pairs={{0,8},{8,16},{16,24},{24,32},{32,40},{40,48},{48,56},{56,0},{1,9},... | collective-permute-start | bytes 688136 | tf_op jit(solution)/shard_map/ppermute | solution.py:67
  87.0 0.0 collective-permute-done.4
  87.0 0.1 fusion.47
  87.1 5.6 %collective-permute-start.8 = (bf16[64,1920]{1,0:T(8,128)(2,1)S(1)}, bf16[64,1920]{1,0:T(8,128)(2,1)S(1)}, u32[]{:S(2)}, u32[]{:S(2)}) collective-permute-start(bf16[64,1920]{1,0:T(8,128)(2,1)S(1)} %get-tuple-element.6), channel_id=1, source_target_pairs={{0,56},{8,0},{16,8},{24,16},{32,24},{40,32},{48,40},{56,48},{1,57}... | collective-permute-start | bytes 737288 | tf_op jit(solution)/shard_map/ppermute | solution.py:67
  92.7 1.9 %collective-permute-start.5 = (bf16[64,1920]{1,0:T(8,128)(2,1)S(1)}, bf16[64,1920]{1,0:T(8,128)(2,1)S(1)}, u32[]{:S(2)}, u32[]{:S(2)}) collective-permute-start(bf16[64,1920]{1,0:T(8,128)(2,1)S(1)} %get-tuple-element.5), channel_id=1, source_target_pairs={{0,8},{8,16},{16,24},{24,32},{32,40},{40,48},{48,56},{56,0},{1,9},... | collective-permute-start | bytes 737288 | tf_op jit(solution)/shard_map/ppermute | solution.py:67
  94.6 0.0 collective-permute-done.15
  94.7 0.1 fusion.58
  94.8 1.6 %collective-permute-done.8 = bf16[64,1920]{1,0:T(8,128)(2,1)S(1)} collective-permute-done((bf16[64,1920]{1,0:T(8,128)(2,1)S(1)}, bf16[64,1920]{1,0:T(8,128)(2,1)S(1)}, u32[]{:S(2)}, u32[]{:S(2)}) %collective-permute-start.8) | collective-permute-done | bytes 245792 | tf_op jit(solution)/shard_map/ppermute | solution.py:67
  96.4 5.6 %collective-permute-done.5 = bf16[64,1920]{1,0:T(8,128)(2,1)S(1)} collective-permute-done((bf16[64,1920]{1,0:T(8,128)(2,1)S(1)}, bf16[64,1920]{1,0:T(8,128)(2,1)S(1)}, u32[]{:S(2)}, u32[]{:S(2)}) %collective-permute-start.5) | collective-permute-done | bytes 245792 | tf_op jit(solution)/shard_map/ppermute | solution.py:67
  102.0 0.1 fusion.51
  102.2 0.1 reshape.35
  102.3 30.4 %all_to_all.5 = bf16[16,4,3712]{2,1,0:T(4,128)(2,1)S(1)} all-to-all(bf16[16,4,3712]{2,1,0:T(4,128)(2,1)S(1)} %reshape.35), channel_id=1, replica_groups=mesh['inner'=16,'y'=8,'core'=2,'x'=4] {'inner'}, dimensions={0} | all-to-all | bytes 950272 | tf_op jit(solution)/shard_map/all_to_all | solution.py:79
  132.7 0.8 convert_reduce_fusion
  (16 shorter events, 0.2 us)
Async XLA Ops:
  0.0 2.1 %copy-start = (bf16[96,1024]{1,0:T(8,128)(2,1)S(1)}, bf16[96,1024]{1,0:T(8,128)(2,1)}, u32[]{:S(2)}) copy-start(bf16[96,1024]{1,0:T(8,128)(2,1)} %param.3) | copy-start | bytes 589828
  0.0 32.9 %collective-permute-start.1 = (bf16[384,3712]{1,0:T(8,128)(2,1)}, bf16[384,3712]{1,0:T(8,128)(2,1)}, u32[]{:S(2)}, u32[]{:S(2)}) collective-permute-start(bf16[384,3712]{1,0:T(8,128)(2,1)} %param.2), channel_id=1, source_target_pairs={{0,4},{4,0},{1,5},{5,1},{2,6},{6,2},{3,7},{7,3},{8,12},{12,8},{9,1... | collective-permute-start | bytes 8552456 | tf_op jit(solution)/shard_map/ppermute | solution.py:34
  2.1 28.3 %copy-start.1 = (bf16[384,3712]{1,0:T(8,128)(2,1)S(1)}, bf16[384,3712]{1,0:T(8,128)(2,1)}, u32[]{:S(2)}) copy-start(bf16[384,3712]{1,0:T(8,128)(2,1)} %param.2) | copy-start | bytes 8552452
  28.5 5.8 %collective-permute-start = (bf16[384,512]{1,0:T(8,128)(2,1)}, bf16[384,512]{1,0:T(8,128)(2,1)}, u32[]{:S(2)}, u32[]{:S(2)}) collective-permute-start(bf16[384,512]{1,0:T(8,128)(2,1)} %get-tuple-element.18), channel_id=1, source_target_pairs={{0,4},{4,0},{1,5},{5,1},{2,6},{6,2},{3,7},{7,3},{8,12},{12,8},{9,1... | collective-permute-start | bytes 1179656 | tf_op jit(solution)/shard_map/ppermute | solution.py:41
  37.4 8.7 %copy-start.2 = (bf16[384,1920]{1,0:T(8,128)(2,1)S(1)}, bf16[384,1920]{1,0:T(8,128)(2,1)}, u32[]{:S(2)}) copy-start(bf16[384,1920]{1,0:T(8,128)(2,1)} %slice.12) | copy-start | bytes 4423684
  37.5 24.7 %collective-permute-start.9 = (bf16[64,1792]{1,0:T(8,128)(2,1)S(1)}, bf16[64,1792]{1,0:T(8,128)(2,1)S(1)}, u32[]{:S(2)}, u32[]{:S(2)}) collective-permute-start(bf16[64,1792]{1,0:T(8,128)(2,1)S(1)} %get-tuple-element.15), channel_id=1, source_target_pairs={{0,8},{8,16},{16,24},{24,32},{32,40},{40,48},{48,56},{56,0},{1,9},... | collective-permute-start | bytes 688136 | tf_op jit(solution)/shard_map/ppermute | solution.py:67
  39.5 16.6 %collective-permute-start.12 = (bf16[64,1792]{1,0:T(8,128)(2,1)S(1)}, bf16[64,1792]{1,0:T(8,128)(2,1)S(1)}, u32[]{:S(2)}, u32[]{:S(2)}) collective-permute-start(bf16[64,1792]{1,0:T(8,128)(2,1)S(1)} %get-tuple-element.16), channel_id=1, source_target_pairs={{0,56},{8,0},{16,8},{24,16},{32,24},{40,32},{48,40},{56,48},{1,57}... | collective-permute-start | bytes 688136 | tf_op jit(solution)/shard_map/ppermute | solution.py:67
  49.1 10.9 %collective-permute-start.2 = (bf16[64,1920]{1,0:T(8,128)(2,1)S(1)}, bf16[64,1920]{1,0:T(8,128)(2,1)S(1)}, u32[]{:S(2)}, u32[]{:S(2)}) collective-permute-start(bf16[64,1920]{1,0:T(8,128)(2,1)S(1)} %get-tuple-element.9), channel_id=1, source_target_pairs={{0,8},{8,16},{16,24},{24,32},{32,40},{40,48},{48,56},{56,0},{1,9},... | collective-permute-start | bytes 737288 | tf_op jit(solution)/shard_map/ppermute | solution.py:67
  51.0 22.7 %collective-permute-start.6 = (bf16[64,1920]{1,0:T(8,128)(2,1)S(1)}, bf16[64,1920]{1,0:T(8,128)(2,1)S(1)}, u32[]{:S(2)}, u32[]{:S(2)}) collective-permute-start(bf16[64,1920]{1,0:T(8,128)(2,1)S(1)} %get-tuple-element.10), channel_id=1, source_target_pairs={{0,56},{8,0},{16,8},{24,16},{32,24},{40,32},{48,40},{56,48},{1,57}... | collective-permute-start | bytes 737288 | tf_op jit(solution)/shard_map/ppermute | solution.py:67
  56.2 9.9 %collective-permute-start.13 = (bf16[64,1792]{1,0:T(8,128)(2,1)S(1)}, bf16[64,1792]{1,0:T(8,128)(2,1)S(1)}, u32[]{:S(2)}, u32[]{:S(2)}) collective-permute-start(bf16[64,1792]{1,0:T(8,128)(2,1)S(1)} %fusion.54), channel_id=1, source_target_pairs={{0,56},{8,0},{16,8},{24,16},{32,24},{40,32},{48,40},{56,48},{1,57}... | collective-permute-start | bytes 688136 | tf_op jit(solution)/shard_map/ppermute | solution.py:67
  60.1 13.7 %collective-permute-start.3 = (bf16[64,1920]{1,0:T(8,128)(2,1)S(1)}, bf16[64,1920]{1,0:T(8,128)(2,1)S(1)}, u32[]{:S(2)}, u32[]{:S(2)}) collective-permute-start(bf16[64,1920]{1,0:T(8,128)(2,1)S(1)} %fusion.49), channel_id=1, source_target_pairs={{0,8},{8,16},{16,24},{24,32},{32,40},{40,48},{48,56},{56,0},{1,9},... | collective-permute-start | bytes 737288 | tf_op jit(solution)/shard_map/ppermute | solution.py:67
  66.2 14.8 %collective-permute-start.10 = (bf16[64,1792]{1,0:T(8,128)(2,1)S(1)}, bf16[64,1792]{1,0:T(8,128)(2,1)S(1)}, u32[]{:S(2)}, u32[]{:S(2)}) collective-permute-start(bf16[64,1792]{1,0:T(8,128)(2,1)S(1)} %get-tuple-element.13), channel_id=1, source_target_pairs={{0,8},{8,16},{16,24},{24,32},{32,40},{40,48},{48,56},{56,0},{1,9},... | collective-permute-start | bytes 688136 | tf_op jit(solution)/shard_map/ppermute | solution.py:67
  68.1 12.8 %collective-permute-start.14 = (bf16[64,1792]{1,0:T(8,128)(2,1)S(1)}, bf16[64,1792]{1,0:T(8,128)(2,1)S(1)}, u32[]{:S(2)}, u32[]{:S(2)}) collective-permute-start(bf16[64,1792]{1,0:T(8,128)(2,1)S(1)} %get-tuple-element.14), channel_id=1, source_target_pairs={{0,56},{8,0},{16,8},{24,16},{32,24},{40,32},{48,40},{56,48},{1,57}... | collective-permute-start | bytes 688136 | tf_op jit(solution)/shard_map/ppermute | solution.py:67
  73.9 13.1 %collective-permute-start.4 = (bf16[64,1920]{1,0:T(8,128)(2,1)S(1)}, bf16[64,1920]{1,0:T(8,128)(2,1)S(1)}, u32[]{:S(2)}, u32[]{:S(2)}) collective-permute-start(bf16[64,1920]{1,0:T(8,128)(2,1)S(1)} %get-tuple-element.7), channel_id=1, source_target_pairs={{0,8},{8,16},{16,24},{24,32},{32,40},{40,48},{48,56},{56,0},{1,9},... | collective-permute-start | bytes 737288 | tf_op jit(solution)/shard_map/ppermute | solution.py:67
  75.8 11.2 %collective-permute-start.7 = (bf16[64,1920]{1,0:T(8,128)(2,1)S(1)}, bf16[64,1920]{1,0:T(8,128)(2,1)S(1)}, u32[]{:S(2)}, u32[]{:S(2)}) collective-permute-start(bf16[64,1920]{1,0:T(8,128)(2,1)S(1)} %get-tuple-element.8), channel_id=1, source_target_pairs={{0,56},{8,0},{16,8},{24,16},{32,24},{40,32},{48,40},{56,48},{1,57}... | collective-permute-start | bytes 737288 | tf_op jit(solution)/shard_map/ppermute | solution.py:67
  81.1 13.5 %collective-permute-start.15 = (bf16[64,1792]{1,0:T(8,128)(2,1)S(1)}, bf16[64,1792]{1,0:T(8,128)(2,1)S(1)}, u32[]{:S(2)}, u32[]{:S(2)}) collective-permute-start(bf16[64,1792]{1,0:T(8,128)(2,1)S(1)} %get-tuple-element.12), channel_id=1, source_target_pairs={{0,56},{8,0},{16,8},{24,16},{32,24},{40,32},{48,40},{56,48},{1,57}... | collective-permute-start | bytes 688136 | tf_op jit(solution)/shard_map/ppermute | solution.py:67
  83.8 10.8 %collective-permute-start.11 = (bf16[64,1792]{1,0:T(8,128)(2,1)S(1)}, bf16[64,1792]{1,0:T(8,128)(2,1)S(1)}, u32[]{:S(2)}, u32[]{:S(2)}) collective-permute-start(bf16[64,1792]{1,0:T(8,128)(2,1)S(1)} %get-tuple-element.11), channel_id=1, source_target_pairs={{0,8},{8,16},{16,24},{24,32},{32,40},{40,48},{48,56},{56,0},{1,9},... | collective-permute-start | bytes 688136 | tf_op jit(solution)/shard_map/ppermute | solution.py:67
  87.1 9.3 %collective-permute-start.8 = (bf16[64,1920]{1,0:T(8,128)(2,1)S(1)}, bf16[64,1920]{1,0:T(8,128)(2,1)S(1)}, u32[]{:S(2)}, u32[]{:S(2)}) collective-permute-start(bf16[64,1920]{1,0:T(8,128)(2,1)S(1)} %get-tuple-element.6), channel_id=1, source_target_pairs={{0,56},{8,0},{16,8},{24,16},{32,24},{40,32},{48,40},{56,48},{1,57}... | collective-permute-start | bytes 737288 | tf_op jit(solution)/shard_map/ppermute | solution.py:67
  92.7 9.3 %collective-permute-start.5 = (bf16[64,1920]{1,0:T(8,128)(2,1)S(1)}, bf16[64,1920]{1,0:T(8,128)(2,1)S(1)}, u32[]{:S(2)}, u32[]{:S(2)}) collective-permute-start(bf16[64,1920]{1,0:T(8,128)(2,1)S(1)} %get-tuple-element.5), channel_id=1, source_target_pairs={{0,8},{8,16},{16,24},{24,32},{32,40},{40,48},{48,56},{56,0},{1,9},... | collective-permute-start | bytes 737288 | tf_op jit(solution)/shard_map/ppermute | solution.py:67

commit v4 on v3

v4 whole, which is shorter than its diff:
```python
import jax
import jax.numpy as jnp
from jax import lax
from jax.sharding import Mesh, PartitionSpec as P

LANES = 128
SWAP = [(0, 1), (1, 0)]


def in_owner_order(out_grad, inner, outer):
    columns = out_grad.shape[1]
    rows = columns // (inner * outer * 2)
    new = lax.broadcasted_iota(jnp.int32, (columns, columns), 1)
    old = lax.broadcasted_iota(jnp.int32, (columns, columns), 0)
    row, rest = new % rows, new // rows
    i, rest = rest % inner, rest // inner
    y, core = rest % outer, rest // outer
    source = ((i * outer + y) * 2 + core) * rows + row
    one_hot = (source == old).astype(out_grad.dtype)
    moved = lax.dot_general(
        out_grad, one_hot, (((1,), (0,)), ((), ())), preferred_element_type=jnp.float32
    )
    return moved.astype(out_grad.dtype)


def add(left, right):
    return (left.astype(jnp.float32) + right.astype(jnp.float32)).astype(jnp.bfloat16)


def on_device(activations, out_grad):
    inner, outer = lax.axis_size("inner"), lax.axis_size("y")
    core, me = lax.axis_index("core"), lax.axis_index("y")
    width = activations.shape[1]
    ordered = in_owner_order(out_grad, inner, outer)
    columns = ordered.shape[1] // 2

    def half_of(owner):
        return lax.dynamic_slice_in_dim(
            ordered, owner * columns, columns, 1, allow_negative_indices=False
        )

    grads_other = lax.ppermute(half_of(1 - core), "core", SWAP)
    grads_other, sent = lax.optimization_barrier((grads_other, activations))
    activations_other = lax.ppermute(sent, "core", SWAP)
    grads = jnp.stack([half_of(core), grads_other])
    grads = lax.all_gather(grads, "x", axis=1, tiled=True)
    tokens = jnp.concatenate([activations, activations_other], axis=0)
    chunks = lax.dot_general(
        grads.reshape(tokens.shape[0], columns),
        tokens,
        (((0,), (0,)), ((), ())),
        preferred_element_type=jnp.float32,
    ).astype(jnp.bfloat16).reshape(outer, columns // outer, width)
    cut = -(-(width // LANES) // 2) * LANES
    spans = ((0, cut), (cut, width - cut))

    pairings = (
        [(s, s ^ 1) for s in range(outer)],
        [((s + 1) % outer, ((s ^ 1) + 1) % outer) for s in range(outer)],
    )
    way = 1 - 2 * lax.rem(me, 2)

    def own(piece, pairing, distance):
        start, size = spans[piece]
        owner = lax.rem(me + way * (distance if pairing == 0 else -distance) + outer, outer)
        block = lax.dynamic_slice(
            chunks, (owner, 0, start), (1, chunks.shape[1], size), allow_negative_indices=False
        )
        return block[0]

    far = outer // 2
    arrived = {}
    for distance in range(far, 0, -1):
        leaving = {}
        for piece in (0, 1):
            for pairing in (0, 1):
                if distance == far and piece != pairing:
                    continue
                block = own(piece, pairing, distance)
                if (piece, 1 - pairing) in arrived:
                    block = add(arrived[piece, 1 - pairing], block)
                elif (piece, pairing) in arrived:
                    block, arrived[piece, pairing] = lax.optimization_barrier(
                        (block, arrived[piece, pairing])
                    )
                leaving[piece, pairing] = lax.ppermute(block, "y", pairings[pairing])
        arrived = leaving
    sums = [
        (
            own(piece, 0, 0).astype(jnp.float32)
            + arrived[piece, 0].astype(jnp.float32)
            + arrived[piece, 1].astype(jnp.float32)
        ).astype(jnp.bfloat16)
        for piece in (0, 1)
    ]
    first = jnp.concatenate(sums, axis=1).reshape(inner, columns // outer // inner, width)
    blocks = lax.all_to_all(first, "inner", split_axis=0, concat_axis=0, tiled=True)
    return jnp.sum(blocks, axis=0, dtype=jnp.float32)


def solution(mesh):
    inner, outer, tensor = (mesh.shape[name] for name in ("inner", "outer", "tensor"))
    fine = Mesh(
        mesh.devices.reshape(inner, outer // 2, 2, tensor), ("inner", "y", "core", "x")
    )
    in_specs = (P(("inner", "y", "core"), "x"), P(("inner", "y", "core", "x"), None))
    out_specs = P(("inner", "y", "core"), "x")
    return jax.shard_map(
        on_device, mesh=fine, in_specs=in_specs, out_specs=out_specs, check_vma=False
    )
```

time: 134 us -> 123 us (0.918)
  starting transfers between devices: 50.1 us -> 42.8 us
  local copies, waits for them, and re-layouts: 6.4 us -> 1.12 us
  waiting for transfers between devices: 13 us -> 16.2 us
    ppermute x16, starting transfers between devices: 50.1 us -> 42.8 us  [the longest x14 38.9 us: on_device(): leaving[piece, pairing] = lax.ppermute(block, 'y', pairings[pairing])]
    slice x4 -> x0, local copies, waits for them, and re-layouts: 5.34 us -> none  [the longest x2 2.91 us: partial_sum(): activations_other[:, low:high]]
    ppermute x16, waiting for transfers between devices: 13 us -> 16.2 us  [the longest x14 14.9 us: on_device(): leaving[piece, pairing] = lax.ppermute(block, 'y', pairings[pairing])]
    dot_general x2 -> x1, matrix products: 5.96 us -> 5.1 us  [on_device(): lax.dot_general(grads.reshape(tokens.shape[0], columns), tokens, (((0,),...]
  transfers between devices with their start and end apart: 16 -> 16, of which waited for: 4 -> 7; matrix products, arithmetic and copies ran while one was open for 8% -> 1% of each run, Pallas kernels for 0% -> 0%
where the time goes in v4:
time: 123 us; the launch traced here: 122 us
  blocking collectives  53.3 us (43%)
  starting transfers between devices  42.8 us (35%)
  waiting for transfers between devices  16.2 us (13%)
  matrix products  6.53 us (5%)
  other arithmetic  1.71 us (1%)
    ppermute x14, starting transfers between devices, on_device(): leaving[piece, pairing] = lax.ppermute(block, 'y', pairings[pairing])  38.9 us
    all_to_all x1, blocking collectives, on_device(): lax.all_to_all(first, 'inner', split_axis=0, concat_axis=0, tiled=True)  29.1 us
    all_gather x1, blocking collectives, on_device(): grads = lax.all_gather(grads, 'x', axis=1, tiled=True)  24.1 us
    ppermute x14, waiting for transfers between devices, on_device(): leaving[piece, pairing] = lax.ppermute(block, 'y', pairings[pairing])  14.9 us
    dot_general x1, matrix products, on_device(): lax.dot_general(grads.reshape(tokens.shape[0], columns), tokens, (((0,),...  5.1 us
  transfers between devices with their start and end apart: 16, of which 7 were waited for; matrix products, arithmetic and copies ran while one was open for 1% of the time, Pallas kernels for 0%

profile of v4, /device:TPU:6, one launch (start us, length us, event | category | flops | bytes accessed | tf_op | source)
XLA Modules:
  0.0 122.0 jit_solution(1828404825211290909)
XLA Ops:
  0.0 0.0 copy-start
  0.0 0.9 copy-done
  0.9 1.4 %fusion.36 = bf16[1024,96]{0,1:T(8,128)(2,1)S(1)} fusion(bf16[96,1024]{1,0:T(8,128)(2,1)S(1)} %copy-done, s32[1024]{0:T(1024)S(1)} %get-tuple-element.32, s32[1024]{0:T(1024)S(1)} %get-tuple-element.33, s32[1024]{0:T(1024)S(1)} %get-tuple-element.31, s32[1024]{0:T(1024)S(1)} %get-tuple-element.34, pred[1024]{0:T(1024)(128)(4,1)S(1)} %get-tuple-element.29, ...), kind=kOutput, calls=%fused_computation.50 | convolution fusion | flops 250707968 | bytes 411648 | tf_op jit(solution)/shard_map/dot_general | solution.py:20
  2.4 1.9 %collective-permute-start = (bf16[96,512]{1,0:T(8,128)(2,1)S(1)}, bf16[96,512]{1,0:T(8,128)(2,1)S(1)}, u32[]{:S(2)}, u32[]{:S(2)}) collective-permute-start(bf16[96,512]{1,0:T(8,128)(2,1)S(1)} %get-tuple-element.28), channel_id=1, source_target_pairs={{0,4},{4,0},{1,5},{5,1},{2,6},{6,2},{3,7},{7,3},{8,12},{12,8},{9,1... | collective-permute-start | bytes 294920 | tf_op jit(solution)/shard_map/ppermute | solution.py:42
  4.3 1.3 %collective-permute-done = bf16[96,512]{1,0:T(8,128)(2,1)S(1)} collective-permute-done((bf16[96,512]{1,0:T(8,128)(2,1)S(1)}, bf16[96,512]{1,0:T(8,128)(2,1)S(1)}, u32[]{:S(2)}, u32[]{:S(2)}) %collective-permute-start) | collective-permute-done | bytes 98336 | tf_op jit(solution)/shard_map/ppermute | solution.py:42
  5.6 2.1 %collective-permute-start.1 = (bf16[384,3712]{1,0:T(8,128)(2,1)S(1)}, bf16[384,3712]{1,0:T(8,128)(2,1)}, u32[]{:S(2)}, u32[]{:S(2)}) collective-permute-start(bf16[384,3712]{1,0:T(8,128)(2,1)S(1)} %copy-done.1), channel_id=1, source_target_pairs={{0,4},{4,0},{1,5},{5,1},{2,6},{6,2},{3,7},{7,3},{8,12},{12,8},{9,1... | collective-permute-start | bytes 8552456 | tf_op jit(solution)/shard_map/ppermute | solution.py:44
  7.7 24.1 %all_gather.3 = bf16[2,384,512]{2,1,0:T(8,128)(2,1)S(1)} all-gather(bf16[2,96,512]{2,1,0:T(8,128)(2,1)S(1)} %pad_maximum_fusion.1), channel_id=1, replica_groups=mesh['inner'=16,'y'=8,'core'=2,'x'=4] {'x'}, dimensions={1}, use_global_device_ids=true | all-gather | bytes 983040 | tf_op jit(solution)/shard_map/all_gather | solution.py:46
  31.9 0.0 collective-permute-done.1
  31.9 5.1 %convolution_convert_fusion = bf16[512,3712]{1,0:T(8,128)(2,1)S(1)} fusion(bf16[768,512]{1,0:T(8,128)(2,1)S(1)} %bitcast.65, bf16[384,3712]{1,0:T(8,128)(2,1)} %collective-permute-done.1, bf16[384,3712]{1,0:T(8,128)(2,1)S(1)} %copy-done.1), kind=kOutput, calls=%fused_computation.13 | convolution fusion | flops 2932539392 | bytes 10289152 | tf_op jit(solution)/shard_map/dot_general | solution.py:48
  37.0 1.9 %collective-permute-start.9 = (bf16[64,1792]{1,0:T(8,128)(2,1)S(1)}, bf16[64,1792]{1,0:T(8,128)(2,1)S(1)}, u32[]{:S(2)}, u32[]{:S(2)}) collective-permute-start(bf16[64,1792]{1,0:T(8,128)(2,1)S(1)} %get-tuple-element.25), channel_id=1, source_target_pairs={{8,16},{16,8},{24,32},{32,24},{40,48},{48,40},{56,0},{0,56},{9,17}... | collective-permute-start | bytes 688136 | tf_op jit(solution)/shard_map/ppermute | solution.py:86
  39.0 1.9 %collective-permute-start.2 = (bf16[64,1920]{1,0:T(8,128)(2,1)S(1)}, bf16[64,1920]{1,0:T(8,128)(2,1)S(1)}, u32[]{:S(2)}, u32[]{:S(2)}) collective-permute-start(bf16[64,1920]{1,0:T(8,128)(2,1)S(1)} %get-tuple-element.19), channel_id=1, source_target_pairs={{0,8},{8,0},{16,24},{24,16},{32,40},{40,32},{48,56},{56,48},{1,9},... | collective-permute-start | bytes 737288 | tf_op jit(solution)/shard_map/ppermute | solution.py:86
  40.9 5.5 %collective-permute-done.9 = bf16[64,1792]{1,0:T(8,128)(2,1)S(1)} collective-permute-done((bf16[64,1792]{1,0:T(8,128)(2,1)S(1)}, bf16[64,1792]{1,0:T(8,128)(2,1)S(1)}, u32[]{:S(2)}, u32[]{:S(2)}) %collective-permute-start.9) | collective-permute-done | bytes 229408 | tf_op jit(solution)/shard_map/ppermute | solution.py:86
  46.5 0.1 fusion.50
  46.5 1.9 %collective-permute-start.10 = (bf16[64,1792]{1,0:T(8,128)(2,1)S(1)}, bf16[64,1792]{1,0:T(8,128)(2,1)S(1)}, u32[]{:S(2)}, u32[]{:S(2)}) collective-permute-start(bf16[64,1792]{1,0:T(8,128)(2,1)S(1)} %fusion.50), channel_id=1, source_target_pairs={{0,8},{8,0},{16,24},{24,16},{32,40},{40,32},{48,56},{56,48},{1,9},... | collective-permute-start | bytes 688136 | tf_op jit(solution)/shard_map/ppermute | solution.py:86
  48.5 2.2 %collective-permute-start.13 = (bf16[64,1792]{1,0:T(8,128)(2,1)S(1)}, bf16[64,1792]{1,0:T(8,128)(2,1)S(1)}, u32[]{:S(2)}, u32[]{:S(2)}) collective-permute-start(bf16[64,1792]{1,0:T(8,128)(2,1)S(1)} %get-tuple-element.14), channel_id=1, source_target_pairs={{8,16},{16,8},{24,32},{32,24},{40,48},{48,40},{56,0},{0,56},{9,17}... | collective-permute-start | bytes 688136 | tf_op jit(solution)/shard_map/ppermute | solution.py:86
  50.7 0.0 collective-permute-done.2
  50.7 3.6 %collective-permute-start.3 = (bf16[64,1920]{1,0:T(8,128)(2,1)S(1)}, bf16[64,1920]{1,0:T(8,128)(2,1)S(1)}, u32[]{:S(2)}, u32[]{:S(2)}) collective-permute-start(bf16[64,1920]{1,0:T(8,128)(2,1)S(1)} %get-tuple-element.12), channel_id=1, source_target_pairs={{0,8},{8,0},{16,24},{24,16},{32,40},{40,32},{48,56},{56,48},{1,9},... | collective-permute-start | bytes 737288 | tf_op jit(solution)/shard_map/ppermute | solution.py:86
  54.3 0.1 fusion.41
  54.4 3.1 %collective-permute-start.6 = (bf16[64,1920]{1,0:T(8,128)(2,1)S(1)}, bf16[64,1920]{1,0:T(8,128)(2,1)S(1)}, u32[]{:S(2)}, u32[]{:S(2)}) collective-permute-start(bf16[64,1920]{1,0:T(8,128)(2,1)S(1)} %fusion.41), channel_id=1, source_target_pairs={{8,16},{16,8},{24,32},{32,24},{40,48},{48,40},{56,0},{0,56},{9,17}... | collective-permute-start | bytes 737288 | tf_op jit(solution)/shard_map/ppermute | solution.py:86
  57.5 0.0 collective-permute-done.10
  57.5 0.1 collective-permute-done.13
  57.6 0.1 fusion.49
  57.8 3.8 %collective-permute-start.11 = (bf16[64,1792]{1,0:T(8,128)(2,1)S(1)}, bf16[64,1792]{1,0:T(8,128)(2,1)S(1)}, u32[]{:S(2)}, u32[]{:S(2)}) collective-permute-start(bf16[64,1792]{1,0:T(8,128)(2,1)S(1)} %get-tuple-element.23), channel_id=1, source_target_pairs={{8,16},{16,8},{24,32},{32,24},{40,48},{48,40},{56,0},{0,56},{9,17}... | collective-permute-start | bytes 688136 | tf_op jit(solution)/shard_map/ppermute | solution.py:86
  61.6 2.3 %collective-permute-start.14 = (bf16[64,1792]{1,0:T(8,128)(2,1)S(1)}, bf16[64,1792]{1,0:T(8,128)(2,1)S(1)}, u32[]{:S(2)}, u32[]{:S(2)}) collective-permute-start(bf16[64,1792]{1,0:T(8,128)(2,1)S(1)} %get-tuple-element.24), channel_id=1, source_target_pairs={{0,8},{8,0},{16,24},{24,16},{32,40},{40,32},{48,56},{56,48},{1,9},... | collective-permute-start | bytes 688136 | tf_op jit(solution)/shard_map/ppermute | solution.py:86
  63.9 0.0 collective-permute-done.3
  63.9 1.9 %collective-permute-done.6 = bf16[64,1920]{1,0:T(8,128)(2,1)S(1)} collective-permute-done((bf16[64,1920]{1,0:T(8,128)(2,1)S(1)}, bf16[64,1920]{1,0:T(8,128)(2,1)S(1)}, u32[]{:S(2)}, u32[]{:S(2)}) %collective-permute-start.6) | collective-permute-done | bytes 245792 | tf_op jit(solution)/shard_map/ppermute | solution.py:86
  65.8 0.1 fusion.43
  66.0 3.5 %collective-permute-start.4 = (bf16[64,1920]{1,0:T(8,128)(2,1)S(1)}, bf16[64,1920]{1,0:T(8,128)(2,1)S(1)}, u32[]{:S(2)}, u32[]{:S(2)}) collective-permute-start(bf16[64,1920]{1,0:T(8,128)(2,1)S(1)} %get-tuple-element.17), channel_id=1, source_target_pairs={{8,16},{16,8},{24,32},{32,24},{40,48},{48,40},{56,0},{0,56},{9,17}... | collective-permute-start | bytes 737288 | tf_op jit(solution)/shard_map/ppermute | solution.py:86
  69.4 2.1 %collective-permute-start.7 = (bf16[64,1920]{1,0:T(8,128)(2,1)S(1)}, bf16[64,1920]{1,0:T(8,128)(2,1)S(1)}, u32[]{:S(2)}, u32[]{:S(2)}) collective-permute-start(bf16[64,1920]{1,0:T(8,128)(2,1)S(1)} %get-tuple-element.18), channel_id=1, source_target_pairs={{0,8},{8,0},{16,24},{24,16},{32,40},{40,32},{48,56},{56,48},{1,9},... | collective-permute-start | bytes 737288 | tf_op jit(solution)/shard_map/ppermute | solution.py:86
  71.6 0.0 collective-permute-done.11
  71.6 0.0 collective-permute-done.14
  71.6 0.1 fusion.48
  71.7 3.4 %collective-permute-start.15 = (bf16[64,1792]{1,0:T(8,128)(2,1)S(1)}, bf16[64,1792]{1,0:T(8,128)(2,1)S(1)}, u32[]{:S(2)}, u32[]{:S(2)}) collective-permute-start(bf16[64,1792]{1,0:T(8,128)(2,1)S(1)} %get-tuple-element.22), channel_id=1, source_target_pairs={{8,16},{16,8},{24,32},{32,24},{40,48},{48,40},{56,0},{0,56},{9,17}... | collective-permute-start | bytes 688136 | tf_op jit(solution)/shard_map/ppermute | solution.py:86
  75.1 2.7 %collective-permute-start.12 = (bf16[64,1792]{1,0:T(8,128)(2,1)S(1)}, bf16[64,1792]{1,0:T(8,128)(2,1)S(1)}, u32[]{:S(2)}, u32[]{:S(2)}) collective-permute-start(bf16[64,1792]{1,0:T(8,128)(2,1)S(1)} %get-tuple-element.21), channel_id=1, source_target_pairs={{0,8},{8,0},{16,24},{24,16},{32,40},{40,32},{48,56},{56,48},{1,9},... | collective-permute-start | bytes 688136 | tf_op jit(solution)/shard_map/ppermute | solution.py:86
  77.8 0.0 collective-permute-done.4
  77.8 1.4 %collective-permute-done.7 = bf16[64,1920]{1,0:T(8,128)(2,1)S(1)} collective-permute-done((bf16[64,1920]{1,0:T(8,128)(2,1)S(1)}, bf16[64,1920]{1,0:T(8,128)(2,1)S(1)}, u32[]{:S(2)}, u32[]{:S(2)}) %collective-permute-start.7) | collective-permute-done | bytes 245792 | tf_op jit(solution)/shard_map/ppermute | solution.py:86
  79.2 0.1 fusion.42
  79.3 4.4 %collective-permute-start.8 = (bf16[64,1920]{1,0:T(8,128)(2,1)S(1)}, bf16[64,1920]{1,0:T(8,128)(2,1)S(1)}, u32[]{:S(2)}, u32[]{:S(2)}) collective-permute-start(bf16[64,1920]{1,0:T(8,128)(2,1)S(1)} %get-tuple-element.16), channel_id=1, source_target_pairs={{8,16},{16,8},{24,32},{32,24},{40,48},{48,40},{56,0},{0,56},{9,17}... | collective-permute-start | bytes 737288 | tf_op jit(solution)/shard_map/ppermute | solution.py:86
  83.7 1.9 %collective-permute-start.5 = (bf16[64,1920]{1,0:T(8,128)(2,1)S(1)}, bf16[64,1920]{1,0:T(8,128)(2,1)S(1)}, u32[]{:S(2)}, u32[]{:S(2)}) collective-permute-start(bf16[64,1920]{1,0:T(8,128)(2,1)S(1)} %get-tuple-element.15), channel_id=1, source_target_pairs={{0,8},{8,0},{16,24},{24,16},{32,40},{40,32},{48,56},{56,48},{1,9},... | collective-permute-start | bytes 737288 | tf_op jit(solution)/shard_map/ppermute | solution.py:86
  85.6 0.0 collective-permute-done.15
  85.6 0.0 collective-permute-done.12
  85.6 0.1 fusion.52
  85.7 2.9 %collective-permute-done.8 = bf16[64,1920]{1,0:T(8,128)(2,1)S(1)} collective-permute-done((bf16[64,1920]{1,0:T(8,128)(2,1)S(1)}, bf16[64,1920]{1,0:T(8,128)(2,1)S(1)}, u32[]{:S(2)}, u32[]{:S(2)}) %collective-permute-start.8) | collective-permute-done | bytes 245792 | tf_op jit(solution)/shard_map/ppermute | solution.py:86
  88.6 3.2 %collective-permute-done.5 = bf16[64,1920]{1,0:T(8,128)(2,1)S(1)} collective-permute-done((bf16[64,1920]{1,0:T(8,128)(2,1)S(1)}, bf16[64,1920]{1,0:T(8,128)(2,1)S(1)}, u32[]{:S(2)}, u32[]{:S(2)}) %collective-permute-start.5) | collective-permute-done | bytes 245792 | tf_op jit(solution)/shard_map/ppermute | solution.py:86
  91.8 0.1 fusion.45
  91.9 0.1 reshape.35
  92.0 29.1 %all_to_all.5 = bf16[16,4,3712]{2,1,0:T(4,128)(2,1)S(1)} all-to-all(bf16[16,4,3712]{2,1,0:T(4,128)(2,1)S(1)} %reshape.35), channel_id=1, replica_groups=mesh['inner'=16,'y'=8,'core'=2,'x'=4] {'inner'}, dimensions={0} | all-to-all | bytes 950272 | tf_op jit(solution)/shard_map/all_to_all | solution.py:97
  121.2 0.8 convert_reduce_fusion
  (10 shorter events, 0.2 us)
Async XLA Ops:
  0.0 0.9 copy-start
  0.9 4.7 %copy-start.1 = (bf16[384,3712]{1,0:T(8,128)(2,1)S(1)}, bf16[384,3712]{1,0:T(8,128)(2,1)}, u32[]{:S(2)}) copy-start(bf16[384,3712]{1,0:T(8,128)(2,1)} %param.2) | copy-start | bytes 8552452
  2.4 3.2 %collective-permute-start = (bf16[96,512]{1,0:T(8,128)(2,1)S(1)}, bf16[96,512]{1,0:T(8,128)(2,1)S(1)}, u32[]{:S(2)}, u32[]{:S(2)}) collective-permute-start(bf16[96,512]{1,0:T(8,128)(2,1)S(1)} %get-tuple-element.28), channel_id=1, source_target_pairs={{0,4},{4,0},{1,5},{5,1},{2,6},{6,2},{3,7},{7,3},{8,12},{12,8},{9,1... | collective-permute-start | bytes 294920 | tf_op jit(solution)/shard_map/ppermute | solution.py:42
  5.6 26.3 %collective-permute-start.1 = (bf16[384,3712]{1,0:T(8,128)(2,1)S(1)}, bf16[384,3712]{1,0:T(8,128)(2,1)}, u32[]{:S(2)}, u32[]{:S(2)}) collective-permute-start(bf16[384,3712]{1,0:T(8,128)(2,1)S(1)} %copy-done.1), channel_id=1, source_target_pairs={{0,4},{4,0},{1,5},{5,1},{2,6},{6,2},{3,7},{7,3},{8,12},{12,8},{9,1... | collective-permute-start | bytes 8552456 | tf_op jit(solution)/shard_map/ppermute | solution.py:44
  37.0 9.4 %collective-permute-start.9 = (bf16[64,1792]{1,0:T(8,128)(2,1)S(1)}, bf16[64,1792]{1,0:T(8,128)(2,1)S(1)}, u32[]{:S(2)}, u32[]{:S(2)}) collective-permute-start(bf16[64,1792]{1,0:T(8,128)(2,1)S(1)} %get-tuple-element.25), channel_id=1, source_target_pairs={{8,16},{16,8},{24,32},{32,24},{40,48},{48,40},{56,0},{0,56},{9,17}... | collective-permute-start | bytes 688136 | tf_op jit(solution)/shard_map/ppermute | solution.py:86
  39.0 11.7 %collective-permute-start.2 = (bf16[64,1920]{1,0:T(8,128)(2,1)S(1)}, bf16[64,1920]{1,0:T(8,128)(2,1)S(1)}, u32[]{:S(2)}, u32[]{:S(2)}) collective-permute-start(bf16[64,1920]{1,0:T(8,128)(2,1)S(1)} %get-tuple-element.19), channel_id=1, source_target_pairs={{0,8},{8,0},{16,24},{24,16},{32,40},{40,32},{48,56},{56,48},{1,9},... | collective-permute-start | bytes 737288 | tf_op jit(solution)/shard_map/ppermute | solution.py:86
  46.5 11.0 %collective-permute-start.10 = (bf16[64,1792]{1,0:T(8,128)(2,1)S(1)}, bf16[64,1792]{1,0:T(8,128)(2,1)S(1)}, u32[]{:S(2)}, u32[]{:S(2)}) collective-permute-start(bf16[64,1792]{1,0:T(8,128)(2,1)S(1)} %fusion.50), channel_id=1, source_target_pairs={{0,8},{8,0},{16,24},{24,16},{32,40},{40,32},{48,56},{56,48},{1,9},... | collective-permute-start | bytes 688136 | tf_op jit(solution)/shard_map/ppermute | solution.py:86
  48.5 9.2 %collective-permute-start.13 = (bf16[64,1792]{1,0:T(8,128)(2,1)S(1)}, bf16[64,1792]{1,0:T(8,128)(2,1)S(1)}, u32[]{:S(2)}, u32[]{:S(2)}) collective-permute-start(bf16[64,1792]{1,0:T(8,128)(2,1)S(1)} %get-tuple-element.14), channel_id=1, source_target_pairs={{8,16},{16,8},{24,32},{32,24},{40,48},{48,40},{56,0},{0,56},{9,17}... | collective-permute-start | bytes 688136 | tf_op jit(solution)/shard_map/ppermute | solution.py:86
  50.7 13.3 %collective-permute-start.3 = (bf16[64,1920]{1,0:T(8,128)(2,1)S(1)}, bf16[64,1920]{1,0:T(8,128)(2,1)S(1)}, u32[]{:S(2)}, u32[]{:S(2)}) collective-permute-start(bf16[64,1920]{1,0:T(8,128)(2,1)S(1)} %get-tuple-element.12), channel_id=1, source_target_pairs={{0,8},{8,0},{16,24},{24,16},{32,40},{40,32},{48,56},{56,48},{1,9},... | collective-permute-start | bytes 737288 | tf_op jit(solution)/shard_map/ppermute | solution.py:86
  54.4 11.4 %collective-permute-start.6 = (bf16[64,1920]{1,0:T(8,128)(2,1)S(1)}, bf16[64,1920]{1,0:T(8,128)(2,1)S(1)}, u32[]{:S(2)}, u32[]{:S(2)}) collective-permute-start(bf16[64,1920]{1,0:T(8,128)(2,1)S(1)} %fusion.41), channel_id=1, source_target_pairs={{8,16},{16,8},{24,32},{32,24},{40,48},{48,40},{56,0},{0,56},{9,17}... | collective-permute-start | bytes 737288 | tf_op jit(solution)/shard_map/ppermute | solution.py:86
  57.8 13.8 %collective-permute-start.11 = (bf16[64,1792]{1,0:T(8,128)(2,1)S(1)}, bf16[64,1792]{1,0:T(8,128)(2,1)S(1)}, u32[]{:S(2)}, u32[]{:S(2)}) collective-permute-start(bf16[64,1792]{1,0:T(8,128)(2,1)S(1)} %get-tuple-element.23), channel_id=1, source_target_pairs={{8,16},{16,8},{24,32},{32,24},{40,48},{48,40},{56,0},{0,56},{9,17}... | collective-permute-start | bytes 688136 | tf_op jit(solution)/shard_map/ppermute | solution.py:86
  61.6 10.0 %collective-permute-start.14 = (bf16[64,1792]{1,0:T(8,128)(2,1)S(1)}, bf16[64,1792]{1,0:T(8,128)(2,1)S(1)}, u32[]{:S(2)}, u32[]{:S(2)}) collective-permute-start(bf16[64,1792]{1,0:T(8,128)(2,1)S(1)} %get-tuple-element.24), channel_id=1, source_target_pairs={{0,8},{8,0},{16,24},{24,16},{32,40},{40,32},{48,56},{56,48},{1,9},... | collective-permute-start | bytes 688136 | tf_op jit(solution)/shard_map/ppermute | solution.py:86
  66.0 11.9 %collective-permute-start.4 = (bf16[64,1920]{1,0:T(8,128)(2,1)S(1)}, bf16[64,1920]{1,0:T(8,128)(2,1)S(1)}, u32[]{:S(2)}, u32[]{:S(2)}) collective-permute-start(bf16[64,1920]{1,0:T(8,128)(2,1)S(1)} %get-tuple-element.17), channel_id=1, source_target_pairs={{8,16},{16,8},{24,32},{32,24},{40,48},{48,40},{56,0},{0,56},{9,17}... | collective-permute-start | bytes 737288 | tf_op jit(solution)/shard_map/ppermute | solution.py:86
  69.4 9.8 %collective-permute-start.7 = (bf16[64,1920]{1,0:T(8,128)(2,1)S(1)}, bf16[64,1920]{1,0:T(8,128)(2,1)S(1)}, u32[]{:S(2)}, u32[]{:S(2)}) collective-permute-start(bf16[64,1920]{1,0:T(8,128)(2,1)S(1)} %get-tuple-element.18), channel_id=1, source_target_pairs={{0,8},{8,0},{16,24},{24,16},{32,40},{40,32},{48,56},{56,48},{1,9},... | collective-permute-start | bytes 737288 | tf_op jit(solution)/shard_map/ppermute | solution.py:86
  71.7 13.9 %collective-permute-start.15 = (bf16[64,1792]{1,0:T(8,128)(2,1)S(1)}, bf16[64,1792]{1,0:T(8,128)(2,1)S(1)}, u32[]{:S(2)}, u32[]{:S(2)}) collective-permute-start(bf16[64,1792]{1,0:T(8,128)(2,1)S(1)} %get-tuple-element.22), channel_id=1, source_target_pairs={{8,16},{16,8},{24,32},{32,24},{40,48},{48,40},{56,0},{0,56},{9,17}... | collective-permute-start | bytes 688136 | tf_op jit(solution)/shard_map/ppermute | solution.py:86
  75.1 10.5 %collective-permute-start.12 = (bf16[64,1792]{1,0:T(8,128)(2,1)S(1)}, bf16[64,1792]{1,0:T(8,128)(2,1)S(1)}, u32[]{:S(2)}, u32[]{:S(2)}) collective-permute-start(bf16[64,1792]{1,0:T(8,128)(2,1)S(1)} %get-tuple-element.21), channel_id=1, source_target_pairs={{0,8},{8,0},{16,24},{24,16},{32,40},{40,32},{48,56},{56,48},{1,9},... | collective-permute-start | bytes 688136 | tf_op jit(solution)/shard_map/ppermute | solution.py:86
  79.3 9.3 %collective-permute-start.8 = (bf16[64,1920]{1,0:T(8,128)(2,1)S(1)}, bf16[64,1920]{1,0:T(8,128)(2,1)S(1)}, u32[]{:S(2)}, u32[]{:S(2)}) collective-permute-start(bf16[64,1920]{1,0:T(8,128)(2,1)S(1)} %get-tuple-element.16), channel_id=1, source_target_pairs={{8,16},{16,8},{24,32},{32,24},{40,48},{48,40},{56,0},{0,56},{9,17}... | collective-permute-start | bytes 737288 | tf_op jit(solution)/shard_map/ppermute | solution.py:86
  83.7 8.1 %collective-permute-start.5 = (bf16[64,1920]{1,0:T(8,128)(2,1)S(1)}, bf16[64,1920]{1,0:T(8,128)(2,1)S(1)}, u32[]{:S(2)}, u32[]{:S(2)}) collective-permute-start(bf16[64,1920]{1,0:T(8,128)(2,1)S(1)} %get-tuple-element.15), channel_id=1, source_target_pairs={{0,8},{8,0},{16,24},{24,16},{32,40},{40,32},{48,56},{56,48},{1,9},... | collective-permute-start | bytes 737288 | tf_op jit(solution)/shard_map/ppermute | solution.py:86

commit v5 on v1

v5 whole, which is shorter than its diff:
```python
import jax
import jax.numpy as jnp
from jax import lax
from jax.sharding import Mesh, PartitionSpec as P

LANES = 128
SWAP = [(0, 1), (1, 0)]


def in_owner_order(out_grad, far, near, outer):
    columns = out_grad.shape[1]
    rows = columns // (far * near * outer * 2)
    new = lax.broadcasted_iota(jnp.int32, (columns, columns), 1)
    old = lax.broadcasted_iota(jnp.int32, (columns, columns), 0)
    row, rest = new % rows, new // rows
    f, rest = rest % far, rest // far
    y, rest = rest % outer, rest // outer
    n, core = rest % near, rest // near
    source = (((f * near + n) * outer + y) * 2 + core) * rows + row
    one_hot = (source == old).astype(out_grad.dtype)
    moved = lax.dot_general(
        out_grad, one_hot, (((1,), (0,)), ((), ())), preferred_element_type=jnp.float32
    )
    return moved.astype(out_grad.dtype)


def pairings_of(count):
    return (
        [(s, s ^ 1) for s in range(count)],
        [((s + 1) % count, ((s ^ 1) + 1) % count) for s in range(count)],
    )


def on_device(activations, out_grad):
    far_z, near_z, outer = (lax.axis_size(name) for name in ("far", "near", "y"))
    core, me, near = (lax.axis_index(name) for name in ("core", "y", "near"))
    width = activations.shape[1]
    ordered = in_owner_order(out_grad, far_z, near_z, outer)
    columns = ordered.shape[1] // 2

    def half_of(owner):
        return lax.dynamic_slice_in_dim(
            ordered, owner * columns, columns, 1, allow_negative_indices=False
        )

    grads_other = lax.ppermute(half_of(1 - core), "core", SWAP)
    grads_other, sent = lax.optimization_barrier((grads_other, activations))
    activations_other = lax.ppermute(sent, "core", SWAP)
    grads = jnp.stack([half_of(core), grads_other])
    grads = lax.all_gather(grads, "x", axis=1, tiled=True)
    grads = grads.reshape(2 * grads.shape[1], columns)
    rows = columns // outer // near_z
    half = columns // near_z

    def rows_for(owner, mine, theirs):
        product = lax.dot_general(
            lax.dynamic_slice_in_dim(grads, owner * half, half, 1, allow_negative_indices=False),
            jnp.concatenate([mine, theirs], axis=0),
            (((0,), (0,)), ((), ())),
            preferred_element_type=jnp.float32,
        )
        return product.astype(jnp.bfloat16).reshape(outer, rows, width)

    leaving = rows_for(1 - near, activations, activations_other)
    kept = rows_for(near, *lax.optimization_barrier((activations, activations_other)))

    groups = width // LANES
    part = groups * 5 // 18
    cut, middle = (LANES * (groups - 2 * part), LANES * (groups - part))
    pieces = (((0, cut),), ((cut, middle), (middle, width)))

    def block_of(source, owner, low, high):
        block = lax.dynamic_slice(
            source, (owner, 0, low), (1, rows, high - low), allow_negative_indices=False
        )
        return block[0].astype(jnp.float32)

    z_pairings = pairings_of(far_z * near_z)
    incoming = [
        lax.ppermute(leaving[:, :, low:high], ("far", "near"), z_pairings[k])
        for k, (low, high) in enumerate(pieces[1])
    ]

    y_pairings = pairings_of(outer)
    way = 1 - 2 * lax.rem(me, 2)

    def own(piece, pairing, distance):
        owner = lax.rem(me + way * (distance if pairing == 0 else -distance) + outer, outer)
        if piece == 0:
            sources = (leaving, kept)
            return jnp.concatenate([block_of(rows_, owner, 0, cut) for rows_ in sources], axis=0)
        parts = [
            block_of(kept, owner, low, high) + block_of(incoming[k], owner, 0, high - low)
            for k, (low, high) in enumerate(pieces[1])
        ]
        return jnp.concatenate(parts, axis=1)

    farthest = outer // 2

    def step(piece, distance, arrived):
        blocks = {}
        for pairing in (0, 1):
            if distance == farthest and piece != pairing:
                continue
            block = own(piece, pairing, distance)
            if 1 - pairing in arrived:
                block = block + arrived[1 - pairing].astype(jnp.float32)
            blocks[pairing] = block.astype(jnp.bfloat16)
        if distance == farthest - 1:
            blocks = lax.optimization_barrier(blocks)
        moved = {k: lax.ppermute(block, "y", y_pairings[k]) for k, block in blocks.items()}
        return lax.optimization_barrier(moved)

    arrived = [{}, {}]
    for distance in range(farthest, 0, -1):
        for piece in (0, 1):
            arrived[piece] = step(piece, distance, arrived[piece])
            if distance == farthest and piece == 0:
                arrived[0], incoming[:] = lax.optimization_barrier((arrived[0], incoming))
    sums = [
        own(piece, 0, 0)
        + arrived[piece][0].astype(jnp.float32)
        + arrived[piece][1].astype(jnp.float32)
        for piece in (0, 1)
    ]
    late_other = lax.ppermute(sums[0][:rows].astype(jnp.bfloat16), "near", SWAP)
    late = sums[0][rows:] + late_other.astype(jnp.float32)
    first = jnp.concatenate([late.astype(jnp.bfloat16), sums[1].astype(jnp.bfloat16)], axis=1)
    first = first.reshape(far_z, rows // far_z, width)
    blocks = lax.all_to_all(first, "far", split_axis=0, concat_axis=0, tiled=True)
    return jnp.sum(blocks, axis=0, dtype=jnp.float32)


def solution(mesh):
    inner, outer, tensor = (mesh.shape[name] for name in ("inner", "outer", "tensor"))
    fine = Mesh(
        mesh.devices.reshape(inner // 2, 2, outer // 2, 2, tensor),
        ("far", "near", "y", "core", "x"),
    )
    groups = ("far", "near", "y", "core")
    in_specs = (P(groups, "x"), P(groups + ("x",), None))
    return jax.shard_map(
        on_device, mesh=fine, in_specs=in_specs, out_specs=P(groups, "x"), check_vma=False
    )
```

time: 450 us -> 138 us (0.31)
  waiting for transfers between devices: 368 us -> 16.7 us
  starting transfers between devices: 0.01 us -> 64.4 us
  local copies, waits for them, and re-layouts: 37.1 us -> 1.33 us
  blocking collectives: 23.6 us -> 44.5 us
  between operations: 13.4 us -> 0.44 us
    unnamed x2 -> x0, waiting for transfers between devices: 368 us -> none
    ppermute x0 -> x19, starting transfers between devices: none -> 64.4 us  [the longest x14 46.1 us: step(): lax.ppermute(block, 'y', y_pairings[k])]
    reshape x2 -> x1, local copies, waits for them, and re-layouts: 24.2 us -> 0.06 us  [on_device(): first = first.reshape(far_z, rows // far_z, width)]
    all_to_all x0 -> x1, blocking collectives: none -> 20.4 us  [on_device(): lax.all_to_all(first, 'far', split_axis=0, concat_axis=0, tiled=True)]
    ppermute x0 -> x19, waiting for transfers between devices: none -> 16.7 us  [the longest x14 12.2 us: step(): lax.ppermute(block, 'y', y_pairings[k])]
    transpose x1 -> x0, local copies, waits for them, and re-layouts: 11.5 us -> none  [on_device(): partial_sum.reshape(owners, rows, groups, LANES).transpose(0, 2, 1, 3)]
  transfers between devices with their start and end apart: 1 -> 19, of which waited for: 1 -> 8; matrix products, arithmetic and copies ran while one was open for 0% -> 3% of each run, Pallas kernels for 0% -> 0%
where the time goes in v5:
time: 138 us
  starting transfers between devices  64.4 us (47%)
  blocking collectives  44.5 us (32%)
  waiting for transfers between devices  16.7 us (12%)
  matrix products  8.56 us (6%)
  other arithmetic  1.78 us (1%)
    ppermute x14, starting transfers between devices, step(): lax.ppermute(block, 'y', y_pairings[k])  46.1 us
    all_gather x1, blocking collectives, on_device(): grads = lax.all_gather(grads, 'x', axis=1, tiled=True)  24.1 us
    all_to_all x1, blocking collectives, on_device(): lax.all_to_all(first, 'far', split_axis=0, concat_axis=0, tiled=True)  20.4 us
    ppermute x14, waiting for transfers between devices, step(): lax.ppermute(block, 'y', y_pairings[k])  12.2 us
    ppermute x2, starting transfers between devices, on_device(): lax.ppermute(leaving[:, :, low:high], ('far', 'near'), z_pairings[k])  10.4 us
    dot_general x2, matrix products, rows_for(): lax.dot_general(lax.dynamic_slice_in_dim(grads, owner * half, half, 1, al...  7.1 us
    ppermute x1, starting transfers between devices, on_device(): late_other = lax.ppermute(sums[0][:rows].astype(jnp.bfloat16), 'near', SWAP)  3.91 us
    ppermute x1, waiting for transfers between devices, on_device(): late_other = lax.ppermute(sums[0][:rows].astype(jnp.bfloat16), 'near', SWAP)  3.26 us
  transfers between devices with their start and end apart: 19, of which 8 were waited for; matrix products, arithmetic and copies ran while one was open for 3% of the time, Pallas kernels for 0%

profile of v5, /device:TPU:6, one launch (start us, length us, event | category | flops | bytes accessed | tf_op | source)
XLA Modules:
  0.0 137.7 jit_solution(17014990510047001356)
XLA Ops:
  0.0 0.9 copy-done
  0.9 1.5 %fusion.49 = bf16[1024,96]{0,1:T(8,128)(2,1)S(1)} fusion(bf16[96,1024]{1,0:T(8,128)(2,1)S(1)} %copy-done, s32[1024]{0:T(1024)S(1)} %get-tuple-element.98, s32[1024]{0:T(1024)S(1)} %get-tuple-element.99, s32[1024]{0:T(1024)S(1)} %get-tuple-element.97, s32[1024]{0:T(1024)S(1)} %get-tuple-element.100, pred[1024]{0:T(1024)(128)(4,1)S(1)} %get-tuple-element.95, ...), kind=kOutput, calls=%fused_computation.64 | convolution fusion | flops 272728064 | bytes 411648 | tf_op jit(solution)/shard_map/dot_general | solution.py:21
  2.4 1.9 %collective-permute-start = (bf16[96,512]{1,0:T(8,128)(2,1)S(1)}, bf16[96,512]{1,0:T(8,128)(2,1)S(1)}, u32[]{:S(2)}, u32[]{:S(2)}) collective-permute-start(bf16[96,512]{1,0:T(8,128)(2,1)S(1)} %get-tuple-element.94), channel_id=1, source_target_pairs={{0,4},{4,0},{1,5},{5,1},{2,6},{6,2},{3,7},{7,3},{8,12},{12,8},{9,1... | collective-permute-start | bytes 294920 | tf_op jit(solution)/shard_map/ppermute | solution.py:46
  4.4 1.3 collective-permute-done
  5.6 2.1 %collective-permute-start.1 = (bf16[384,3712]{1,0:T(8,128)(2,1)S(1)}, bf16[384,3712]{1,0:T(8,128)(2,1)}, u32[]{:S(2)}, u32[]{:S(2)}) collective-permute-start(bf16[384,3712]{1,0:T(8,128)(2,1)S(1)} %copy-done.1), channel_id=1, source_target_pairs={{0,4},{4,0},{1,5},{5,1},{2,6},{6,2},{3,7},{7,3},{8,12},{12,8},{9,1... | collective-permute-start | bytes 8552456 | tf_op jit(solution)/shard_map/ppermute | solution.py:48
  7.8 24.1 %all_gather.3 = bf16[2,384,512]{2,1,0:T(8,128)(2,1)S(1)} all-gather(bf16[2,96,512]{2,1,0:T(8,128)(2,1)S(1)} %pad_maximum_fusion.3), channel_id=1, replica_groups=mesh['far'=8,'near'=2,'y'=8,'core'=2,'x'=4] {'x'}, dimensions={1}, use_global_device_ids=true | all-gather | bytes 983040 | tf_op jit(solution)/shard_map/all_gather | solution.py:50
  31.9 3.5 %fusion.11 = bf16[256,3712]{1,0:T(8,128)(2,1)S(1)} fusion(bf16[384,3712]{1,0:T(8,128)(2,1)} %collective-permute-done.1, bf16[384,3712]{1,0:T(8,128)(2,1)S(1)} %copy-done.1, bf16[768,512]{1,0:T(8,128)(2,1)S(1)} %bitcast.79, s32[]{:T(128)S(6)} %mul.61), kind=kOutput, calls=%fused_computation.27 | convolution fusion | flops 1471971328 | bytes 7995396 | tf_op jit(solution)/shard_map/dot_general | solution.py:56
  35.4 0.1 fusion.84
  35.6 8.5 %collective-permute-start.4 = (bf16[8,32,1024]{2,1,0:T(8,128)(2,1)S(1)}, bf16[8,32,1024]{2,1,0:T(8,128)(2,1)S(1)}, u32[]{:S(2)}, u32[]{:S(2)}) collective-permute-start(bf16[8,32,1024]{2,1,0:T(8,128)(2,1)S(1)} %get-tuple-element.91), channel_id=1, source_target_pairs={{64,128},{128,64},{192,256},{256,192},{320,384},{384,320},{448,512... | collective-permute-start | bytes 1572872 | tf_op jit(solution)/shard_map/ppermute | solution.py:80
  44.1 1.9 %collective-permute-start.3 = (bf16[8,32,1024]{2,1,0:T(8,128)(2,1)S(1)}, bf16[8,32,1024]{2,1,0:T(8,128)(2,1)S(1)}, u32[]{:S(2)}, u32[]{:S(2)}) collective-permute-start(bf16[8,32,1024]{2,1,0:T(8,128)(2,1)S(1)} %get-tuple-element.92), channel_id=1, source_target_pairs={{0,64},{64,0},{128,192},{192,128},{256,320},{320,256},{384,448},{4... | collective-permute-start | bytes 1572872 | tf_op jit(solution)/shard_map/ppermute | solution.py:80
  46.0 3.6 %fusion.8 = bf16[256,3712]{1,0:T(8,128)(2,1)S(1)} fusion(bf16[384,3712]{1,0:T(8,128)(2,1)} %collective-permute-done.1, bf16[384,3712]{1,0:T(8,128)(2,1)S(1)} %copy-done.1, bf16[768,512]{1,0:T(8,128)(2,1)S(1)} %bitcast.80, s32[]{:T(128)S(6)} %mul.62), kind=kOutput, calls=%fused_computation.26 | convolution fusion | flops 1471971328 | bytes 7995396 | tf_op jit(solution)/shard_map/dot_general | solution.py:56
  49.6 0.1 dynamic-slice_bitcast_fusion.15
  49.7 0.1 dynamic-slice_bitcast_fusion.14
  49.8 3.5 %collective-permute-start.2 = (bf16[64,1664]{1,0:T(8,128)(2,1)S(1)}, bf16[64,1664]{1,0:T(8,128)(2,1)S(1)}, u32[]{:S(2)}, u32[]{:S(2)}) collective-permute-start(bf16[64,1664]{1,0:T(8,128)(2,1)S(1)} %pad_maximum_fusion.2), channel_id=1, source_target_pairs={{0,8},{8,0},{16,24},{24,16},{32,40},{40,32},{48,56},{56,48},{1,9},... | collective-permute-start | bytes 638984 | tf_op jit(solution)/shard_map/ppermute | solution.py:111
  53.4 4.2 %collective-permute-done.2 = bf16[64,1664]{1,0:T(8,128)(2,1)S(1)} collective-permute-done((bf16[64,1664]{1,0:T(8,128)(2,1)S(1)}, bf16[64,1664]{1,0:T(8,128)(2,1)S(1)}, u32[]{:S(2)}, u32[]{:S(2)}) %collective-permute-start.2) | collective-permute-done | bytes 213024 | tf_op jit(solution)/shard_map/ppermute | solution.py:111
  57.6 0.0 collective-permute-done.4
  57.6 0.0 collective-permute-done.3
  57.6 0.1 add_convert_fusion.4
  57.6 0.3 add_bitcast_fusion.1
  58.0 5.4 %collective-permute-start.12 = (bf16[32,2048]{1,0:T(8,128)(2,1)S(1)}, bf16[32,2048]{1,0:T(8,128)(2,1)S(1)}, u32[]{:S(2)}, u32[]{:S(2)}) collective-permute-start(bf16[32,2048]{1,0:T(8,128)(2,1)S(1)} %pad_maximum_fusion.4), channel_id=1, source_target_pairs={{8,16},{16,8},{24,32},{32,24},{40,48},{48,40},{56,0},{0,56},{9,17}... | collective-permute-start | bytes 393224 | tf_op jit(solution)/shard_map/ppermute | solution.py:111
  63.4 1.9 %collective-permute-start.5 = (bf16[64,1664]{1,0:T(8,128)(2,1)S(1)}, bf16[64,1664]{1,0:T(8,128)(2,1)S(1)}, u32[]{:S(2)}, u32[]{:S(2)}) collective-permute-start(bf16[64,1664]{1,0:T(8,128)(2,1)S(1)} %pad_maximum_fusion.1), channel_id=1, source_target_pairs={{0,8},{8,0},{16,24},{24,16},{32,40},{40,32},{48,56},{56,48},{1,9},... | collective-permute-start | bytes 638984 | tf_op jit(solution)/shard_map/ppermute | solution.py:111
  65.3 4.6 %collective-permute-start.6 = (bf16[64,1664]{1,0:T(8,128)(2,1)S(1)}, bf16[64,1664]{1,0:T(8,128)(2,1)S(1)}, u32[]{:S(2)}, u32[]{:S(2)}) collective-permute-start(bf16[64,1664]{1,0:T(8,128)(2,1)S(1)} %add_convert_fusion.4), channel_id=1, source_target_pairs={{8,16},{16,8},{24,32},{32,24},{40,48},{48,40},{56,0},{0,56},{9,17}... | collective-permute-start | bytes 638984 | tf_op jit(solution)/shard_map/ppermute | solution.py:111
  70.0 3.2 %collective-permute-start.13 = (bf16[32,2048]{1,0:T(8,128)(2,1)S(1)}, bf16[32,2048]{1,0:T(8,128)(2,1)S(1)}, u32[]{:S(2)}, u32[]{:S(2)}) collective-permute-start(bf16[32,2048]{1,0:T(8,128)(2,1)S(1)} %fusion.58), channel_id=1, source_target_pairs={{0,8},{8,0},{16,24},{24,16},{32,40},{40,32},{48,56},{56,48},{1,9},... | collective-permute-start | bytes 393224 | tf_op jit(solution)/shard_map/ppermute | solution.py:111
  73.2 2.4 %collective-permute-start.14 = (bf16[32,2048]{1,0:T(8,128)(2,1)S(1)}, bf16[32,2048]{1,0:T(8,128)(2,1)S(1)}, u32[]{:S(2)}, u32[]{:S(2)}) collective-permute-start(bf16[32,2048]{1,0:T(8,128)(2,1)S(1)} %pad_maximum_fusion.5), channel_id=1, source_target_pairs={{8,16},{16,8},{24,32},{32,24},{40,48},{48,40},{56,0},{0,56},{9,17}... | collective-permute-start | bytes 393224 | tf_op jit(solution)/shard_map/ppermute | solution.py:111
  75.6 0.0 collective-permute-done.5
  75.6 0.1 add_convert_fusion.2
  75.7 4.7 %collective-permute-start.8 = (bf16[64,1664]{1,0:T(8,128)(2,1)S(1)}, bf16[64,1664]{1,0:T(8,128)(2,1)S(1)}, u32[]{:S(2)}, u32[]{:S(2)}) collective-permute-start(bf16[64,1664]{1,0:T(8,128)(2,1)S(1)} %add_convert_fusion.2), channel_id=1, source_target_pairs={{8,16},{16,8},{24,32},{32,24},{40,48},{48,40},{56,0},{0,56},{9,17}... | collective-permute-start | bytes 638984 | tf_op jit(solution)/shard_map/ppermute | solution.py:111
  80.4 0.9 collective-permute-done.14
  81.3 1.9 %collective-permute-start.15 = (bf16[32,2048]{1,0:T(8,128)(2,1)S(1)}, bf16[32,2048]{1,0:T(8,128)(2,1)S(1)}, u32[]{:S(2)}, u32[]{:S(2)}) collective-permute-start(bf16[32,2048]{1,0:T(8,128)(2,1)S(1)} %fusion.57), channel_id=1, source_target_pairs={{0,8},{8,0},{16,24},{24,16},{32,40},{40,32},{48,56},{56,48},{1,9},... | collective-permute-start | bytes 393224 | tf_op jit(solution)/shard_map/ppermute | solution.py:111
  83.3 3.5 %collective-permute-start.16 = (bf16[32,2048]{1,0:T(8,128)(2,1)S(1)}, bf16[32,2048]{1,0:T(8,128)(2,1)S(1)}, u32[]{:S(2)}, u32[]{:S(2)}) collective-permute-start(bf16[32,2048]{1,0:T(8,128)(2,1)S(1)} %fusion.59), channel_id=1, source_target_pairs={{8,16},{16,8},{24,32},{32,24},{40,48},{48,40},{56,0},{0,56},{9,17}... | collective-permute-start | bytes 393224 | tf_op jit(solution)/shard_map/ppermute | solution.py:111
  86.8 0.1 add_convert_fusion.3
  86.9 2.5 %collective-permute-start.7 = (bf16[64,1664]{1,0:T(8,128)(2,1)S(1)}, bf16[64,1664]{1,0:T(8,128)(2,1)S(1)}, u32[]{:S(2)}, u32[]{:S(2)}) collective-permute-start(bf16[64,1664]{1,0:T(8,128)(2,1)S(1)} %add_convert_fusion.3), channel_id=1, source_target_pairs={{0,8},{8,0},{16,24},{24,16},{32,40},{40,32},{48,56},{56,48},{1,9},... | collective-permute-start | bytes 638984 | tf_op jit(solution)/shard_map/ppermute | solution.py:111
  89.4 0.1 collective-permute-done.15
  89.5 1.9 %collective-permute-done.16 = bf16[32,2048]{1,0:T(8,128)(2,1)S(1)} collective-permute-done((bf16[32,2048]{1,0:T(8,128)(2,1)S(1)}, bf16[32,2048]{1,0:T(8,128)(2,1)S(1)}, u32[]{:S(2)}, u32[]{:S(2)}) %collective-permute-start.16) | collective-permute-done | bytes 131104 | tf_op jit(solution)/shard_map/ppermute | solution.py:111
  91.4 2.7 %collective-permute-start.17 = (bf16[32,2048]{1,0:T(8,128)(2,1)S(1)}, bf16[32,2048]{1,0:T(8,128)(2,1)S(1)}, u32[]{:S(2)}, u32[]{:S(2)}) collective-permute-start(bf16[32,2048]{1,0:T(8,128)(2,1)S(1)} %fusion.56), channel_id=1, source_target_pairs={{0,8},{8,0},{16,24},{24,16},{32,40},{40,32},{48,56},{56,48},{1,9},... | collective-permute-start | bytes 393224 | tf_op jit(solution)/shard_map/ppermute | solution.py:111
  94.1 0.5 collective-permute-done.7
  94.6 0.1 add_convert_fusion
  94.7 3.7 %collective-permute-start.10 = (bf16[64,1664]{1,0:T(8,128)(2,1)S(1)}, bf16[64,1664]{1,0:T(8,128)(2,1)S(1)}, u32[]{:S(2)}, u32[]{:S(2)}) collective-permute-start(bf16[64,1664]{1,0:T(8,128)(2,1)S(1)} %add_convert_fusion), channel_id=1, source_target_pairs={{8,16},{16,8},{24,32},{32,24},{40,48},{48,40},{56,0},{0,56},{9,17}... | collective-permute-start | bytes 638984 | tf_op jit(solution)/shard_map/ppermute | solution.py:111
  98.4 0.1 add_convert_fusion.1
  98.5 2.5 %collective-permute-start.9 = (bf16[64,1664]{1,0:T(8,128)(2,1)S(1)}, bf16[64,1664]{1,0:T(8,128)(2,1)S(1)}, u32[]{:S(2)}, u32[]{:S(2)}) collective-permute-start(bf16[64,1664]{1,0:T(8,128)(2,1)S(1)} %add_convert_fusion.1), channel_id=1, source_target_pairs={{0,8},{8,0},{16,24},{24,16},{32,40},{40,32},{48,56},{56,48},{1,9},... | collective-permute-start | bytes 638984 | tf_op jit(solution)/shard_map/ppermute | solution.py:111
  101.1 3.5 %collective-permute-start.18 = (bf16[32,2048]{1,0:T(8,128)(2,1)S(1)}, bf16[32,2048]{1,0:T(8,128)(2,1)S(1)}, u32[]{:S(2)}, u32[]{:S(2)}) collective-permute-start(bf16[32,2048]{1,0:T(8,128)(2,1)S(1)} %fusion.60), channel_id=1, source_target_pairs={{8,16},{16,8},{24,32},{32,24},{40,48},{48,40},{56,0},{0,56},{9,17}... | collective-permute-start | bytes 393224 | tf_op jit(solution)/shard_map/ppermute | solution.py:111
  104.6 4.6 %collective-permute-done.18 = bf16[32,2048]{1,0:T(8,128)(2,1)S(1)} collective-permute-done((bf16[32,2048]{1,0:T(8,128)(2,1)S(1)}, bf16[32,2048]{1,0:T(8,128)(2,1)S(1)}, u32[]{:S(2)}, u32[]{:S(2)}) %collective-permute-start.18) | collective-permute-done | bytes 131104 | tf_op jit(solution)/shard_map/ppermute | solution.py:111
  109.1 0.1 convert_add_fusion
  109.3 3.9 %collective-permute-start.11 = (bf16[32,1664]{1,0:T(8,128)(2,1)S(1)}, bf16[32,1664]{1,0:T(8,128)(2,1)S(1)}, u32[]{:S(2)}, u32[]{:S(2)}) collective-permute-start(bf16[32,1664]{1,0:T(8,128)(2,1)S(1)} %slice.25), channel_id=1, source_target_pairs={{0,64},{64,0},{1,65},{65,1},{2,66},{66,2},{3,67},{67,3},{4,68},{68... | collective-permute-start | bytes 319496 | tf_op jit(solution)/shard_map/ppermute | solution.py:126
  113.2 3.3 %collective-permute-done.11 = bf16[32,1664]{1,0:T(8,128)(2,1)S(1)} collective-permute-done((bf16[32,1664]{1,0:T(8,128)(2,1)S(1)}, bf16[32,1664]{1,0:T(8,128)(2,1)S(1)}, u32[]{:S(2)}, u32[]{:S(2)}) %collective-permute-start.11) | collective-permute-done | bytes 106528 | tf_op jit(solution)/shard_map/ppermute | solution.py:126
  116.5 0.1 reshape.99
  116.6 20.4 %all_to_all.5 = bf16[8,4,3712]{2,1,0:T(4,128)(2,1)S(1)} all-to-all(bf16[8,4,3712]{2,1,0:T(4,128)(2,1)S(1)} %reshape.99), channel_id=1, replica_groups=mesh['far'=8,'near'=2,'y'=8,'core'=2,'x'=4] {'far'}, dimensions={0} | all-to-all | bytes 475136 | tf_op jit(solution)/shard_map/all_to_all | solution.py:130
  137.0 0.7 convert_reduce_fusion
  (29 shorter events, 0.4 us)
Async XLA Ops:
  0.0 0.9 copy-start
  0.9 4.7 %copy-start.1 = (bf16[384,3712]{1,0:T(8,128)(2,1)S(1)}, bf16[384,3712]{1,0:T(8,128)(2,1)}, u32[]{:S(2)}) copy-start(bf16[384,3712]{1,0:T(8,128)(2,1)} %param.2) | copy-start | bytes 8552452
  2.4 3.2 %collective-permute-start = (bf16[96,512]{1,0:T(8,128)(2,1)S(1)}, bf16[96,512]{1,0:T(8,128)(2,1)S(1)}, u32[]{:S(2)}, u32[]{:S(2)}) collective-permute-start(bf16[96,512]{1,0:T(8,128)(2,1)S(1)} %get-tuple-element.94), channel_id=1, source_target_pairs={{0,4},{4,0},{1,5},{5,1},{2,6},{6,2},{3,7},{7,3},{8,12},{12,8},{9,1... | collective-permute-start | bytes 294920 | tf_op jit(solution)/shard_map/ppermute | solution.py:46
  5.6 26.3 %collective-permute-start.1 = (bf16[384,3712]{1,0:T(8,128)(2,1)S(1)}, bf16[384,3712]{1,0:T(8,128)(2,1)}, u32[]{:S(2)}, u32[]{:S(2)}) collective-permute-start(bf16[384,3712]{1,0:T(8,128)(2,1)S(1)} %copy-done.1), channel_id=1, source_target_pairs={{0,4},{4,0},{1,5},{5,1},{2,6},{6,2},{3,7},{7,3},{8,12},{12,8},{9,1... | collective-permute-start | bytes 8552456 | tf_op jit(solution)/shard_map/ppermute | solution.py:48
  35.6 22.0 %collective-permute-start.4 = (bf16[8,32,1024]{2,1,0:T(8,128)(2,1)S(1)}, bf16[8,32,1024]{2,1,0:T(8,128)(2,1)S(1)}, u32[]{:S(2)}, u32[]{:S(2)}) collective-permute-start(bf16[8,32,1024]{2,1,0:T(8,128)(2,1)S(1)} %get-tuple-element.91), channel_id=1, source_target_pairs={{64,128},{128,64},{192,256},{256,192},{320,384},{384,320},{448,512... | collective-permute-start | bytes 1572872 | tf_op jit(solution)/shard_map/ppermute | solution.py:80
  44.1 13.5 %collective-permute-start.3 = (bf16[8,32,1024]{2,1,0:T(8,128)(2,1)S(1)}, bf16[8,32,1024]{2,1,0:T(8,128)(2,1)S(1)}, u32[]{:S(2)}, u32[]{:S(2)}) collective-permute-start(bf16[8,32,1024]{2,1,0:T(8,128)(2,1)S(1)} %get-tuple-element.92), channel_id=1, source_target_pairs={{0,64},{64,0},{128,192},{192,128},{256,320},{320,256},{384,448},{4... | collective-permute-start | bytes 1572872 | tf_op jit(solution)/shard_map/ppermute | solution.py:80
  49.8 7.7 %collective-permute-start.2 = (bf16[64,1664]{1,0:T(8,128)(2,1)S(1)}, bf16[64,1664]{1,0:T(8,128)(2,1)S(1)}, u32[]{:S(2)}, u32[]{:S(2)}) collective-permute-start(bf16[64,1664]{1,0:T(8,128)(2,1)S(1)} %pad_maximum_fusion.2), channel_id=1, source_target_pairs={{0,8},{8,0},{16,24},{24,16},{32,40},{40,32},{48,56},{56,48},{1,9},... | collective-permute-start | bytes 638984 | tf_op jit(solution)/shard_map/ppermute | solution.py:111
  58.0 11.9 %collective-permute-start.12 = (bf16[32,2048]{1,0:T(8,128)(2,1)S(1)}, bf16[32,2048]{1,0:T(8,128)(2,1)S(1)}, u32[]{:S(2)}, u32[]{:S(2)}) collective-permute-start(bf16[32,2048]{1,0:T(8,128)(2,1)S(1)} %pad_maximum_fusion.4), channel_id=1, source_target_pairs={{8,16},{16,8},{24,32},{32,24},{40,48},{48,40},{56,0},{0,56},{9,17}... | collective-permute-start | bytes 393224 | tf_op jit(solution)/shard_map/ppermute | solution.py:111
  63.4 12.2 %collective-permute-start.5 = (bf16[64,1664]{1,0:T(8,128)(2,1)S(1)}, bf16[64,1664]{1,0:T(8,128)(2,1)S(1)}, u32[]{:S(2)}, u32[]{:S(2)}) collective-permute-start(bf16[64,1664]{1,0:T(8,128)(2,1)S(1)} %pad_maximum_fusion.1), channel_id=1, source_target_pairs={{0,8},{8,0},{16,24},{24,16},{32,40},{40,32},{48,56},{56,48},{1,9},... | collective-permute-start | bytes 638984 | tf_op jit(solution)/shard_map/ppermute | solution.py:111
  65.3 10.3 %collective-permute-start.6 = (bf16[64,1664]{1,0:T(8,128)(2,1)S(1)}, bf16[64,1664]{1,0:T(8,128)(2,1)S(1)}, u32[]{:S(2)}, u32[]{:S(2)}) collective-permute-start(bf16[64,1664]{1,0:T(8,128)(2,1)S(1)} %add_convert_fusion.4), channel_id=1, source_target_pairs={{8,16},{16,8},{24,32},{32,24},{40,48},{48,40},{56,0},{0,56},{9,17}... | collective-permute-start | bytes 638984 | tf_op jit(solution)/shard_map/ppermute | solution.py:111
  70.0 10.4 %collective-permute-start.13 = (bf16[32,2048]{1,0:T(8,128)(2,1)S(1)}, bf16[32,2048]{1,0:T(8,128)(2,1)S(1)}, u32[]{:S(2)}, u32[]{:S(2)}) collective-permute-start(bf16[32,2048]{1,0:T(8,128)(2,1)S(1)} %fusion.58), channel_id=1, source_target_pairs={{0,8},{8,0},{16,24},{24,16},{32,40},{40,32},{48,56},{56,48},{1,9},... | collective-permute-start | bytes 393224 | tf_op jit(solution)/shard_map/ppermute | solution.py:111
  73.2 8.1 %collective-permute-start.14 = (bf16[32,2048]{1,0:T(8,128)(2,1)S(1)}, bf16[32,2048]{1,0:T(8,128)(2,1)S(1)}, u32[]{:S(2)}, u32[]{:S(2)}) collective-permute-start(bf16[32,2048]{1,0:T(8,128)(2,1)S(1)} %pad_maximum_fusion.5), channel_id=1, source_target_pairs={{8,16},{16,8},{24,32},{32,24},{40,48},{48,40},{56,0},{0,56},{9,17}... | collective-permute-start | bytes 393224 | tf_op jit(solution)/shard_map/ppermute | solution.py:111
  75.7 18.5 %collective-permute-start.8 = (bf16[64,1664]{1,0:T(8,128)(2,1)S(1)}, bf16[64,1664]{1,0:T(8,128)(2,1)S(1)}, u32[]{:S(2)}, u32[]{:S(2)}) collective-permute-start(bf16[64,1664]{1,0:T(8,128)(2,1)S(1)} %add_convert_fusion.2), channel_id=1, source_target_pairs={{8,16},{16,8},{24,32},{32,24},{40,48},{48,40},{56,0},{0,56},{9,17}... | collective-permute-start | bytes 638984 | tf_op jit(solution)/shard_map/ppermute | solution.py:111
  81.3 8.2 %collective-permute-start.15 = (bf16[32,2048]{1,0:T(8,128)(2,1)S(1)}, bf16[32,2048]{1,0:T(8,128)(2,1)S(1)}, u32[]{:S(2)}, u32[]{:S(2)}) collective-permute-start(bf16[32,2048]{1,0:T(8,128)(2,1)S(1)} %fusion.57), channel_id=1, source_target_pairs={{0,8},{8,0},{16,24},{24,16},{32,40},{40,32},{48,56},{56,48},{1,9},... | collective-permute-start | bytes 393224 | tf_op jit(solution)/shard_map/ppermute | solution.py:111
  83.3 8.1 %collective-permute-start.16 = (bf16[32,2048]{1,0:T(8,128)(2,1)S(1)}, bf16[32,2048]{1,0:T(8,128)(2,1)S(1)}, u32[]{:S(2)}, u32[]{:S(2)}) collective-permute-start(bf16[32,2048]{1,0:T(8,128)(2,1)S(1)} %fusion.59), channel_id=1, source_target_pairs={{8,16},{16,8},{24,32},{32,24},{40,48},{48,40},{56,0},{0,56},{9,17}... | collective-permute-start | bytes 393224 | tf_op jit(solution)/shard_map/ppermute | solution.py:111
  86.9 7.7 %collective-permute-start.7 = (bf16[64,1664]{1,0:T(8,128)(2,1)S(1)}, bf16[64,1664]{1,0:T(8,128)(2,1)S(1)}, u32[]{:S(2)}, u32[]{:S(2)}) collective-permute-start(bf16[64,1664]{1,0:T(8,128)(2,1)S(1)} %add_convert_fusion.3), channel_id=1, source_target_pairs={{0,8},{8,0},{16,24},{24,16},{32,40},{40,32},{48,56},{56,48},{1,9},... | collective-permute-start | bytes 638984 | tf_op jit(solution)/shard_map/ppermute | solution.py:111
  91.4 13.2 %collective-permute-start.17 = (bf16[32,2048]{1,0:T(8,128)(2,1)S(1)}, bf16[32,2048]{1,0:T(8,128)(2,1)S(1)}, u32[]{:S(2)}, u32[]{:S(2)}) collective-permute-start(bf16[32,2048]{1,0:T(8,128)(2,1)S(1)} %fusion.56), channel_id=1, source_target_pairs={{0,8},{8,0},{16,24},{24,16},{32,40},{40,32},{48,56},{56,48},{1,9},... | collective-permute-start | bytes 393224 | tf_op jit(solution)/shard_map/ppermute | solution.py:111
  94.7 14.5 %collective-permute-start.10 = (bf16[64,1664]{1,0:T(8,128)(2,1)S(1)}, bf16[64,1664]{1,0:T(8,128)(2,1)S(1)}, u32[]{:S(2)}, u32[]{:S(2)}) collective-permute-start(bf16[64,1664]{1,0:T(8,128)(2,1)S(1)} %add_convert_fusion), channel_id=1, source_target_pairs={{8,16},{16,8},{24,32},{32,24},{40,48},{48,40},{56,0},{0,56},{9,17}... | collective-permute-start | bytes 638984 | tf_op jit(solution)/shard_map/ppermute | solution.py:111
  98.5 10.6 %collective-permute-start.9 = (bf16[64,1664]{1,0:T(8,128)(2,1)S(1)}, bf16[64,1664]{1,0:T(8,128)(2,1)S(1)}, u32[]{:S(2)}, u32[]{:S(2)}) collective-permute-start(bf16[64,1664]{1,0:T(8,128)(2,1)S(1)} %add_convert_fusion.1), channel_id=1, source_target_pairs={{0,8},{8,0},{16,24},{24,16},{32,40},{40,32},{48,56},{56,48},{1,9},... | collective-permute-start | bytes 638984 | tf_op jit(solution)/shard_map/ppermute | solution.py:111
  101.1 8.1 %collective-permute-start.18 = (bf16[32,2048]{1,0:T(8,128)(2,1)S(1)}, bf16[32,2048]{1,0:T(8,128)(2,1)S(1)}, u32[]{:S(2)}, u32[]{:S(2)}) collective-permute-start(bf16[32,2048]{1,0:T(8,128)(2,1)S(1)} %fusion.60), channel_id=1, source_target_pairs={{8,16},{16,8},{24,32},{32,24},{40,48},{48,40},{56,0},{0,56},{9,17}... | collective-permute-start | bytes 393224 | tf_op jit(solution)/shard_map/ppermute | solution.py:111
  109.3 7.2 %collective-permute-start.11 = (bf16[32,1664]{1,0:T(8,128)(2,1)S(1)}, bf16[32,1664]{1,0:T(8,128)(2,1)S(1)}, u32[]{:S(2)}, u32[]{:S(2)}) collective-permute-start(bf16[32,1664]{1,0:T(8,128)(2,1)S(1)} %slice.25), channel_id=1, source_target_pairs={{0,64},{64,0},{1,65},{65,1},{2,66},{66,2},{3,67},{67,3},{4,68},{68... | collective-permute-start | bytes 319496 | tf_op jit(solution)/shard_map/ppermute | solution.py:126

commit v6 on v4

--- a/solution.py
+++ b/solution.py
@@ -21,10 +21,6 @@
         out_grad, one_hot, (((1,), (0,)), ((), ())), preferred_element_type=jnp.float32
     )
     return moved.astype(out_grad.dtype)
-
-
-def add(left, right):
-    return (left.astype(jnp.float32) + right.astype(jnp.float32)).astype(jnp.bfloat16)
 
 
 def on_device(activations, out_grad):
@@ -52,48 +48,45 @@
         preferred_element_type=jnp.float32,
     ).astype(jnp.bfloat16).reshape(outer, columns // outer, width)
     cut = -(-(width // LANES) // 2) * LANES
-    spans = ((0, cut), (cut, width - cut))
 
     pairings = (
-        [(s, s ^ 1) for s in range(outer)],
-        [((s + 1) % outer, ((s ^ 1) + 1) % outer) for s in range(outer)],
+        [s ^ 1 for s in range(outer)],
+        [(((s + outer - 1) ^ 1) + 1) % outer for s in range(outer)],
     )
-    way = 1 - 2 * lax.rem(me, 2)
+    swaps = [
+        [(2 * s + c, 2 * pairings[(c + k) % 2][s] + c) for s in range(outer) for c in (0, 1)]
+        for k in (0, 1)
+    ]
+    way = (1 - 2 * lax.rem(me, 2)) * (1 - 2 * core)
 
-    def own(piece, pairing, distance):
-        start, size = spans[piece]
-        owner = lax.rem(me + way * (distance if pairing == 0 else -distance) + outer, outer)
+    def own(swap, distance, low=0, high=width):
+        owner = lax.rem(me + way * (distance if swap == 0 else -distance) + outer, outer)
         block = lax.dynamic_slice(
-            chunks, (owner, 0, start), (1, chunks.shape[1], size), allow_negative_indices=False
+            chunks, (owner, 0, low), (1, chunks.shape[1], high - low), allow_negative_indices=False
         )
-        return block[0]
+        return block[0].astype(jnp.float32)
 
-    far = outer // 2
-    arrived = {}
-    for distance in range(far, 0, -1):
+    farthest = outer // 2
+    arrived, before = {}, None
+    for distance in range(farthest, 0, -1):
         leaving = {}
-        for piece in (0, 1):
-            for pairing in (0, 1):
-                if distance == far and piece != pairing:
-                    continue
-                block = own(piece, pairing, distance)
-                if (piece, 1 - pairing) in arrived:
-                    block = add(arrived[piece, 1 - pairing], block)
-                elif (piece, pairing) in arrived:
-                    block, arrived[piece, pairing] = lax.optimization_barrier(
-                        (block, arrived[piece, pairing])
-                    )
-                leaving[piece, pairing] = lax.ppermute(block, "y", pairings[pairing])
+        for swap in (0, 1) if (farthest - distance) % 2 == 0 else (1, 0):
+            if distance == farthest:
+                block = own(swap, distance, *((0, cut) if swap == 0 else (cut, width)))
+            else:
+                come, before = lax.optimization_barrier((arrived[1 - swap], before))
+                come = come.astype(jnp.float32)
+                if distance < farthest - 1:
+                    block = own(swap, distance) + come
+                else:
+                    left, right = own(swap, distance, 0, cut), own(swap, distance, cut, width)
+                    sides = (left + come, right) if swap == 1 else (left, right + come)
+                    block = jnp.concatenate(sides, axis=1)
+            before = block.astype(jnp.bfloat16)
+            leaving[swap] = lax.ppermute(before, ("y", "core"), swaps[swap])
         arrived = leaving
-    sums = [
-        (
-            own(piece, 0, 0).astype(jnp.float32)
-            + arrived[piece, 0].astype(jnp.float32)
-            + arrived[piece, 1].astype(jnp.float32)
-        ).astype(jnp.bfloat16)
-        for piece in (0, 1)
-    ]
-    first = jnp.concatenate(sums, axis=1).reshape(inner, columns // outer // inner, width)
+    total = own(0, 0) + arrived[0].astype(jnp.float32) + arrived[1].astype(jnp.float32)
+    first = total.astype(jnp.bfloat16).reshape(inner, columns // outer // inner, width)
     blocks = lax.all_to_all(first, "inner", split_axis=0, concat_axis=0, tiled=True)
     return jnp.sum(blocks, axis=0, dtype=jnp.float32)
 

time: 123 us -> 133 us (1.081)
  the two profiles are of different devices: /device:TPU:6 before, /device:TPU:2 now
where the time goes in v6:
time: 133 us; the launch traced here: 132 us
  blocking collectives  58.2 us (44%)
  waiting for transfers between devices  38.4 us (29%)
  starting transfers between devices  20.2 us (15%)
  matrix products  6.53 us (5%)
  other arithmetic  4.59 us (3%)
  local copies, waits for them, and re-layouts  4.13 us (3%)
    ppermute x8, waiting for transfers between devices, on_device(): leaving[swap] = lax.ppermute(before, ('y', 'core'), swaps[swap])  37.1 us
    all_to_all x1, blocking collectives, on_device(): lax.all_to_all(first, 'inner', split_axis=0, concat_axis=0, tiled=True)  34 us
    all_gather x1, blocking collectives, on_device(): grads = lax.all_gather(grads, 'x', axis=1, tiled=True)  24.2 us
    ppermute x8, starting transfers between devices, on_device(): leaving[swap] = lax.ppermute(before, ('y', 'core'), swaps[swap])  16.3 us
    dot_general x1, matrix products, on_device(): lax.dot_general(grads.reshape(tokens.shape[0], columns), tokens, (((0,),...  5.1 us
    unnamed x8, local copies, waits for them, and re-layouts  2.72 us
  transfers between devices with their start and end apart: 10, of which 5 were waited for; matrix products, arithmetic and copies ran while one was open for 3% of the time, Pallas kernels for 0%

profile of v6, /device:TPU:2, one launch (start us, length us, event | category | flops | bytes accessed | tf_op | source)
XLA Modules:
  0.0 132.4 jit_solution(15736233722909077661)
XLA Ops:
  0.0 0.0 copy-start
  0.0 0.9 copy-done
  0.9 0.0 copy-start.3
  0.9 1.4 %fusion.36 = bf16[1024,96]{0,1:T(8,128)(2,1)S(1)} fusion(bf16[96,1024]{1,0:T(8,128)(2,1)S(1)} %copy-done, s32[1024]{0:T(1024)S(1)} %get-tuple-element.30, s32[1024]{0:T(1024)S(1)} %get-tuple-element.31, s32[1024]{0:T(1024)S(1)} %get-tuple-element.29, s32[1024]{0:T(1024)S(1)} %get-tuple-element.32, pred[1024]{0:T(1024)(128)(4,1)S(1)} %get-tuple-element.27, ...), kind=kOutput, calls=%fused_computation.50 | convolution fusion | flops 250707968 | bytes 411648 | tf_op jit(solution)/shard_map/dot_general | solution.py:20
  2.4 1.9 %collective-permute-start = (bf16[96,512]{1,0:T(8,128)(2,1)S(1)}, bf16[96,512]{1,0:T(8,128)(2,1)S(1)}, u32[]{:S(2)}, u32[]{:S(2)}) collective-permute-start(bf16[96,512]{1,0:T(8,128)(2,1)S(1)} %get-tuple-element.26), channel_id=1, source_target_pairs={{0,4},{4,0},{1,5},{5,1},{2,6},{6,2},{3,7},{7,3},{8,12},{12,8},{9,1... | collective-permute-start | bytes 294920 | tf_op jit(solution)/shard_map/ppermute | solution.py:38
  4.3 1.3 collective-permute-done
  5.6 0.0 copy-done.3
  5.6 2.1 %collective-permute-start.1 = (bf16[384,3712]{1,0:T(8,128)(2,1)S(1)}, bf16[384,3712]{1,0:T(8,128)(2,1)}, u32[]{:S(2)}, u32[]{:S(2)}) collective-permute-start(bf16[384,3712]{1,0:T(8,128)(2,1)S(1)} %copy-done.3), channel_id=1, source_target_pairs={{0,4},{4,0},{1,5},{5,1},{2,6},{6,2},{3,7},{7,3},{8,12},{12,8},{9,1... | collective-permute-start | bytes 8552456 | tf_op jit(solution)/shard_map/ppermute | solution.py:40
  7.7 24.2 %all_gather.3 = bf16[2,384,512]{2,1,0:T(8,128)(2,1)S(1)} all-gather(bf16[2,96,512]{2,1,0:T(8,128)(2,1)S(1)} %pad_maximum_fusion.2), channel_id=1, replica_groups=mesh['inner'=16,'y'=8,'core'=2,'x'=4] {'x'}, dimensions={1}, use_global_device_ids=true | all-gather | bytes 983040 | tf_op jit(solution)/shard_map/all_gather | solution.py:42
  31.9 0.0 collective-permute-done.1
  31.9 5.1 %convolution_convert_fusion = bf16[512,3712]{1,0:T(8,128)(2,1)S(1)} fusion(bf16[768,512]{1,0:T(8,128)(2,1)S(1)} %bitcast.49, bf16[384,3712]{1,0:T(8,128)(2,1)} %collective-permute-done.1, bf16[384,3712]{1,0:T(8,128)(2,1)S(1)} %copy-done.3), kind=kOutput, calls=%fused_computation.13 | convolution fusion | flops 2932539392 | bytes 10289152 | tf_op jit(solution)/shard_map/dot_general | solution.py:44
  37.0 0.0 copy-start.1
  37.0 1.8 %copy-done.1 = bf16[512,3712]{1,0:T(8,128)(2,1)} copy-done((bf16[512,3712]{1,0:T(8,128)(2,1)}, bf16[512,3712]{1,0:T(8,128)(2,1)S(1)}, u32[]{:S(2)}) %copy-start.1) | copy-done | bytes 3801112
  38.9 1.9 %collective-permute-start.3 = (bf16[64,1920]{1,0:T(8,128)(2,1)S(1)}, bf16[64,1920]{1,0:T(8,128)(2,1)S(1)}, u32[]{:S(2)}, u32[]{:S(2)}) collective-permute-start(bf16[64,1920]{1,0:T(8,128)(2,1)S(1)} %get-tuple-element.22), channel_id=1, source_target_pairs={{0,8},{4,60},{8,0},{12,20},{16,24},{20,12},{24,16},{28,36},{32,40}... | collective-permute-start | bytes 737288 | tf_op jit(solution)/shard_map/ppermute | solution.py:86
  40.8 0.0 copy-start.2
  40.8 1.2 dynamic-slice_bitcast_fusion.3
  42.1 2.1 %collective-permute-start.2 = (bf16[64,1792]{1,0:T(8,128)(2,1)S(1)}, bf16[64,1792]{1,0:T(8,128)(2,1)S(1)}, u32[]{:S(2)}, u32[]{:S(2)}) collective-permute-start(bf16[64,1792]{1,0:T(8,128)(2,1)S(1)} %get-tuple-element.23), channel_id=1, source_target_pairs={{0,56},{4,12},{8,16},{12,4},{16,8},{20,28},{24,32},{28,20},{32,24}... | collective-permute-start | bytes 688136 | tf_op jit(solution)/shard_map/ppermute | solution.py:86
  44.1 4.2 %collective-permute-done.3 = bf16[64,1920]{1,0:T(8,128)(2,1)S(1)} collective-permute-done((bf16[64,1920]{1,0:T(8,128)(2,1)S(1)}, bf16[64,1920]{1,0:T(8,128)(2,1)S(1)}, u32[]{:S(2)}, u32[]{:S(2)}) %collective-permute-start.3) | collective-permute-done | bytes 245792 | tf_op jit(solution)/shard_map/ppermute | solution.py:86
  48.4 1.0 fusion.45
  49.4 1.9 %collective-permute-start.5 = (bf16[64,3712]{1,0:T(8,128)(2,1)S(1)}, bf16[64,3712]{1,0:T(8,128)(2,1)S(1)}, u32[]{:S(2)}, u32[]{:S(2)}) collective-permute-start(bf16[64,3712]{1,0:T(8,128)(2,1)S(1)} %pad_maximum_fusion), channel_id=1, source_target_pairs={{0,56},{4,12},{8,16},{12,4},{16,8},{20,28},{24,32},{28,20},{32,24}... | collective-permute-start | bytes 1425416 | tf_op jit(solution)/shard_map/ppermute | solution.py:86
  51.3 0.0 collective-permute-done.2
  51.3 1.0 fusion.46
  52.4 2.7 %collective-permute-start.4 = (bf16[64,3712]{1,0:T(8,128)(2,1)S(1)}, bf16[64,3712]{1,0:T(8,128)(2,1)S(1)}, u32[]{:S(2)}, u32[]{:S(2)}) collective-permute-start(bf16[64,3712]{1,0:T(8,128)(2,1)S(1)} %pad_maximum_fusion.1), channel_id=1, source_target_pairs={{0,8},{4,60},{8,0},{12,20},{16,24},{20,12},{24,16},{28,36},{32,40}... | collective-permute-start | bytes 1425416 | tf_op jit(solution)/shard_map/ppermute | solution.py:86
  55.1 11.0 %collective-permute-done.5 = bf16[64,3712]{1,0:T(8,128)(2,1)S(1)} collective-permute-done((bf16[64,3712]{1,0:T(8,128)(2,1)S(1)}, bf16[64,3712]{1,0:T(8,128)(2,1)S(1)}, u32[]{:S(2)}, u32[]{:S(2)}) %collective-permute-start.5) | collective-permute-done | bytes 475168 | tf_op jit(solution)/shard_map/ppermute | solution.py:86
  66.1 0.0 copy-done.2
  66.1 0.1 fusion.40
  66.2 1.9 %collective-permute-start.7 = (bf16[64,3712]{1,0:T(8,128)(2,1)S(1)}, bf16[64,3712]{1,0:T(8,128)(2,1)S(1)}, u32[]{:S(2)}, u32[]{:S(2)}) collective-permute-start(bf16[64,3712]{1,0:T(8,128)(2,1)S(1)} %fusion.40), channel_id=1, source_target_pairs={{0,8},{4,60},{8,0},{12,20},{16,24},{20,12},{24,16},{28,36},{32,40}... | collective-permute-start | bytes 1425416 | tf_op jit(solution)/shard_map/ppermute | solution.py:86
  68.1 0.0 collective-permute-done.4
  68.1 0.1 fusion.41
  68.2 1.9 %collective-permute-start.6 = (bf16[64,3712]{1,0:T(8,128)(2,1)S(1)}, bf16[64,3712]{1,0:T(8,128)(2,1)S(1)}, u32[]{:S(2)}, u32[]{:S(2)}) collective-permute-start(bf16[64,3712]{1,0:T(8,128)(2,1)S(1)} %fusion.41), channel_id=1, source_target_pairs={{0,56},{4,12},{8,16},{12,4},{16,8},{20,28},{24,32},{28,20},{32,24}... | collective-permute-start | bytes 1425416 | tf_op jit(solution)/shard_map/ppermute | solution.py:86
  70.2 11.6 %collective-permute-done.7 = bf16[64,3712]{1,0:T(8,128)(2,1)S(1)} collective-permute-done((bf16[64,3712]{1,0:T(8,128)(2,1)S(1)}, bf16[64,3712]{1,0:T(8,128)(2,1)S(1)}, u32[]{:S(2)}, u32[]{:S(2)}) %collective-permute-start.7) | collective-permute-done | bytes 475168 | tf_op jit(solution)/shard_map/ppermute | solution.py:86
  81.8 0.1 fusion.39
  81.9 1.9 %collective-permute-start.9 = (bf16[64,3712]{1,0:T(8,128)(2,1)S(1)}, bf16[64,3712]{1,0:T(8,128)(2,1)S(1)}, u32[]{:S(2)}, u32[]{:S(2)}) collective-permute-start(bf16[64,3712]{1,0:T(8,128)(2,1)S(1)} %fusion.39), channel_id=1, source_target_pairs={{0,56},{4,12},{8,16},{12,4},{16,8},{20,28},{24,32},{28,20},{32,24}... | collective-permute-start | bytes 1425416 | tf_op jit(solution)/shard_map/ppermute | solution.py:86
  83.8 0.0 collective-permute-done.6
  83.8 0.1 fusion.42
  84.0 1.9 %collective-permute-start.8 = (bf16[64,3712]{1,0:T(8,128)(2,1)S(1)}, bf16[64,3712]{1,0:T(8,128)(2,1)S(1)}, u32[]{:S(2)}, u32[]{:S(2)}) collective-permute-start(bf16[64,3712]{1,0:T(8,128)(2,1)S(1)} %fusion.42), channel_id=1, source_target_pairs={{0,8},{4,60},{8,0},{12,20},{16,24},{20,12},{24,16},{28,36},{32,40}... | collective-permute-start | bytes 1425416 | tf_op jit(solution)/shard_map/ppermute | solution.py:86
  85.9 10.3 %collective-permute-done.9 = bf16[64,3712]{1,0:T(8,128)(2,1)S(1)} collective-permute-done((bf16[64,3712]{1,0:T(8,128)(2,1)S(1)}, bf16[64,3712]{1,0:T(8,128)(2,1)S(1)}, u32[]{:S(2)}, u32[]{:S(2)}) %collective-permute-start.9) | collective-permute-done | bytes 475168 | tf_op jit(solution)/shard_map/ppermute | solution.py:86
  96.2 0.0 collective-permute-done.8
  96.2 1.2 fusion.44
  97.4 0.1 reshape.29
  97.5 34.0 %all_to_all.5 = bf16[16,4,3712]{2,1,0:T(4,128)(2,1)S(1)} all-to-all(bf16[16,4,3712]{2,1,0:T(4,128)(2,1)S(1)} %reshape.29), channel_id=1, replica_groups=mesh['inner'=16,'y'=8,'core'=2,'x'=4] {'inner'}, dimensions={0} | all-to-all | bytes 950272 | tf_op jit(solution)/shard_map/all_to_all | solution.py:90
  131.6 0.8 convert_reduce_fusion
  (8 shorter events, 0.2 us)
Async XLA Ops:
  0.0 0.9 copy-start
  0.9 4.7 %copy-start.3 = (bf16[384,3712]{1,0:T(8,128)(2,1)S(1)}, bf16[384,3712]{1,0:T(8,128)(2,1)}, u32[]{:S(2)}) copy-start(bf16[384,3712]{1,0:T(8,128)(2,1)} %param.2) | copy-start | bytes 8552452
  2.4 3.2 %collective-permute-start = (bf16[96,512]{1,0:T(8,128)(2,1)S(1)}, bf16[96,512]{1,0:T(8,128)(2,1)S(1)}, u32[]{:S(2)}, u32[]{:S(2)}) collective-permute-start(bf16[96,512]{1,0:T(8,128)(2,1)S(1)} %get-tuple-element.26), channel_id=1, source_target_pairs={{0,4},{4,0},{1,5},{5,1},{2,6},{6,2},{3,7},{7,3},{8,12},{12,8},{9,1... | collective-permute-start | bytes 294920 | tf_op jit(solution)/shard_map/ppermute | solution.py:38
  5.6 26.3 %collective-permute-start.1 = (bf16[384,3712]{1,0:T(8,128)(2,1)S(1)}, bf16[384,3712]{1,0:T(8,128)(2,1)}, u32[]{:S(2)}, u32[]{:S(2)}) collective-permute-start(bf16[384,3712]{1,0:T(8,128)(2,1)S(1)} %copy-done.3), channel_id=1, source_target_pairs={{0,4},{4,0},{1,5},{5,1},{2,6},{6,2},{3,7},{7,3},{8,12},{12,8},{9,1... | collective-permute-start | bytes 8552456 | tf_op jit(solution)/shard_map/ppermute | solution.py:40
  37.0 1.8 %copy-start.1 = (bf16[512,3712]{1,0:T(8,128)(2,1)}, bf16[512,3712]{1,0:T(8,128)(2,1)S(1)}, u32[]{:S(2)}) copy-start(bf16[512,3712]{1,0:T(8,128)(2,1)S(1)} %convolution_convert_fusion) | copy-start | bytes 11403268
  38.9 9.5 %collective-permute-start.3 = (bf16[64,1920]{1,0:T(8,128)(2,1)S(1)}, bf16[64,1920]{1,0:T(8,128)(2,1)S(1)}, u32[]{:S(2)}, u32[]{:S(2)}) collective-permute-start(bf16[64,1920]{1,0:T(8,128)(2,1)S(1)} %get-tuple-element.22), channel_id=1, source_target_pairs={{0,8},{4,60},{8,0},{12,20},{16,24},{20,12},{24,16},{28,36},{32,40}... | collective-permute-start | bytes 737288 | tf_op jit(solution)/shard_map/ppermute | solution.py:86
  40.8 25.2 %copy-start.2 = (bf16[512,3712]{1,0:T(8,128)(2,1)S(1)}, bf16[512,3712]{1,0:T(8,128)(2,1)}, u32[]{:S(2)}) copy-start(bf16[512,3712]{1,0:T(8,128)(2,1)} %copy-done.1) | copy-start | bytes 11403268
  42.1 9.3 %collective-permute-start.2 = (bf16[64,1792]{1,0:T(8,128)(2,1)S(1)}, bf16[64,1792]{1,0:T(8,128)(2,1)S(1)}, u32[]{:S(2)}, u32[]{:S(2)}) collective-permute-start(bf16[64,1792]{1,0:T(8,128)(2,1)S(1)} %get-tuple-element.23), channel_id=1, source_target_pairs={{0,56},{4,12},{8,16},{12,4},{16,8},{20,28},{24,32},{28,20},{32,24}... | collective-permute-start | bytes 688136 | tf_op jit(solution)/shard_map/ppermute | solution.py:86
  49.4 16.6 %collective-permute-start.5 = (bf16[64,3712]{1,0:T(8,128)(2,1)S(1)}, bf16[64,3712]{1,0:T(8,128)(2,1)S(1)}, u32[]{:S(2)}, u32[]{:S(2)}) collective-permute-start(bf16[64,3712]{1,0:T(8,128)(2,1)S(1)} %pad_maximum_fusion), channel_id=1, source_target_pairs={{0,56},{4,12},{8,16},{12,4},{16,8},{20,28},{24,32},{28,20},{32,24}... | collective-permute-start | bytes 1425416 | tf_op jit(solution)/shard_map/ppermute | solution.py:86
  52.4 15.7 %collective-permute-start.4 = (bf16[64,3712]{1,0:T(8,128)(2,1)S(1)}, bf16[64,3712]{1,0:T(8,128)(2,1)S(1)}, u32[]{:S(2)}, u32[]{:S(2)}) collective-permute-start(bf16[64,3712]{1,0:T(8,128)(2,1)S(1)} %pad_maximum_fusion.1), channel_id=1, source_target_pairs={{0,8},{4,60},{8,0},{12,20},{16,24},{20,12},{24,16},{28,36},{32,40}... | collective-permute-start | bytes 1425416 | tf_op jit(solution)/shard_map/ppermute | solution.py:86
  66.2 15.6 %collective-permute-start.7 = (bf16[64,3712]{1,0:T(8,128)(2,1)S(1)}, bf16[64,3712]{1,0:T(8,128)(2,1)S(1)}, u32[]{:S(2)}, u32[]{:S(2)}) collective-permute-start(bf16[64,3712]{1,0:T(8,128)(2,1)S(1)} %fusion.40), channel_id=1, source_target_pairs={{0,8},{4,60},{8,0},{12,20},{16,24},{20,12},{24,16},{28,36},{32,40}... | collective-permute-start | bytes 1425416 | tf_op jit(solution)/shard_map/ppermute | solution.py:86
  68.2 15.6 %collective-permute-start.6 = (bf16[64,3712]{1,0:T(8,128)(2,1)S(1)}, bf16[64,3712]{1,0:T(8,128)(2,1)S(1)}, u32[]{:S(2)}, u32[]{:S(2)}) collective-permute-start(bf16[64,3712]{1,0:T(8,128)(2,1)S(1)} %fusion.41), channel_id=1, source_target_pairs={{0,56},{4,12},{8,16},{12,4},{16,8},{20,28},{24,32},{28,20},{32,24}... | collective-permute-start | bytes 1425416 | tf_op jit(solution)/shard_map/ppermute | solution.py:86
  81.9 14.3 %collective-permute-start.9 = (bf16[64,3712]{1,0:T(8,128)(2,1)S(1)}, bf16[64,3712]{1,0:T(8,128)(2,1)S(1)}, u32[]{:S(2)}, u32[]{:S(2)}) collective-permute-start(bf16[64,3712]{1,0:T(8,128)(2,1)S(1)} %fusion.39), channel_id=1, source_target_pairs={{0,56},{4,12},{8,16},{12,4},{16,8},{20,28},{24,32},{28,20},{32,24}... | collective-permute-start | bytes 1425416 | tf_op jit(solution)/shard_map/ppermute | solution.py:86
  84.0 12.3 %collective-permute-start.8 = (bf16[64,3712]{1,0:T(8,128)(2,1)S(1)}, bf16[64,3712]{1,0:T(8,128)(2,1)S(1)}, u32[]{:S(2)}, u32[]{:S(2)}) collective-permute-start(bf16[64,3712]{1,0:T(8,128)(2,1)S(1)} %fusion.42), channel_id=1, source_target_pairs={{0,8},{4,60},{8,0},{12,20},{16,24},{20,12},{24,16},{28,36},{32,40}... | collective-permute-start | bytes 1425416 | tf_op jit(solution)/shard_map/ppermute | solution.py:86

commit v7 on v6

--- a/solution.py
+++ b/solution.py
@@ -59,7 +59,10 @@
     ]
     way = (1 - 2 * lax.rem(me, 2)) * (1 - 2 * core)
 
-    def own(swap, distance, low=0, high=width):
+    spans = ((0, cut), (cut, width))
+
+    def own(piece, swap, distance):
+        low, high = spans[piece]
         owner = lax.rem(me + way * (distance if swap == 0 else -distance) + outer, outer)
         block = lax.dynamic_slice(
             chunks, (owner, 0, low), (1, chunks.shape[1], high - low), allow_negative_indices=False
@@ -67,26 +70,32 @@
         return block[0].astype(jnp.float32)
 
     farthest = outer // 2
+    order = [(farthest, 0, 0), (farthest, 1, 1)]
+    for distance in range(farthest - 1, 0, -1):
+        first_way = (farthest - 1 - distance) % 2
+        order += [(distance, p, p ^ first_way ^ late) for late in (0, 1) for p in (0, 1)]
     arrived, before = {}, None
-    for distance in range(farthest, 0, -1):
-        leaving = {}
-        for swap in (0, 1) if (farthest - distance) % 2 == 0 else (1, 0):
-            if distance == farthest:
-                block = own(swap, distance, *((0, cut) if swap == 0 else (cut, width)))
-            else:
-                come, before = lax.optimization_barrier((arrived[1 - swap], before))
-                come = come.astype(jnp.float32)
-                if distance < farthest - 1:
-                    block = own(swap, distance) + come
-                else:
-                    left, right = own(swap, distance, 0, cut), own(swap, distance, cut, width)
-                    sides = (left + come, right) if swap == 1 else (left, right + come)
-                    block = jnp.concatenate(sides, axis=1)
-            before = block.astype(jnp.bfloat16)
-            leaving[swap] = lax.ppermute(before, ("y", "core"), swaps[swap])
-        arrived = leaving
-    total = own(0, 0) + arrived[0].astype(jnp.float32) + arrived[1].astype(jnp.float32)
-    first = total.astype(jnp.bfloat16).reshape(inner, columns // outer // inner, width)
+    for distance, piece, swap in order:
+        block = own(piece, swap, distance)
+        source = (distance + 1, piece, 1 - swap)
+        if source in arrived:
+            come, before = lax.optimization_barrier((arrived[source], before))
+            block = (block + come.astype(jnp.float32)).astype(jnp.bfloat16)
+        else:
+            block = block.astype(jnp.bfloat16)
+            if before is not None:
+                block, before = lax.optimization_barrier((block, before))
+        before = block
+        arrived[distance, piece, swap] = lax.ppermute(block, ("y", "core"), swaps[swap])
+    sums = []
+    for piece in (0, 1):
+        come = (arrived[1, piece, 0], arrived[1, piece, 1])
+        come, before = lax.optimization_barrier((come, before))
+        total = own(piece, 0, 0) + come[0].astype(jnp.float32) + come[1].astype(jnp.float32)
+        before = total.astype(jnp.bfloat16)
+        sums.append(before)
+    first = jnp.concatenate(sums, axis=1)
+    first = first.reshape(inner, columns // outer // inner, width)
     blocks = lax.all_to_all(first, "inner", split_axis=0, concat_axis=0, tiled=True)
     return jnp.sum(blocks, axis=0, dtype=jnp.float32)
 

time: 133 us -> 134 us (level)
  the two profiles are of different devices: /device:TPU:2 before, /device:TPU:6 now
where the time goes in v7:
time: 134 us; the launch traced here: 132 us
  blocking collectives  57 us (43%)
  starting transfers between devices  45.3 us (34%)
  other arithmetic  13 us (10%)
  matrix products  6.53 us (5%)
  waiting for transfers between devices  6.23 us (5%)
  local copies, waits for them, and re-layouts  3.97 us (3%)
    ppermute x14, starting transfers between devices, on_device(): lax.ppermute(block, ('y', 'core'), swaps[swap])  41.3 us
    all_to_all x1, blocking collectives, on_device(): lax.all_to_all(first, 'inner', split_axis=0, concat_axis=0, tiled=True)  32.8 us
    all_gather x1, blocking collectives, on_device(): grads = lax.all_gather(grads, 'x', axis=1, tiled=True)  24.1 us
    convert_element_type x10, other arithmetic, on_device(): block = (block + come.astype(jnp.float32)).astype(jnp.bfloat16)  10.1 us
    dot_general x1, matrix products, on_device(): lax.dot_general(grads.reshape(tokens.shape[0], columns), tokens, (((0,),...  5.1 us
    ppermute x14, waiting for transfers between devices, on_device(): lax.ppermute(block, ('y', 'core'), swaps[swap])  4.96 us
    unnamed x6, local copies, waits for them, and re-layouts  2.71 us
  transfers between devices with their start and end apart: 16, of which 3 were waited for; matrix products, arithmetic and copies ran while one was open for 9% of the time, Pallas kernels for 0%

profile of v7, /device:TPU:6, one launch (start us, length us, event | category | flops | bytes accessed | tf_op | source)
XLA Modules:
  0.0 132.4 jit_solution(3363074583218248486)
XLA Ops:
  0.0 0.9 copy-done
  0.9 1.4 %fusion.36 = bf16[1024,96]{0,1:T(8,128)(2,1)S(1)} fusion(bf16[96,1024]{1,0:T(8,128)(2,1)S(1)} %copy-done, s32[1024]{0:T(1024)S(1)} %get-tuple-element.52, s32[1024]{0:T(1024)S(1)} %get-tuple-element.53, s32[1024]{0:T(1024)S(1)} %get-tuple-element.51, s32[1024]{0:T(1024)S(1)} %get-tuple-element.54, pred[1024]{0:T(1024)(128)(4,1)S(1)} %get-tuple-element.49, ...), kind=kOutput, calls=%fused_computation.50 | convolution fusion | flops 250707968 | bytes 411648 | tf_op jit(solution)/shard_map/dot_general | solution.py:20
  2.4 1.9 %collective-permute-start = (bf16[96,512]{1,0:T(8,128)(2,1)S(1)}, bf16[96,512]{1,0:T(8,128)(2,1)S(1)}, u32[]{:S(2)}, u32[]{:S(2)}) collective-permute-start(bf16[96,512]{1,0:T(8,128)(2,1)S(1)} %get-tuple-element.48), channel_id=1, source_target_pairs={{0,4},{4,0},{1,5},{5,1},{2,6},{6,2},{3,7},{7,3},{8,12},{12,8},{9,1... | collective-permute-start | bytes 294920 | tf_op jit(solution)/shard_map/ppermute | solution.py:38
  4.3 1.3 collective-permute-done
  5.6 2.1 %collective-permute-start.1 = (bf16[384,3712]{1,0:T(8,128)(2,1)S(1)}, bf16[384,3712]{1,0:T(8,128)(2,1)}, u32[]{:S(2)}, u32[]{:S(2)}) collective-permute-start(bf16[384,3712]{1,0:T(8,128)(2,1)S(1)} %copy-done.2), channel_id=1, source_target_pairs={{0,4},{4,0},{1,5},{5,1},{2,6},{6,2},{3,7},{7,3},{8,12},{12,8},{9,1... | collective-permute-start | bytes 8552456 | tf_op jit(solution)/shard_map/ppermute | solution.py:40
  7.7 24.1 %all_gather.3 = bf16[2,384,512]{2,1,0:T(8,128)(2,1)S(1)} all-gather(bf16[2,96,512]{2,1,0:T(8,128)(2,1)S(1)} %pad_maximum_fusion.1), channel_id=1, replica_groups=mesh['inner'=16,'y'=8,'core'=2,'x'=4] {'x'}, dimensions={1}, use_global_device_ids=true | all-gather | bytes 983040 | tf_op jit(solution)/shard_map/all_gather | solution.py:42
  31.8 0.0 collective-permute-done.1
  31.8 5.1 %convolution_convert_fusion = bf16[512,3712]{1,0:T(8,128)(2,1)S(1)} fusion(bf16[768,512]{1,0:T(8,128)(2,1)S(1)} %bitcast.69, bf16[384,3712]{1,0:T(8,128)(2,1)} %collective-permute-done.1, bf16[384,3712]{1,0:T(8,128)(2,1)S(1)} %copy-done.2), kind=kOutput, calls=%fused_computation.13 | convolution fusion | flops 2932539392 | bytes 10289152 | tf_op jit(solution)/shard_map/dot_general | solution.py:44
  37.0 1.8 %copy-done.1 = bf16[512,3712]{1,0:T(8,128)(2,1)} copy-done((bf16[512,3712]{1,0:T(8,128)(2,1)}, bf16[512,3712]{1,0:T(8,128)(2,1)S(1)}, u32[]{:S(2)}) %copy-start.1) | copy-done | bytes 3801112
  38.8 1.9 %collective-permute-start.4 = (bf16[64,1920]{1,0:T(8,128)(2,1)S(1)}, bf16[64,1920]{1,0:T(8,128)(2,1)S(1)}, u32[]{:S(2)}, u32[]{:S(2)}) collective-permute-start(bf16[64,1920]{1,0:T(8,128)(2,1)S(1)} %get-tuple-element.44), channel_id=1, source_target_pairs={{0,8},{4,60},{8,0},{12,20},{16,24},{20,12},{24,16},{28,36},{32,40}... | collective-permute-start | bytes 737288 | tf_op jit(solution)/shard_map/ppermute | solution.py:89
  40.8 1.1 dynamic-slice_bitcast_fusion.2
  41.9 1.9 %collective-permute-start.3 = (bf16[64,1792]{1,0:T(8,128)(2,1)S(1)}, bf16[64,1792]{1,0:T(8,128)(2,1)S(1)}, u32[]{:S(2)}, u32[]{:S(2)}) collective-permute-start(bf16[64,1792]{1,0:T(8,128)(2,1)S(1)} %get-tuple-element.26), channel_id=1, source_target_pairs={{0,56},{4,12},{8,16},{12,4},{16,8},{20,28},{24,32},{28,20},{32,24}... | collective-permute-start | bytes 688136 | tf_op jit(solution)/shard_map/ppermute | solution.py:89
  43.8 3.9 %collective-permute-start.2 = (bf16[64,1920]{1,0:T(8,128)(2,1)S(1)}, bf16[64,1920]{1,0:T(8,128)(2,1)S(1)}, u32[]{:S(2)}, u32[]{:S(2)}) collective-permute-start(bf16[64,1920]{1,0:T(8,128)(2,1)S(1)} %get-tuple-element.27), channel_id=1, source_target_pairs={{0,8},{4,60},{8,0},{12,20},{16,24},{20,12},{24,16},{28,36},{32,40}... | collective-permute-start | bytes 737288 | tf_op jit(solution)/shard_map/ppermute | solution.py:89
  47.7 3.1 %collective-permute-start.8 = (bf16[64,1792]{1,0:T(8,128)(2,1)S(1)}, bf16[64,1792]{1,0:T(8,128)(2,1)S(1)}, u32[]{:S(2)}, u32[]{:S(2)}) collective-permute-start(bf16[64,1792]{1,0:T(8,128)(2,1)S(1)} %get-tuple-element.28), channel_id=1, source_target_pairs={{0,56},{4,12},{8,16},{12,4},{16,8},{20,28},{24,32},{28,20},{32,24}... | collective-permute-start | bytes 688136 | tf_op jit(solution)/shard_map/ppermute | solution.py:89
  50.9 1.0 fusion.41
  51.9 3.9 %collective-permute-start.7 = (bf16[64,1920]{1,0:T(8,128)(2,1)S(1)}, bf16[64,1920]{1,0:T(8,128)(2,1)S(1)}, u32[]{:S(2)}, u32[]{:S(2)}) collective-permute-start(bf16[64,1920]{1,0:T(8,128)(2,1)S(1)} %fusion.41), channel_id=1, source_target_pairs={{0,56},{4,12},{8,16},{12,4},{16,8},{20,28},{24,32},{28,20},{32,24}... | collective-permute-start | bytes 737288 | tf_op jit(solution)/shard_map/ppermute | solution.py:89
  55.8 0.0 collective-permute-done.3
  55.8 1.0 fusion.52
  56.8 1.9 %collective-permute-start.6 = (bf16[64,1792]{1,0:T(8,128)(2,1)S(1)}, bf16[64,1792]{1,0:T(8,128)(2,1)S(1)}, u32[]{:S(2)}, u32[]{:S(2)}) collective-permute-start(bf16[64,1792]{1,0:T(8,128)(2,1)S(1)} %fusion.52), channel_id=1, source_target_pairs={{0,8},{4,60},{8,0},{12,20},{16,24},{20,12},{24,16},{28,36},{32,40}... | collective-permute-start | bytes 688136 | tf_op jit(solution)/shard_map/ppermute | solution.py:89
  58.8 0.0 collective-permute-done.2
  58.8 1.0 fusion.42
  59.8 3.9 %collective-permute-start.5 = (bf16[64,1920]{1,0:T(8,128)(2,1)S(1)}, bf16[64,1920]{1,0:T(8,128)(2,1)S(1)}, u32[]{:S(2)}, u32[]{:S(2)}) collective-permute-start(bf16[64,1920]{1,0:T(8,128)(2,1)S(1)} %fusion.42), channel_id=1, source_target_pairs={{0,56},{4,12},{8,16},{12,4},{16,8},{20,28},{24,32},{28,20},{32,24}... | collective-permute-start | bytes 737288 | tf_op jit(solution)/shard_map/ppermute | solution.py:89
  63.7 1.0 fusion.50
  64.7 4.0 %collective-permute-start.11 = (bf16[64,1792]{1,0:T(8,128)(2,1)S(1)}, bf16[64,1792]{1,0:T(8,128)(2,1)S(1)}, u32[]{:S(2)}, u32[]{:S(2)}) collective-permute-start(bf16[64,1792]{1,0:T(8,128)(2,1)S(1)} %fusion.50), channel_id=1, source_target_pairs={{0,8},{4,60},{8,0},{12,20},{16,24},{20,12},{24,16},{28,36},{32,40}... | collective-permute-start | bytes 688136 | tf_op jit(solution)/shard_map/ppermute | solution.py:89
  68.7 1.0 fusion.40
  69.7 1.9 %collective-permute-start.10 = (bf16[64,1920]{1,0:T(8,128)(2,1)S(1)}, bf16[64,1920]{1,0:T(8,128)(2,1)S(1)}, u32[]{:S(2)}, u32[]{:S(2)}) collective-permute-start(bf16[64,1920]{1,0:T(8,128)(2,1)S(1)} %fusion.40), channel_id=1, source_target_pairs={{0,8},{4,60},{8,0},{12,20},{16,24},{20,12},{24,16},{28,36},{32,40}... | collective-permute-start | bytes 737288 | tf_op jit(solution)/shard_map/ppermute | solution.py:89
  71.6 0.0 collective-permute-done.6
  71.6 1.0 fusion.51
  72.7 3.1 %collective-permute-start.13 = (bf16[64,1792]{1,0:T(8,128)(2,1)S(1)}, bf16[64,1792]{1,0:T(8,128)(2,1)S(1)}, u32[]{:S(2)}, u32[]{:S(2)}) collective-permute-start(bf16[64,1792]{1,0:T(8,128)(2,1)S(1)} %fusion.51), channel_id=1, source_target_pairs={{0,56},{4,12},{8,16},{12,4},{16,8},{20,28},{24,32},{28,20},{32,24}... | collective-permute-start | bytes 688136 | tf_op jit(solution)/shard_map/ppermute | solution.py:89
  75.8 0.0 collective-permute-done.5
  75.8 1.0 fusion.43
  76.8 2.7 %collective-permute-start.9 = (bf16[64,1920]{1,0:T(8,128)(2,1)S(1)}, bf16[64,1920]{1,0:T(8,128)(2,1)S(1)}, u32[]{:S(2)}, u32[]{:S(2)}) collective-permute-start(bf16[64,1920]{1,0:T(8,128)(2,1)S(1)} %fusion.43), channel_id=1, source_target_pairs={{0,8},{4,60},{8,0},{12,20},{16,24},{20,12},{24,16},{28,36},{32,40}... | collective-permute-start | bytes 737288 | tf_op jit(solution)/shard_map/ppermute | solution.py:89
  79.5 0.0 collective-permute-done.11
  79.5 1.0 fusion.49
  80.6 3.1 %collective-permute-start.15 = (bf16[64,1792]{1,0:T(8,128)(2,1)S(1)}, bf16[64,1792]{1,0:T(8,128)(2,1)S(1)}, u32[]{:S(2)}, u32[]{:S(2)}) collective-permute-start(bf16[64,1792]{1,0:T(8,128)(2,1)S(1)} %fusion.49), channel_id=1, source_target_pairs={{0,56},{4,12},{8,16},{12,4},{16,8},{20,28},{24,32},{28,20},{32,24}... | collective-permute-start | bytes 688136 | tf_op jit(solution)/shard_map/ppermute | solution.py:89
  83.7 1.0 fusion.39
  84.7 3.9 %collective-permute-start.12 = (bf16[64,1920]{1,0:T(8,128)(2,1)S(1)}, bf16[64,1920]{1,0:T(8,128)(2,1)S(1)}, u32[]{:S(2)}, u32[]{:S(2)}) collective-permute-start(bf16[64,1920]{1,0:T(8,128)(2,1)S(1)} %fusion.39), channel_id=1, source_target_pairs={{0,56},{4,12},{8,16},{12,4},{16,8},{20,28},{24,32},{28,20},{32,24}... | collective-permute-start | bytes 737288 | tf_op jit(solution)/shard_map/ppermute | solution.py:89
  88.6 0.0 collective-permute-done.13
  88.7 1.0 fusion.48
  89.7 1.9 %collective-permute-start.14 = (bf16[64,1792]{1,0:T(8,128)(2,1)S(1)}, bf16[64,1792]{1,0:T(8,128)(2,1)S(1)}, u32[]{:S(2)}, u32[]{:S(2)}) collective-permute-start(bf16[64,1792]{1,0:T(8,128)(2,1)S(1)} %fusion.48), channel_id=1, source_target_pairs={{0,8},{4,60},{8,0},{12,20},{16,24},{20,12},{24,16},{28,36},{32,40}... | collective-permute-start | bytes 688136 | tf_op jit(solution)/shard_map/ppermute | solution.py:89
  91.6 0.0 collective-permute-done.9
  91.6 4.3 %collective-permute-done.12 = bf16[64,1920]{1,0:T(8,128)(2,1)S(1)} collective-permute-done((bf16[64,1920]{1,0:T(8,128)(2,1)S(1)}, bf16[64,1920]{1,0:T(8,128)(2,1)S(1)}, u32[]{:S(2)}, u32[]{:S(2)}) %collective-permute-start.12) | collective-permute-done | bytes 245792 | tf_op jit(solution)/shard_map/ppermute | solution.py:89
  95.9 1.0 fusion.45
  96.9 0.6 collective-permute-done.14
  97.6 1.0 fusion.47
  98.6 0.1 reshape.35
  98.8 32.8 %all_to_all.5 = bf16[16,4,3712]{2,1,0:T(4,128)(2,1)S(1)} all-to-all(bf16[16,4,3712]{2,1,0:T(4,128)(2,1)S(1)} %reshape.35), channel_id=1, replica_groups=mesh['inner'=16,'y'=8,'core'=2,'x'=4] {'inner'}, dimensions={0} | all-to-all | bytes 950272 | tf_op jit(solution)/shard_map/all_to_all | solution.py:99
  131.6 0.8 convert_reduce_fusion
  (16 shorter events, 0.2 us)
Async XLA Ops:
  0.0 0.9 copy-start
  0.9 4.7 %copy-start.2 = (bf16[384,3712]{1,0:T(8,128)(2,1)S(1)}, bf16[384,3712]{1,0:T(8,128)(2,1)}, u32[]{:S(2)}) copy-start(bf16[384,3712]{1,0:T(8,128)(2,1)} %param.2) | copy-start | bytes 8552452
  2.4 3.2 %collective-permute-start = (bf16[96,512]{1,0:T(8,128)(2,1)S(1)}, bf16[96,512]{1,0:T(8,128)(2,1)S(1)}, u32[]{:S(2)}, u32[]{:S(2)}) collective-permute-start(bf16[96,512]{1,0:T(8,128)(2,1)S(1)} %get-tuple-element.48), channel_id=1, source_target_pairs={{0,4},{4,0},{1,5},{5,1},{2,6},{6,2},{3,7},{7,3},{8,12},{12,8},{9,1... | collective-permute-start | bytes 294920 | tf_op jit(solution)/shard_map/ppermute | solution.py:38
  5.6 26.3 %collective-permute-start.1 = (bf16[384,3712]{1,0:T(8,128)(2,1)S(1)}, bf16[384,3712]{1,0:T(8,128)(2,1)}, u32[]{:S(2)}, u32[]{:S(2)}) collective-permute-start(bf16[384,3712]{1,0:T(8,128)(2,1)S(1)} %copy-done.2), channel_id=1, source_target_pairs={{0,4},{4,0},{1,5},{5,1},{2,6},{6,2},{3,7},{7,3},{8,12},{12,8},{9,1... | collective-permute-start | bytes 8552456 | tf_op jit(solution)/shard_map/ppermute | solution.py:40
  37.0 1.8 %copy-start.1 = (bf16[512,3712]{1,0:T(8,128)(2,1)}, bf16[512,3712]{1,0:T(8,128)(2,1)S(1)}, u32[]{:S(2)}) copy-start(bf16[512,3712]{1,0:T(8,128)(2,1)S(1)} %convolution_convert_fusion) | copy-start | bytes 11403268
  38.8 12.1 %collective-permute-start.4 = (bf16[64,1920]{1,0:T(8,128)(2,1)S(1)}, bf16[64,1920]{1,0:T(8,128)(2,1)S(1)}, u32[]{:S(2)}, u32[]{:S(2)}) collective-permute-start(bf16[64,1920]{1,0:T(8,128)(2,1)S(1)} %get-tuple-element.44), channel_id=1, source_target_pairs={{0,8},{4,60},{8,0},{12,20},{16,24},{20,12},{24,16},{28,36},{32,40}... | collective-permute-start | bytes 737288 | tf_op jit(solution)/shard_map/ppermute | solution.py:89
  41.9 14.0 %collective-permute-start.3 = (bf16[64,1792]{1,0:T(8,128)(2,1)S(1)}, bf16[64,1792]{1,0:T(8,128)(2,1)S(1)}, u32[]{:S(2)}, u32[]{:S(2)}) collective-permute-start(bf16[64,1792]{1,0:T(8,128)(2,1)S(1)} %get-tuple-element.26), channel_id=1, source_target_pairs={{0,56},{4,12},{8,16},{12,4},{16,8},{20,28},{24,32},{28,20},{32,24}... | collective-permute-start | bytes 688136 | tf_op jit(solution)/shard_map/ppermute | solution.py:89
  43.8 15.0 %collective-permute-start.2 = (bf16[64,1920]{1,0:T(8,128)(2,1)S(1)}, bf16[64,1920]{1,0:T(8,128)(2,1)S(1)}, u32[]{:S(2)}, u32[]{:S(2)}) collective-permute-start(bf16[64,1920]{1,0:T(8,128)(2,1)S(1)} %get-tuple-element.27), channel_id=1, source_target_pairs={{0,8},{4,60},{8,0},{12,20},{16,24},{20,12},{24,16},{28,36},{32,40}... | collective-permute-start | bytes 737288 | tf_op jit(solution)/shard_map/ppermute | solution.py:89
  47.7 16.0 %collective-permute-start.8 = (bf16[64,1792]{1,0:T(8,128)(2,1)S(1)}, bf16[64,1792]{1,0:T(8,128)(2,1)S(1)}, u32[]{:S(2)}, u32[]{:S(2)}) collective-permute-start(bf16[64,1792]{1,0:T(8,128)(2,1)S(1)} %get-tuple-element.28), channel_id=1, source_target_pairs={{0,56},{4,12},{8,16},{12,4},{16,8},{20,28},{24,32},{28,20},{32,24}... | collective-permute-start | bytes 688136 | tf_op jit(solution)/shard_map/ppermute | solution.py:89
  51.9 16.8 %collective-permute-start.7 = (bf16[64,1920]{1,0:T(8,128)(2,1)S(1)}, bf16[64,1920]{1,0:T(8,128)(2,1)S(1)}, u32[]{:S(2)}, u32[]{:S(2)}) collective-permute-start(bf16[64,1920]{1,0:T(8,128)(2,1)S(1)} %fusion.41), channel_id=1, source_target_pairs={{0,56},{4,12},{8,16},{12,4},{16,8},{20,28},{24,32},{28,20},{32,24}... | collective-permute-start | bytes 737288 | tf_op jit(solution)/shard_map/ppermute | solution.py:89
  56.8 14.8 %collective-permute-start.6 = (bf16[64,1792]{1,0:T(8,128)(2,1)S(1)}, bf16[64,1792]{1,0:T(8,128)(2,1)S(1)}, u32[]{:S(2)}, u32[]{:S(2)}) collective-permute-start(bf16[64,1792]{1,0:T(8,128)(2,1)S(1)} %fusion.52), channel_id=1, source_target_pairs={{0,8},{4,60},{8,0},{12,20},{16,24},{20,12},{24,16},{28,36},{32,40}... | collective-permute-start | bytes 688136 | tf_op jit(solution)/shard_map/ppermute | solution.py:89
  59.8 16.0 %collective-permute-start.5 = (bf16[64,1920]{1,0:T(8,128)(2,1)S(1)}, bf16[64,1920]{1,0:T(8,128)(2,1)S(1)}, u32[]{:S(2)}, u32[]{:S(2)}) collective-permute-start(bf16[64,1920]{1,0:T(8,128)(2,1)S(1)} %fusion.42), channel_id=1, source_target_pairs={{0,56},{4,12},{8,16},{12,4},{16,8},{20,28},{24,32},{28,20},{32,24}... | collective-permute-start | bytes 737288 | tf_op jit(solution)/shard_map/ppermute | solution.py:89
  64.7 14.8 %collective-permute-start.11 = (bf16[64,1792]{1,0:T(8,128)(2,1)S(1)}, bf16[64,1792]{1,0:T(8,128)(2,1)S(1)}, u32[]{:S(2)}, u32[]{:S(2)}) collective-permute-start(bf16[64,1792]{1,0:T(8,128)(2,1)S(1)} %fusion.50), channel_id=1, source_target_pairs={{0,8},{4,60},{8,0},{12,20},{16,24},{20,12},{24,16},{28,36},{32,40}... | collective-permute-start | bytes 688136 | tf_op jit(solution)/shard_map/ppermute | solution.py:89
  69.7 14.0 %collective-permute-start.10 = (bf16[64,1920]{1,0:T(8,128)(2,1)S(1)}, bf16[64,1920]{1,0:T(8,128)(2,1)S(1)}, u32[]{:S(2)}, u32[]{:S(2)}) collective-permute-start(bf16[64,1920]{1,0:T(8,128)(2,1)S(1)} %fusion.40), channel_id=1, source_target_pairs={{0,8},{4,60},{8,0},{12,20},{16,24},{20,12},{24,16},{28,36},{32,40}... | collective-permute-start | bytes 737288 | tf_op jit(solution)/shard_map/ppermute | solution.py:89
  72.7 16.0 %collective-permute-start.13 = (bf16[64,1792]{1,0:T(8,128)(2,1)S(1)}, bf16[64,1792]{1,0:T(8,128)(2,1)S(1)}, u32[]{:S(2)}, u32[]{:S(2)}) collective-permute-start(bf16[64,1792]{1,0:T(8,128)(2,1)S(1)} %fusion.51), channel_id=1, source_target_pairs={{0,56},{4,12},{8,16},{12,4},{16,8},{20,28},{24,32},{28,20},{32,24}... | collective-permute-start | bytes 688136 | tf_op jit(solution)/shard_map/ppermute | solution.py:89
  76.8 14.8 %collective-permute-start.9 = (bf16[64,1920]{1,0:T(8,128)(2,1)S(1)}, bf16[64,1920]{1,0:T(8,128)(2,1)S(1)}, u32[]{:S(2)}, u32[]{:S(2)}) collective-permute-start(bf16[64,1920]{1,0:T(8,128)(2,1)S(1)} %fusion.43), channel_id=1, source_target_pairs={{0,8},{4,60},{8,0},{12,20},{16,24},{20,12},{24,16},{28,36},{32,40}... | collective-permute-start | bytes 737288 | tf_op jit(solution)/shard_map/ppermute | solution.py:89
  80.6 16.4 %collective-permute-start.15 = (bf16[64,1792]{1,0:T(8,128)(2,1)S(1)}, bf16[64,1792]{1,0:T(8,128)(2,1)S(1)}, u32[]{:S(2)}, u32[]{:S(2)}) collective-permute-start(bf16[64,1792]{1,0:T(8,128)(2,1)S(1)} %fusion.49), channel_id=1, source_target_pairs={{0,56},{4,12},{8,16},{12,4},{16,8},{20,28},{24,32},{28,20},{32,24}... | collective-permute-start | bytes 688136 | tf_op jit(solution)/shard_map/ppermute | solution.py:89
  84.7 11.2 %collective-permute-start.12 = (bf16[64,1920]{1,0:T(8,128)(2,1)S(1)}, bf16[64,1920]{1,0:T(8,128)(2,1)S(1)}, u32[]{:S(2)}, u32[]{:S(2)}) collective-permute-start(bf16[64,1920]{1,0:T(8,128)(2,1)S(1)} %fusion.39), channel_id=1, source_target_pairs={{0,56},{4,12},{8,16},{12,4},{16,8},{20,28},{24,32},{28,20},{32,24}... | collective-permute-start | bytes 737288 | tf_op jit(solution)/shard_map/ppermute | solution.py:89
  89.7 7.9 %collective-permute-start.14 = (bf16[64,1792]{1,0:T(8,128)(2,1)S(1)}, bf16[64,1792]{1,0:T(8,128)(2,1)S(1)}, u32[]{:S(2)}, u32[]{:S(2)}) collective-permute-start(bf16[64,1792]{1,0:T(8,128)(2,1)S(1)} %fusion.48), channel_id=1, source_target_pairs={{0,8},{4,60},{8,0},{12,20},{16,24},{20,12},{24,16},{28,36},{32,40}... | collective-permute-start | bytes 688136 | tf_op jit(solution)/shard_map/ppermute | solution.py:89

commit v8 on v7

--- a/solution.py
+++ b/solution.py
@@ -74,26 +74,22 @@
     for distance in range(farthest - 1, 0, -1):
         first_way = (farthest - 1 - distance) % 2
         order += [(distance, p, p ^ first_way ^ late) for late in (0, 1) for p in (0, 1)]
-    arrived, before = {}, None
+    arrived, before = {}, {}
     for distance, piece, swap in order:
         block = own(piece, swap, distance)
         source = (distance + 1, piece, 1 - swap)
         if source in arrived:
-            come, before = lax.optimization_barrier((arrived[source], before))
+            come, before[piece] = lax.optimization_barrier((arrived[source], before[piece]))
             block = (block + come.astype(jnp.float32)).astype(jnp.bfloat16)
         else:
             block = block.astype(jnp.bfloat16)
-            if before is not None:
-                block, before = lax.optimization_barrier((block, before))
-        before = block
+        before[piece] = block
         arrived[distance, piece, swap] = lax.ppermute(block, ("y", "core"), swaps[swap])
     sums = []
     for piece in (0, 1):
         come = (arrived[1, piece, 0], arrived[1, piece, 1])
-        come, before = lax.optimization_barrier((come, before))
         total = own(piece, 0, 0) + come[0].astype(jnp.float32) + come[1].astype(jnp.float32)
-        before = total.astype(jnp.bfloat16)
-        sums.append(before)
+        sums.append(total.astype(jnp.bfloat16))
     first = jnp.concatenate(sums, axis=1)
     first = first.reshape(inner, columns // outer // inner, width)
     blocks = lax.all_to_all(first, "inner", split_axis=0, concat_axis=0, tiled=True)

time: 134 us -> 124 us (0.925)
  other arithmetic: 13 us -> 1.7 us
  starting transfers between devices: 45.3 us -> 49 us
  local copies, waits for them, and re-layouts: 3.97 us -> 1.12 us
    convert_element_type x10, other arithmetic: 10.1 us -> 0.63 us  [on_device(): block = (block + come.astype(jnp.float32)).astype(jnp.bfloat16)]
    ppermute x14, starting transfers between devices: 41.3 us -> 45 us  [on_device(): lax.ppermute(block, ('y', 'core'), swaps[swap])]
    convert_element_type x2, other arithmetic: 2.06 us -> 0.18 us  [on_device(): sums.append(total.astype(jnp.bfloat16))]
    unnamed x6 -> x4, local copies, waits for them, and re-layouts: 2.71 us -> 0.9 us
  transfers between devices with their start and end apart: 16 -> 16, of which waited for: 3 -> 5; matrix products, arithmetic and copies ran while one was open for 9% -> 1% of each run, Pallas kernels for 0% -> 0%
where the time goes in v8:
time: 124 us; the launch traced here: 123 us
  blocking collectives  57.6 us (46%)
  starting transfers between devices  49 us (40%)
  matrix products  6.53 us (5%)
  waiting for transfers between devices  6.44 us (5%)
  other arithmetic  1.7 us (1%)
    ppermute x14, starting transfers between devices, on_device(): lax.ppermute(block, ('y', 'core'), swaps[swap])  45 us
    all_to_all x1, blocking collectives, on_device(): lax.all_to_all(first, 'inner', split_axis=0, concat_axis=0, tiled=True)  33.5 us
    all_gather x1, blocking collectives, on_device(): grads = lax.all_gather(grads, 'x', axis=1, tiled=True)  24.1 us
    ppermute x14, waiting for transfers between devices, on_device(): lax.ppermute(block, ('y', 'core'), swaps[swap])  5.17 us
    dot_general x1, matrix products, on_device(): lax.dot_general(grads.reshape(tokens.shape[0], columns), tokens, (((0,),...  5.1 us
  transfers between devices with their start and end apart: 16, of which 5 were waited for; matrix products, arithmetic and copies ran while one was open for 1% of the time, Pallas kernels for 0%

profile of v8, /device:TPU:6, one launch (start us, length us, event | category | flops | bytes accessed | tf_op | source)
XLA Modules:
  0.0 122.8 jit_solution(590235707715352014)
XLA Ops:
  0.0 0.9 copy-done
  0.9 1.4 %fusion.36 = bf16[1024,96]{0,1:T(8,128)(2,1)S(1)} fusion(bf16[96,1024]{1,0:T(8,128)(2,1)S(1)} %copy-done, s32[1024]{0:T(1024)S(1)} %get-tuple-element.38, s32[1024]{0:T(1024)S(1)} %get-tuple-element.39, s32[1024]{0:T(1024)S(1)} %get-tuple-element.37, s32[1024]{0:T(1024)S(1)} %get-tuple-element.40, pred[1024]{0:T(1024)(128)(4,1)S(1)} %get-tuple-element.35, ...), kind=kOutput, calls=%fused_computation.50 | convolution fusion | flops 250707968 | bytes 411648 | tf_op jit(solution)/shard_map/dot_general | solution.py:20
  2.4 1.9 %collective-permute-start = (bf16[96,512]{1,0:T(8,128)(2,1)S(1)}, bf16[96,512]{1,0:T(8,128)(2,1)S(1)}, u32[]{:S(2)}, u32[]{:S(2)}) collective-permute-start(bf16[96,512]{1,0:T(8,128)(2,1)S(1)} %get-tuple-element.34), channel_id=1, source_target_pairs={{0,4},{4,0},{1,5},{5,1},{2,6},{6,2},{3,7},{7,3},{8,12},{12,8},{9,1... | collective-permute-start | bytes 294920 | tf_op jit(solution)/shard_map/ppermute | solution.py:38
  4.3 1.3 %collective-permute-done = bf16[96,512]{1,0:T(8,128)(2,1)S(1)} collective-permute-done((bf16[96,512]{1,0:T(8,128)(2,1)S(1)}, bf16[96,512]{1,0:T(8,128)(2,1)S(1)}, u32[]{:S(2)}, u32[]{:S(2)}) %collective-permute-start) | collective-permute-done | bytes 98336 | tf_op jit(solution)/shard_map/ppermute | solution.py:38
  5.6 2.1 %collective-permute-start.1 = (bf16[384,3712]{1,0:T(8,128)(2,1)S(1)}, bf16[384,3712]{1,0:T(8,128)(2,1)}, u32[]{:S(2)}, u32[]{:S(2)}) collective-permute-start(bf16[384,3712]{1,0:T(8,128)(2,1)S(1)} %copy-done.1), channel_id=1, source_target_pairs={{0,4},{4,0},{1,5},{5,1},{2,6},{6,2},{3,7},{7,3},{8,12},{12,8},{9,1... | collective-permute-start | bytes 8552456 | tf_op jit(solution)/shard_map/ppermute | solution.py:40
  7.7 24.1 %all_gather.3 = bf16[2,384,512]{2,1,0:T(8,128)(2,1)S(1)} all-gather(bf16[2,96,512]{2,1,0:T(8,128)(2,1)S(1)} %pad_maximum_fusion.1), channel_id=1, replica_groups=mesh['inner'=16,'y'=8,'core'=2,'x'=4] {'x'}, dimensions={1}, use_global_device_ids=true | all-gather | bytes 983040 | tf_op jit(solution)/shard_map/all_gather | solution.py:42
  31.9 0.0 collective-permute-done.1
  31.9 5.1 %convolution_convert_fusion = bf16[512,3712]{1,0:T(8,128)(2,1)S(1)} fusion(bf16[768,512]{1,0:T(8,128)(2,1)S(1)} %bitcast.69, bf16[384,3712]{1,0:T(8,128)(2,1)} %collective-permute-done.1, bf16[384,3712]{1,0:T(8,128)(2,1)S(1)} %copy-done.1), kind=kOutput, calls=%fused_computation.13 | convolution fusion | flops 2932539392 | bytes 10289152 | tf_op jit(solution)/shard_map/dot_general | solution.py:44
  37.0 1.9 %collective-permute-start.11 = (bf16[64,1792]{1,0:T(8,128)(2,1)S(1)}, bf16[64,1792]{1,0:T(8,128)(2,1)S(1)}, u32[]{:S(2)}, u32[]{:S(2)}) collective-permute-start(bf16[64,1792]{1,0:T(8,128)(2,1)S(1)} %get-tuple-element.32), channel_id=1, source_target_pairs={{0,56},{4,12},{8,16},{12,4},{16,8},{20,28},{24,32},{28,20},{32,24}... | collective-permute-start | bytes 688136 | tf_op jit(solution)/shard_map/ppermute | solution.py:87
  39.0 5.1 %collective-permute-start.9 = (bf16[64,1792]{1,0:T(8,128)(2,1)S(1)}, bf16[64,1792]{1,0:T(8,128)(2,1)S(1)}, u32[]{:S(2)}, u32[]{:S(2)}) collective-permute-start(bf16[64,1792]{1,0:T(8,128)(2,1)S(1)} %get-tuple-element.31), channel_id=1, source_target_pairs={{0,56},{4,12},{8,16},{12,4},{16,8},{20,28},{24,32},{28,20},{32,24}... | collective-permute-start | bytes 688136 | tf_op jit(solution)/shard_map/ppermute | solution.py:87
  44.2 1.9 %collective-permute-start.3 = (bf16[64,1920]{1,0:T(8,128)(2,1)S(1)}, bf16[64,1920]{1,0:T(8,128)(2,1)S(1)}, u32[]{:S(2)}, u32[]{:S(2)}) collective-permute-start(bf16[64,1920]{1,0:T(8,128)(2,1)S(1)} %get-tuple-element.30), channel_id=1, source_target_pairs={{0,8},{4,60},{8,0},{12,20},{16,24},{20,12},{24,16},{28,36},{32,40}... | collective-permute-start | bytes 737288 | tf_op jit(solution)/shard_map/ppermute | solution.py:87
  46.1 3.9 %collective-permute-start.2 = (bf16[64,1920]{1,0:T(8,128)(2,1)S(1)}, bf16[64,1920]{1,0:T(8,128)(2,1)S(1)}, u32[]{:S(2)}, u32[]{:S(2)}) collective-permute-start(bf16[64,1920]{1,0:T(8,128)(2,1)S(1)} %get-tuple-element.29), channel_id=1, source_target_pairs={{0,8},{4,60},{8,0},{12,20},{16,24},{20,12},{24,16},{28,36},{32,40}... | collective-permute-start | bytes 737288 | tf_op jit(solution)/shard_map/ppermute | solution.py:87
  50.0 0.2 collective-permute-done.9
  50.2 0.1 fusion.48
  50.3 1.9 %collective-permute-start.10 = (bf16[64,1792]{1,0:T(8,128)(2,1)S(1)}, bf16[64,1792]{1,0:T(8,128)(2,1)S(1)}, u32[]{:S(2)}, u32[]{:S(2)}) collective-permute-start(bf16[64,1792]{1,0:T(8,128)(2,1)S(1)} %fusion.48), channel_id=1, source_target_pairs={{0,8},{4,60},{8,0},{12,20},{16,24},{20,12},{24,16},{28,36},{32,40}... | collective-permute-start | bytes 688136 | tf_op jit(solution)/shard_map/ppermute | solution.py:87
  52.2 0.1 fusion.47
  52.3 3.9 %collective-permute-start.13 = (bf16[64,1792]{1,0:T(8,128)(2,1)S(1)}, bf16[64,1792]{1,0:T(8,128)(2,1)S(1)}, u32[]{:S(2)}, u32[]{:S(2)}) collective-permute-start(bf16[64,1792]{1,0:T(8,128)(2,1)S(1)} %fusion.47), channel_id=1, source_target_pairs={{0,8},{4,60},{8,0},{12,20},{16,24},{20,12},{24,16},{28,36},{32,40}... | collective-permute-start | bytes 688136 | tf_op jit(solution)/shard_map/ppermute | solution.py:87
  56.2 0.0 collective-permute-done.3
  56.3 0.1 fusion.41
  56.3 4.4 %collective-permute-start.5 = (bf16[64,1920]{1,0:T(8,128)(2,1)S(1)}, bf16[64,1920]{1,0:T(8,128)(2,1)S(1)}, u32[]{:S(2)}, u32[]{:S(2)}) collective-permute-start(bf16[64,1920]{1,0:T(8,128)(2,1)S(1)} %fusion.41), channel_id=1, source_target_pairs={{0,56},{4,12},{8,16},{12,4},{16,8},{20,28},{24,32},{28,20},{32,24}... | collective-permute-start | bytes 737288 | tf_op jit(solution)/shard_map/ppermute | solution.py:87
  60.7 0.0 collective-permute-done.2
  60.8 0.1 fusion.42
  60.8 2.6 %collective-permute-start.4 = (bf16[64,1920]{1,0:T(8,128)(2,1)S(1)}, bf16[64,1920]{1,0:T(8,128)(2,1)S(1)}, u32[]{:S(2)}, u32[]{:S(2)}) collective-permute-start(bf16[64,1920]{1,0:T(8,128)(2,1)S(1)} %fusion.42), channel_id=1, source_target_pairs={{0,56},{4,12},{8,16},{12,4},{16,8},{20,28},{24,32},{28,20},{32,24}... | collective-permute-start | bytes 737288 | tf_op jit(solution)/shard_map/ppermute | solution.py:87
  63.5 0.0 collective-permute-done.10
  63.5 0.1 fusion.49
  63.6 4.4 %collective-permute-start.12 = (bf16[64,1792]{1,0:T(8,128)(2,1)S(1)}, bf16[64,1792]{1,0:T(8,128)(2,1)S(1)}, u32[]{:S(2)}, u32[]{:S(2)}) collective-permute-start(bf16[64,1792]{1,0:T(8,128)(2,1)S(1)} %fusion.49), channel_id=1, source_target_pairs={{0,56},{4,12},{8,16},{12,4},{16,8},{20,28},{24,32},{28,20},{32,24}... | collective-permute-start | bytes 688136 | tf_op jit(solution)/shard_map/ppermute | solution.py:87
  68.0 0.0 collective-permute-done.13
  68.0 0.1 fusion.46
  68.1 2.6 %collective-permute-start.15 = (bf16[64,1792]{1,0:T(8,128)(2,1)S(1)}, bf16[64,1792]{1,0:T(8,128)(2,1)S(1)}, u32[]{:S(2)}, u32[]{:S(2)}) collective-permute-start(bf16[64,1792]{1,0:T(8,128)(2,1)S(1)} %fusion.46), channel_id=1, source_target_pairs={{0,56},{4,12},{8,16},{12,4},{16,8},{20,28},{24,32},{28,20},{32,24}... | collective-permute-start | bytes 688136 | tf_op jit(solution)/shard_map/ppermute | solution.py:87
  70.7 0.0 collective-permute-done.5
  70.7 0.1 fusion.40
  70.8 1.9 %collective-permute-start.7 = (bf16[64,1920]{1,0:T(8,128)(2,1)S(1)}, bf16[64,1920]{1,0:T(8,128)(2,1)S(1)}, u32[]{:S(2)}, u32[]{:S(2)}) collective-permute-start(bf16[64,1920]{1,0:T(8,128)(2,1)S(1)} %fusion.40), channel_id=1, source_target_pairs={{0,8},{4,60},{8,0},{12,20},{16,24},{20,12},{24,16},{28,36},{32,40}... | collective-permute-start | bytes 737288 | tf_op jit(solution)/shard_map/ppermute | solution.py:87
  72.7 0.0 collective-permute-done.4
  72.7 0.1 fusion.43
  72.8 3.9 %collective-permute-start.6 = (bf16[64,1920]{1,0:T(8,128)(2,1)S(1)}, bf16[64,1920]{1,0:T(8,128)(2,1)S(1)}, u32[]{:S(2)}, u32[]{:S(2)}) collective-permute-start(bf16[64,1920]{1,0:T(8,128)(2,1)S(1)} %fusion.43), channel_id=1, source_target_pairs={{0,8},{4,60},{8,0},{12,20},{16,24},{20,12},{24,16},{28,36},{32,40}... | collective-permute-start | bytes 737288 | tf_op jit(solution)/shard_map/ppermute | solution.py:87
  76.7 0.0 collective-permute-done.12
  76.7 0.1 fusion.50
  76.8 1.9 %collective-permute-start.14 = (bf16[64,1792]{1,0:T(8,128)(2,1)S(1)}, bf16[64,1792]{1,0:T(8,128)(2,1)S(1)}, u32[]{:S(2)}, u32[]{:S(2)}) collective-permute-start(bf16[64,1792]{1,0:T(8,128)(2,1)S(1)} %fusion.50), channel_id=1, source_target_pairs={{0,8},{4,60},{8,0},{12,20},{16,24},{20,12},{24,16},{28,36},{32,40}... | collective-permute-start | bytes 688136 | tf_op jit(solution)/shard_map/ppermute | solution.py:87
  78.7 0.1 collective-permute-done.7
  78.9 0.1 fusion.39
  78.9 4.4 %collective-permute-start.8 = (bf16[64,1920]{1,0:T(8,128)(2,1)S(1)}, bf16[64,1920]{1,0:T(8,128)(2,1)S(1)}, u32[]{:S(2)}, u32[]{:S(2)}) collective-permute-start(bf16[64,1920]{1,0:T(8,128)(2,1)S(1)} %fusion.39), channel_id=1, source_target_pairs={{0,56},{4,12},{8,16},{12,4},{16,8},{20,28},{24,32},{28,20},{32,24}... | collective-permute-start | bytes 737288 | tf_op jit(solution)/shard_map/ppermute | solution.py:87
  83.4 3.2 %collective-permute-done.14 = bf16[64,1792]{1,0:T(8,128)(2,1)S(1)} collective-permute-done((bf16[64,1792]{1,0:T(8,128)(2,1)S(1)}, bf16[64,1792]{1,0:T(8,128)(2,1)S(1)}, u32[]{:S(2)}, u32[]{:S(2)}) %collective-permute-start.14) | collective-permute-done | bytes 229408 | tf_op jit(solution)/shard_map/ppermute | solution.py:87
  86.6 0.1 fusion.52
  86.7 1.5 %collective-permute-done.8 = bf16[64,1920]{1,0:T(8,128)(2,1)S(1)} collective-permute-done((bf16[64,1920]{1,0:T(8,128)(2,1)S(1)}, bf16[64,1920]{1,0:T(8,128)(2,1)S(1)}, u32[]{:S(2)}, u32[]{:S(2)}) %collective-permute-start.8) | collective-permute-done | bytes 245792 | tf_op jit(solution)/shard_map/ppermute | solution.py:87
  88.2 0.1 fusion.45
  88.4 0.1 reshape.35
  88.5 33.5 %all_to_all.5 = bf16[16,4,3712]{2,1,0:T(4,128)(2,1)S(1)} all-to-all(bf16[16,4,3712]{2,1,0:T(4,128)(2,1)S(1)} %reshape.35), channel_id=1, replica_groups=mesh['inner'=16,'y'=8,'core'=2,'x'=4] {'inner'}, dimensions={0} | all-to-all | bytes 950272 | tf_op jit(solution)/shard_map/all_to_all | solution.py:95
  122.0 0.8 convert_reduce_fusion
  (14 shorter events, 0.2 us)
Async XLA Ops:
  0.0 0.9 copy-start
  0.9 4.7 %copy-start.1 = (bf16[384,3712]{1,0:T(8,128)(2,1)S(1)}, bf16[384,3712]{1,0:T(8,128)(2,1)}, u32[]{:S(2)}) copy-start(bf16[384,3712]{1,0:T(8,128)(2,1)} %param.2) | copy-start | bytes 8552452
  2.4 3.2 %collective-permute-start = (bf16[96,512]{1,0:T(8,128)(2,1)S(1)}, bf16[96,512]{1,0:T(8,128)(2,1)S(1)}, u32[]{:S(2)}, u32[]{:S(2)}) collective-permute-start(bf16[96,512]{1,0:T(8,128)(2,1)S(1)} %get-tuple-element.34), channel_id=1, source_target_pairs={{0,4},{4,0},{1,5},{5,1},{2,6},{6,2},{3,7},{7,3},{8,12},{12,8},{9,1... | collective-permute-start | bytes 294920 | tf_op jit(solution)/shard_map/ppermute | solution.py:38
  5.6 26.3 %collective-permute-start.1 = (bf16[384,3712]{1,0:T(8,128)(2,1)S(1)}, bf16[384,3712]{1,0:T(8,128)(2,1)}, u32[]{:S(2)}, u32[]{:S(2)}) collective-permute-start(bf16[384,3712]{1,0:T(8,128)(2,1)S(1)} %copy-done.1), channel_id=1, source_target_pairs={{0,4},{4,0},{1,5},{5,1},{2,6},{6,2},{3,7},{7,3},{8,12},{12,8},{9,1... | collective-permute-start | bytes 8552456 | tf_op jit(solution)/shard_map/ppermute | solution.py:40
  37.0 15.2 %collective-permute-start.11 = (bf16[64,1792]{1,0:T(8,128)(2,1)S(1)}, bf16[64,1792]{1,0:T(8,128)(2,1)S(1)}, u32[]{:S(2)}, u32[]{:S(2)}) collective-permute-start(bf16[64,1792]{1,0:T(8,128)(2,1)S(1)} %get-tuple-element.32), channel_id=1, source_target_pairs={{0,56},{4,12},{8,16},{12,4},{16,8},{20,28},{24,32},{28,20},{32,24}... | collective-permute-start | bytes 688136 | tf_op jit(solution)/shard_map/ppermute | solution.py:87
  39.0 11.3 %collective-permute-start.9 = (bf16[64,1792]{1,0:T(8,128)(2,1)S(1)}, bf16[64,1792]{1,0:T(8,128)(2,1)S(1)}, u32[]{:S(2)}, u32[]{:S(2)}) collective-permute-start(bf16[64,1792]{1,0:T(8,128)(2,1)S(1)} %get-tuple-element.31), channel_id=1, source_target_pairs={{0,56},{4,12},{8,16},{12,4},{16,8},{20,28},{24,32},{28,20},{32,24}... | collective-permute-start | bytes 688136 | tf_op jit(solution)/shard_map/ppermute | solution.py:87
  44.2 12.1 %collective-permute-start.3 = (bf16[64,1920]{1,0:T(8,128)(2,1)S(1)}, bf16[64,1920]{1,0:T(8,128)(2,1)S(1)}, u32[]{:S(2)}, u32[]{:S(2)}) collective-permute-start(bf16[64,1920]{1,0:T(8,128)(2,1)S(1)} %get-tuple-element.30), channel_id=1, source_target_pairs={{0,8},{4,60},{8,0},{12,20},{16,24},{20,12},{24,16},{28,36},{32,40}... | collective-permute-start | bytes 737288 | tf_op jit(solution)/shard_map/ppermute | solution.py:87
  46.1 14.7 %collective-permute-start.2 = (bf16[64,1920]{1,0:T(8,128)(2,1)S(1)}, bf16[64,1920]{1,0:T(8,128)(2,1)S(1)}, u32[]{:S(2)}, u32[]{:S(2)}) collective-permute-start(bf16[64,1920]{1,0:T(8,128)(2,1)S(1)} %get-tuple-element.29), channel_id=1, source_target_pairs={{0,8},{4,60},{8,0},{12,20},{16,24},{20,12},{24,16},{28,36},{32,40}... | collective-permute-start | bytes 737288 | tf_op jit(solution)/shard_map/ppermute | solution.py:87
  50.3 13.2 %collective-permute-start.10 = (bf16[64,1792]{1,0:T(8,128)(2,1)S(1)}, bf16[64,1792]{1,0:T(8,128)(2,1)S(1)}, u32[]{:S(2)}, u32[]{:S(2)}) collective-permute-start(bf16[64,1792]{1,0:T(8,128)(2,1)S(1)} %fusion.48), channel_id=1, source_target_pairs={{0,8},{4,60},{8,0},{12,20},{16,24},{20,12},{24,16},{28,36},{32,40}... | collective-permute-start | bytes 688136 | tf_op jit(solution)/shard_map/ppermute | solution.py:87
  52.3 15.7 %collective-permute-start.13 = (bf16[64,1792]{1,0:T(8,128)(2,1)S(1)}, bf16[64,1792]{1,0:T(8,128)(2,1)S(1)}, u32[]{:S(2)}, u32[]{:S(2)}) collective-permute-start(bf16[64,1792]{1,0:T(8,128)(2,1)S(1)} %fusion.47), channel_id=1, source_target_pairs={{0,8},{4,60},{8,0},{12,20},{16,24},{20,12},{24,16},{28,36},{32,40}... | collective-permute-start | bytes 688136 | tf_op jit(solution)/shard_map/ppermute | solution.py:87
  56.3 14.4 %collective-permute-start.5 = (bf16[64,1920]{1,0:T(8,128)(2,1)S(1)}, bf16[64,1920]{1,0:T(8,128)(2,1)S(1)}, u32[]{:S(2)}, u32[]{:S(2)}) collective-permute-start(bf16[64,1920]{1,0:T(8,128)(2,1)S(1)} %fusion.41), channel_id=1, source_target_pairs={{0,56},{4,12},{8,16},{12,4},{16,8},{20,28},{24,32},{28,20},{32,24}... | collective-permute-start | bytes 737288 | tf_op jit(solution)/shard_map/ppermute | solution.py:87
  60.8 11.9 %collective-permute-start.4 = (bf16[64,1920]{1,0:T(8,128)(2,1)S(1)}, bf16[64,1920]{1,0:T(8,128)(2,1)S(1)}, u32[]{:S(2)}, u32[]{:S(2)}) collective-permute-start(bf16[64,1920]{1,0:T(8,128)(2,1)S(1)} %fusion.42), channel_id=1, source_target_pairs={{0,56},{4,12},{8,16},{12,4},{16,8},{20,28},{24,32},{28,20},{32,24}... | collective-permute-start | bytes 737288 | tf_op jit(solution)/shard_map/ppermute | solution.py:87
  63.6 13.2 %collective-permute-start.12 = (bf16[64,1792]{1,0:T(8,128)(2,1)S(1)}, bf16[64,1792]{1,0:T(8,128)(2,1)S(1)}, u32[]{:S(2)}, u32[]{:S(2)}) collective-permute-start(bf16[64,1792]{1,0:T(8,128)(2,1)S(1)} %fusion.49), channel_id=1, source_target_pairs={{0,56},{4,12},{8,16},{12,4},{16,8},{20,28},{24,32},{28,20},{32,24}... | collective-permute-start | bytes 688136 | tf_op jit(solution)/shard_map/ppermute | solution.py:87
  68.1 15.3 %collective-permute-start.15 = (bf16[64,1792]{1,0:T(8,128)(2,1)S(1)}, bf16[64,1792]{1,0:T(8,128)(2,1)S(1)}, u32[]{:S(2)}, u32[]{:S(2)}) collective-permute-start(bf16[64,1792]{1,0:T(8,128)(2,1)S(1)} %fusion.46), channel_id=1, source_target_pairs={{0,56},{4,12},{8,16},{12,4},{16,8},{20,28},{24,32},{28,20},{32,24}... | collective-permute-start | bytes 688136 | tf_op jit(solution)/shard_map/ppermute | solution.py:87
  70.8 8.1 %collective-permute-start.7 = (bf16[64,1920]{1,0:T(8,128)(2,1)S(1)}, bf16[64,1920]{1,0:T(8,128)(2,1)S(1)}, u32[]{:S(2)}, u32[]{:S(2)}) collective-permute-start(bf16[64,1920]{1,0:T(8,128)(2,1)S(1)} %fusion.40), channel_id=1, source_target_pairs={{0,8},{4,60},{8,0},{12,20},{16,24},{20,12},{24,16},{28,36},{32,40}... | collective-permute-start | bytes 737288 | tf_op jit(solution)/shard_map/ppermute | solution.py:87
  72.8 13.9 %collective-permute-start.6 = (bf16[64,1920]{1,0:T(8,128)(2,1)S(1)}, bf16[64,1920]{1,0:T(8,128)(2,1)S(1)}, u32[]{:S(2)}, u32[]{:S(2)}) collective-permute-start(bf16[64,1920]{1,0:T(8,128)(2,1)S(1)} %fusion.43), channel_id=1, source_target_pairs={{0,8},{4,60},{8,0},{12,20},{16,24},{20,12},{24,16},{28,36},{32,40}... | collective-permute-start | bytes 737288 | tf_op jit(solution)/shard_map/ppermute | solution.py:87
  76.8 9.8 %collective-permute-start.14 = (bf16[64,1792]{1,0:T(8,128)(2,1)S(1)}, bf16[64,1792]{1,0:T(8,128)(2,1)S(1)}, u32[]{:S(2)}, u32[]{:S(2)}) collective-permute-start(bf16[64,1792]{1,0:T(8,128)(2,1)S(1)} %fusion.50), channel_id=1, source_target_pairs={{0,8},{4,60},{8,0},{12,20},{16,24},{20,12},{24,16},{28,36},{32,40}... | collective-permute-start | bytes 688136 | tf_op jit(solution)/shard_map/ppermute | solution.py:87
  78.9 9.3 %collective-permute-start.8 = (bf16[64,1920]{1,0:T(8,128)(2,1)S(1)}, bf16[64,1920]{1,0:T(8,128)(2,1)S(1)}, u32[]{:S(2)}, u32[]{:S(2)}) collective-permute-start(bf16[64,1920]{1,0:T(8,128)(2,1)S(1)} %fusion.39), channel_id=1, source_target_pairs={{0,56},{4,12},{8,16},{12,4},{16,8},{20,28},{24,32},{28,20},{32,24}... | collective-permute-start | bytes 737288 | tf_op jit(solution)/shard_map/ppermute | solution.py:87

commit v9 on v8

--- a/solution.py
+++ b/solution.py
@@ -83,6 +83,8 @@
             block = (block + come.astype(jnp.float32)).astype(jnp.bfloat16)
         else:
             block = block.astype(jnp.bfloat16)
+            if piece in before:
+                block, before[1 - piece] = lax.optimization_barrier((block, before[1 - piece]))
         before[piece] = block
         arrived[distance, piece, swap] = lax.ppermute(block, ("y", "core"), swaps[swap])
     sums = []

time: 124 us -> 125 us (level)
  blocking collectives: 57.6 us -> 59.7 us
  starting transfers between devices: 49 us -> 47.1 us
    all_to_all x1, blocking collectives: 33.5 us -> 35.5 us  [on_device(): lax.all_to_all(first, 'inner', split_axis=0, concat_axis=0, tiled=True)]
    ppermute x14, starting transfers between devices: 45 us -> 43.2 us  [on_device(): lax.ppermute(block, ('y', 'core'), swaps[swap])]
  transfers between devices with their start and end apart: 16 -> 16, of which waited for: 5 -> 6; matrix products, arithmetic and copies ran while one was open for 1% -> 1% of each run, Pallas kernels for 0% -> 0%
where the time goes in v9:
time: 125 us; the launch traced here: 124 us
  blocking collectives  59.7 us (48%)
  starting transfers between devices  47.1 us (38%)
  waiting for transfers between devices  7.34 us (6%)
  matrix products  6.53 us (5%)
  other arithmetic  1.7 us (1%)
    ppermute x14, starting transfers between devices, on_device(): lax.ppermute(block, ('y', 'core'), swaps[swap])  43.2 us
    all_to_all x1, blocking collectives, on_device(): lax.all_to_all(first, 'inner', split_axis=0, concat_axis=0, tiled=True)  35.5 us
    all_gather x1, blocking collectives, on_device(): grads = lax.all_gather(grads, 'x', axis=1, tiled=True)  24.1 us
    ppermute x14, waiting for transfers between devices, on_device(): lax.ppermute(block, ('y', 'core'), swaps[swap])  6.07 us
    dot_general x1, matrix products, on_device(): lax.dot_general(grads.reshape(tokens.shape[0], columns), tokens, (((0,),...  5.1 us
  transfers between devices with their start and end apart: 16, of which 6 were waited for; matrix products, arithmetic and copies ran while one was open for 1% of the time, Pallas kernels for 0%

profile of v9, /device:TPU:6, one launch (start us, length us, event | category | flops | bytes accessed | tf_op | source)
XLA Modules:
  0.0 123.9 jit_solution(15493684862394619949)
XLA Ops:
  0.0 0.9 copy-done
  0.9 1.4 %fusion.36 = bf16[1024,96]{0,1:T(8,128)(2,1)S(1)} fusion(bf16[96,1024]{1,0:T(8,128)(2,1)S(1)} %copy-done, s32[1024]{0:T(1024)S(1)} %get-tuple-element.40, s32[1024]{0:T(1024)S(1)} %get-tuple-element.41, s32[1024]{0:T(1024)S(1)} %get-tuple-element.39, s32[1024]{0:T(1024)S(1)} %get-tuple-element.42, pred[1024]{0:T(1024)(128)(4,1)S(1)} %get-tuple-element.37, ...), kind=kOutput, calls=%fused_computation.50 | convolution fusion | flops 250707968 | bytes 411648 | tf_op jit(solution)/shard_map/dot_general | solution.py:20
  2.4 1.9 %collective-permute-start = (bf16[96,512]{1,0:T(8,128)(2,1)S(1)}, bf16[96,512]{1,0:T(8,128)(2,1)S(1)}, u32[]{:S(2)}, u32[]{:S(2)}) collective-permute-start(bf16[96,512]{1,0:T(8,128)(2,1)S(1)} %get-tuple-element.36), channel_id=1, source_target_pairs={{0,4},{4,0},{1,5},{5,1},{2,6},{6,2},{3,7},{7,3},{8,12},{12,8},{9,1... | collective-permute-start | bytes 294920 | tf_op jit(solution)/shard_map/ppermute | solution.py:38
  4.3 1.3 %collective-permute-done = bf16[96,512]{1,0:T(8,128)(2,1)S(1)} collective-permute-done((bf16[96,512]{1,0:T(8,128)(2,1)S(1)}, bf16[96,512]{1,0:T(8,128)(2,1)S(1)}, u32[]{:S(2)}, u32[]{:S(2)}) %collective-permute-start) | collective-permute-done | bytes 98336 | tf_op jit(solution)/shard_map/ppermute | solution.py:38
  5.6 2.1 %collective-permute-start.1 = (bf16[384,3712]{1,0:T(8,128)(2,1)S(1)}, bf16[384,3712]{1,0:T(8,128)(2,1)}, u32[]{:S(2)}, u32[]{:S(2)}) collective-permute-start(bf16[384,3712]{1,0:T(8,128)(2,1)S(1)} %copy-done.1), channel_id=1, source_target_pairs={{0,4},{4,0},{1,5},{5,1},{2,6},{6,2},{3,7},{7,3},{8,12},{12,8},{9,1... | collective-permute-start | bytes 8552456 | tf_op jit(solution)/shard_map/ppermute | solution.py:40
  7.7 24.1 %all_gather.3 = bf16[2,384,512]{2,1,0:T(8,128)(2,1)S(1)} all-gather(bf16[2,96,512]{2,1,0:T(8,128)(2,1)S(1)} %pad_maximum_fusion.1), channel_id=1, replica_groups=mesh['inner'=16,'y'=8,'core'=2,'x'=4] {'x'}, dimensions={1}, use_global_device_ids=true | all-gather | bytes 983040 | tf_op jit(solution)/shard_map/all_gather | solution.py:42
  31.9 0.0 collective-permute-done.1
  31.9 5.1 %convolution_convert_fusion = bf16[512,3712]{1,0:T(8,128)(2,1)S(1)} fusion(bf16[768,512]{1,0:T(8,128)(2,1)S(1)} %bitcast.69, bf16[384,3712]{1,0:T(8,128)(2,1)} %collective-permute-done.1, bf16[384,3712]{1,0:T(8,128)(2,1)S(1)} %copy-done.1), kind=kOutput, calls=%fused_computation.13 | convolution fusion | flops 2932539392 | bytes 10289152 | tf_op jit(solution)/shard_map/dot_general | solution.py:44
  37.0 1.9 %collective-permute-start.9 = (bf16[64,1792]{1,0:T(8,128)(2,1)S(1)}, bf16[64,1792]{1,0:T(8,128)(2,1)S(1)}, u32[]{:S(2)}, u32[]{:S(2)}) collective-permute-start(bf16[64,1792]{1,0:T(8,128)(2,1)S(1)} %get-tuple-element.33), channel_id=1, source_target_pairs={{0,56},{4,12},{8,16},{12,4},{16,8},{20,28},{24,32},{28,20},{32,24}... | collective-permute-start | bytes 688136 | tf_op jit(solution)/shard_map/ppermute | solution.py:89
  39.0 1.9 %collective-permute-start.2 = (bf16[64,1920]{1,0:T(8,128)(2,1)S(1)}, bf16[64,1920]{1,0:T(8,128)(2,1)S(1)}, u32[]{:S(2)}, u32[]{:S(2)}) collective-permute-start(bf16[64,1920]{1,0:T(8,128)(2,1)S(1)} %get-tuple-element.20), channel_id=1, source_target_pairs={{0,8},{4,60},{8,0},{12,20},{16,24},{20,12},{24,16},{28,36},{32,40}... | collective-permute-start | bytes 737288 | tf_op jit(solution)/shard_map/ppermute | solution.py:89
  40.9 5.1 %collective-permute-start.11 = (bf16[64,1792]{1,0:T(8,128)(2,1)S(1)}, bf16[64,1792]{1,0:T(8,128)(2,1)S(1)}, u32[]{:S(2)}, u32[]{:S(2)}) collective-permute-start(bf16[64,1792]{1,0:T(8,128)(2,1)S(1)} %get-tuple-element.25), channel_id=1, source_target_pairs={{0,56},{4,12},{8,16},{12,4},{16,8},{20,28},{24,32},{28,20},{32,24}... | collective-permute-start | bytes 688136 | tf_op jit(solution)/shard_map/ppermute | solution.py:89
  46.1 1.9 %collective-permute-start.3 = (bf16[64,1920]{1,0:T(8,128)(2,1)S(1)}, bf16[64,1920]{1,0:T(8,128)(2,1)S(1)}, u32[]{:S(2)}, u32[]{:S(2)}) collective-permute-start(bf16[64,1920]{1,0:T(8,128)(2,1)S(1)} %get-tuple-element.31), channel_id=1, source_target_pairs={{0,8},{4,60},{8,0},{12,20},{16,24},{20,12},{24,16},{28,36},{32,40}... | collective-permute-start | bytes 737288 | tf_op jit(solution)/shard_map/ppermute | solution.py:89
  48.0 0.6 collective-permute-done.9
  48.6 0.1 fusion.48
  48.7 3.3 %collective-permute-start.10 = (bf16[64,1792]{1,0:T(8,128)(2,1)S(1)}, bf16[64,1792]{1,0:T(8,128)(2,1)S(1)}, u32[]{:S(2)}, u32[]{:S(2)}) collective-permute-start(bf16[64,1792]{1,0:T(8,128)(2,1)S(1)} %fusion.48), channel_id=1, source_target_pairs={{0,8},{4,60},{8,0},{12,20},{16,24},{20,12},{24,16},{28,36},{32,40}... | collective-permute-start | bytes 688136 | tf_op jit(solution)/shard_map/ppermute | solution.py:89
  52.0 1.3 %collective-permute-done.11 = bf16[64,1792]{1,0:T(8,128)(2,1)S(1)} collective-permute-done((bf16[64,1792]{1,0:T(8,128)(2,1)S(1)}, bf16[64,1792]{1,0:T(8,128)(2,1)S(1)}, u32[]{:S(2)}, u32[]{:S(2)}) %collective-permute-start.11) | collective-permute-done | bytes 229408 | tf_op jit(solution)/shard_map/ppermute | solution.py:89
  53.3 0.1 fusion.47
  53.3 1.9 %collective-permute-start.13 = (bf16[64,1792]{1,0:T(8,128)(2,1)S(1)}, bf16[64,1792]{1,0:T(8,128)(2,1)S(1)}, u32[]{:S(2)}, u32[]{:S(2)}) collective-permute-start(bf16[64,1792]{1,0:T(8,128)(2,1)S(1)} %fusion.47), channel_id=1, source_target_pairs={{0,8},{4,60},{8,0},{12,20},{16,24},{20,12},{24,16},{28,36},{32,40}... | collective-permute-start | bytes 688136 | tf_op jit(solution)/shard_map/ppermute | solution.py:89
  55.3 0.0 collective-permute-done.3
  55.3 0.1 fusion.41
  55.4 5.1 %collective-permute-start.5 = (bf16[64,1920]{1,0:T(8,128)(2,1)S(1)}, bf16[64,1920]{1,0:T(8,128)(2,1)S(1)}, u32[]{:S(2)}, u32[]{:S(2)}) collective-permute-start(bf16[64,1920]{1,0:T(8,128)(2,1)S(1)} %fusion.41), channel_id=1, source_target_pairs={{0,56},{4,12},{8,16},{12,4},{16,8},{20,28},{24,32},{28,20},{32,24}... | collective-permute-start | bytes 737288 | tf_op jit(solution)/shard_map/ppermute | solution.py:89
  60.5 0.0 collective-permute-done.2
  60.5 0.1 fusion.42
  60.6 1.9 %collective-permute-start.4 = (bf16[64,1920]{1,0:T(8,128)(2,1)S(1)}, bf16[64,1920]{1,0:T(8,128)(2,1)S(1)}, u32[]{:S(2)}, u32[]{:S(2)}) collective-permute-start(bf16[64,1920]{1,0:T(8,128)(2,1)S(1)} %fusion.42), channel_id=1, source_target_pairs={{0,56},{4,12},{8,16},{12,4},{16,8},{20,28},{24,32},{28,20},{32,24}... | collective-permute-start | bytes 737288 | tf_op jit(solution)/shard_map/ppermute | solution.py:89
  62.5 0.0 collective-permute-done.10
  62.5 0.1 fusion.49
  62.6 5.1 %collective-permute-start.12 = (bf16[64,1792]{1,0:T(8,128)(2,1)S(1)}, bf16[64,1792]{1,0:T(8,128)(2,1)S(1)}, u32[]{:S(2)}, u32[]{:S(2)}) collective-permute-start(bf16[64,1792]{1,0:T(8,128)(2,1)S(1)} %fusion.49), channel_id=1, source_target_pairs={{0,56},{4,12},{8,16},{12,4},{16,8},{20,28},{24,32},{28,20},{32,24}... | collective-permute-start | bytes 688136 | tf_op jit(solution)/shard_map/ppermute | solution.py:89
  67.7 0.0 collective-permute-done.13
  67.7 0.1 fusion.46
  67.8 1.9 %collective-permute-start.15 = (bf16[64,1792]{1,0:T(8,128)(2,1)S(1)}, bf16[64,1792]{1,0:T(8,128)(2,1)S(1)}, u32[]{:S(2)}, u32[]{:S(2)}) collective-permute-start(bf16[64,1792]{1,0:T(8,128)(2,1)S(1)} %fusion.46), channel_id=1, source_target_pairs={{0,56},{4,12},{8,16},{12,4},{16,8},{20,28},{24,32},{28,20},{32,24}... | collective-permute-start | bytes 688136 | tf_op jit(solution)/shard_map/ppermute | solution.py:89
  69.7 0.0 collective-permute-done.5
  69.7 0.1 fusion.40
  69.8 1.9 %collective-permute-start.7 = (bf16[64,1920]{1,0:T(8,128)(2,1)S(1)}, bf16[64,1920]{1,0:T(8,128)(2,1)S(1)}, u32[]{:S(2)}, u32[]{:S(2)}) collective-permute-start(bf16[64,1920]{1,0:T(8,128)(2,1)S(1)} %fusion.40), channel_id=1, source_target_pairs={{0,8},{4,60},{8,0},{12,20},{16,24},{20,12},{24,16},{28,36},{32,40}... | collective-permute-start | bytes 737288 | tf_op jit(solution)/shard_map/ppermute | solution.py:89
  71.7 0.0 collective-permute-done.4
  71.8 0.1 fusion.43
  71.8 3.9 %collective-permute-start.6 = (bf16[64,1920]{1,0:T(8,128)(2,1)S(1)}, bf16[64,1920]{1,0:T(8,128)(2,1)S(1)}, u32[]{:S(2)}, u32[]{:S(2)}) collective-permute-start(bf16[64,1920]{1,0:T(8,128)(2,1)S(1)} %fusion.43), channel_id=1, source_target_pairs={{0,8},{4,60},{8,0},{12,20},{16,24},{20,12},{24,16},{28,36},{32,40}... | collective-permute-start | bytes 737288 | tf_op jit(solution)/shard_map/ppermute | solution.py:89
  75.8 0.1 fusion.50
  75.8 1.9 %collective-permute-start.14 = (bf16[64,1792]{1,0:T(8,128)(2,1)S(1)}, bf16[64,1792]{1,0:T(8,128)(2,1)S(1)}, u32[]{:S(2)}, u32[]{:S(2)}) collective-permute-start(bf16[64,1792]{1,0:T(8,128)(2,1)S(1)} %fusion.50), channel_id=1, source_target_pairs={{0,8},{4,60},{8,0},{12,20},{16,24},{20,12},{24,16},{28,36},{32,40}... | collective-permute-start | bytes 688136 | tf_op jit(solution)/shard_map/ppermute | solution.py:89
  77.8 0.1 collective-permute-done.7
  77.9 0.1 fusion.39
  78.0 5.1 %collective-permute-start.8 = (bf16[64,1920]{1,0:T(8,128)(2,1)S(1)}, bf16[64,1920]{1,0:T(8,128)(2,1)S(1)}, u32[]{:S(2)}, u32[]{:S(2)}) collective-permute-start(bf16[64,1920]{1,0:T(8,128)(2,1)S(1)} %fusion.39), channel_id=1, source_target_pairs={{0,56},{4,12},{8,16},{12,4},{16,8},{20,28},{24,32},{28,20},{32,24}... | collective-permute-start | bytes 737288 | tf_op jit(solution)/shard_map/ppermute | solution.py:89
  83.1 2.5 %collective-permute-done.14 = bf16[64,1792]{1,0:T(8,128)(2,1)S(1)} collective-permute-done((bf16[64,1792]{1,0:T(8,128)(2,1)S(1)}, bf16[64,1792]{1,0:T(8,128)(2,1)S(1)}, u32[]{:S(2)}, u32[]{:S(2)}) %collective-permute-start.14) | collective-permute-done | bytes 229408 | tf_op jit(solution)/shard_map/ppermute | solution.py:89
  85.6 0.1 fusion.52
  85.7 1.5 %collective-permute-done.8 = bf16[64,1920]{1,0:T(8,128)(2,1)S(1)} collective-permute-done((bf16[64,1920]{1,0:T(8,128)(2,1)S(1)}, bf16[64,1920]{1,0:T(8,128)(2,1)S(1)}, u32[]{:S(2)}, u32[]{:S(2)}) %collective-permute-start.8) | collective-permute-done | bytes 245792 | tf_op jit(solution)/shard_map/ppermute | solution.py:89
  87.3 0.1 fusion.45
  87.4 0.1 reshape.35
  87.5 35.5 %all_to_all.5 = bf16[16,4,3712]{2,1,0:T(4,128)(2,1)S(1)} all-to-all(bf16[16,4,3712]{2,1,0:T(4,128)(2,1)S(1)} %reshape.35), channel_id=1, replica_groups=mesh['inner'=16,'y'=8,'core'=2,'x'=4] {'inner'}, dimensions={0} | all-to-all | bytes 950272 | tf_op jit(solution)/shard_map/all_to_all | solution.py:97
  123.1 0.8 convert_reduce_fusion
  (14 shorter events, 0.2 us)
Async XLA Ops:
  0.0 0.9 copy-start
  0.9 4.7 %copy-start.1 = (bf16[384,3712]{1,0:T(8,128)(2,1)S(1)}, bf16[384,3712]{1,0:T(8,128)(2,1)}, u32[]{:S(2)}) copy-start(bf16[384,3712]{1,0:T(8,128)(2,1)} %param.2) | copy-start | bytes 8552452
  2.4 3.2 %collective-permute-start = (bf16[96,512]{1,0:T(8,128)(2,1)S(1)}, bf16[96,512]{1,0:T(8,128)(2,1)S(1)}, u32[]{:S(2)}, u32[]{:S(2)}) collective-permute-start(bf16[96,512]{1,0:T(8,128)(2,1)S(1)} %get-tuple-element.36), channel_id=1, source_target_pairs={{0,4},{4,0},{1,5},{5,1},{2,6},{6,2},{3,7},{7,3},{8,12},{12,8},{9,1... | collective-permute-start | bytes 294920 | tf_op jit(solution)/shard_map/ppermute | solution.py:38
  5.6 26.3 %collective-permute-start.1 = (bf16[384,3712]{1,0:T(8,128)(2,1)S(1)}, bf16[384,3712]{1,0:T(8,128)(2,1)}, u32[]{:S(2)}, u32[]{:S(2)}) collective-permute-start(bf16[384,3712]{1,0:T(8,128)(2,1)S(1)} %copy-done.1), channel_id=1, source_target_pairs={{0,4},{4,0},{1,5},{5,1},{2,6},{6,2},{3,7},{7,3},{8,12},{12,8},{9,1... | collective-permute-start | bytes 8552456 | tf_op jit(solution)/shard_map/ppermute | solution.py:40
  37.0 11.6 %collective-permute-start.9 = (bf16[64,1792]{1,0:T(8,128)(2,1)S(1)}, bf16[64,1792]{1,0:T(8,128)(2,1)S(1)}, u32[]{:S(2)}, u32[]{:S(2)}) collective-permute-start(bf16[64,1792]{1,0:T(8,128)(2,1)S(1)} %get-tuple-element.33), channel_id=1, source_target_pairs={{0,56},{4,12},{8,16},{12,4},{16,8},{20,28},{24,32},{28,20},{32,24}... | collective-permute-start | bytes 688136 | tf_op jit(solution)/shard_map/ppermute | solution.py:89
  39.0 21.5 %collective-permute-start.2 = (bf16[64,1920]{1,0:T(8,128)(2,1)S(1)}, bf16[64,1920]{1,0:T(8,128)(2,1)S(1)}, u32[]{:S(2)}, u32[]{:S(2)}) collective-permute-start(bf16[64,1920]{1,0:T(8,128)(2,1)S(1)} %get-tuple-element.20), channel_id=1, source_target_pairs={{0,8},{4,60},{8,0},{12,20},{16,24},{20,12},{24,16},{28,36},{32,40}... | collective-permute-start | bytes 737288 | tf_op jit(solution)/shard_map/ppermute | solution.py:89
  40.9 12.3 %collective-permute-start.11 = (bf16[64,1792]{1,0:T(8,128)(2,1)S(1)}, bf16[64,1792]{1,0:T(8,128)(2,1)S(1)}, u32[]{:S(2)}, u32[]{:S(2)}) collective-permute-start(bf16[64,1792]{1,0:T(8,128)(2,1)S(1)} %get-tuple-element.25), channel_id=1, source_target_pairs={{0,56},{4,12},{8,16},{12,4},{16,8},{20,28},{24,32},{28,20},{32,24}... | collective-permute-start | bytes 688136 | tf_op jit(solution)/shard_map/ppermute | solution.py:89
  46.1 9.2 %collective-permute-start.3 = (bf16[64,1920]{1,0:T(8,128)(2,1)S(1)}, bf16[64,1920]{1,0:T(8,128)(2,1)S(1)}, u32[]{:S(2)}, u32[]{:S(2)}) collective-permute-start(bf16[64,1920]{1,0:T(8,128)(2,1)S(1)} %get-tuple-element.31), channel_id=1, source_target_pairs={{0,8},{4,60},{8,0},{12,20},{16,24},{20,12},{24,16},{28,36},{32,40}... | collective-permute-start | bytes 737288 | tf_op jit(solution)/shard_map/ppermute | solution.py:89
  48.7 13.8 %collective-permute-start.10 = (bf16[64,1792]{1,0:T(8,128)(2,1)S(1)}, bf16[64,1792]{1,0:T(8,128)(2,1)S(1)}, u32[]{:S(2)}, u32[]{:S(2)}) collective-permute-start(bf16[64,1792]{1,0:T(8,128)(2,1)S(1)} %fusion.48), channel_id=1, source_target_pairs={{0,8},{4,60},{8,0},{12,20},{16,24},{20,12},{24,16},{28,36},{32,40}... | collective-permute-start | bytes 688136 | tf_op jit(solution)/shard_map/ppermute | solution.py:89
  53.3 14.4 %collective-permute-start.13 = (bf16[64,1792]{1,0:T(8,128)(2,1)S(1)}, bf16[64,1792]{1,0:T(8,128)(2,1)S(1)}, u32[]{:S(2)}, u32[]{:S(2)}) collective-permute-start(bf16[64,1792]{1,0:T(8,128)(2,1)S(1)} %fusion.47), channel_id=1, source_target_pairs={{0,8},{4,60},{8,0},{12,20},{16,24},{20,12},{24,16},{28,36},{32,40}... | collective-permute-start | bytes 688136 | tf_op jit(solution)/shard_map/ppermute | solution.py:89
  55.4 14.4 %collective-permute-start.5 = (bf16[64,1920]{1,0:T(8,128)(2,1)S(1)}, bf16[64,1920]{1,0:T(8,128)(2,1)S(1)}, u32[]{:S(2)}, u32[]{:S(2)}) collective-permute-start(bf16[64,1920]{1,0:T(8,128)(2,1)S(1)} %fusion.41), channel_id=1, source_target_pairs={{0,56},{4,12},{8,16},{12,4},{16,8},{20,28},{24,32},{28,20},{32,24}... | collective-permute-start | bytes 737288 | tf_op jit(solution)/shard_map/ppermute | solution.py:89
  60.6 11.2 %collective-permute-start.4 = (bf16[64,1920]{1,0:T(8,128)(2,1)S(1)}, bf16[64,1920]{1,0:T(8,128)(2,1)S(1)}, u32[]{:S(2)}, u32[]{:S(2)}) collective-permute-start(bf16[64,1920]{1,0:T(8,128)(2,1)S(1)} %fusion.42), channel_id=1, source_target_pairs={{0,56},{4,12},{8,16},{12,4},{16,8},{20,28},{24,32},{28,20},{32,24}... | collective-permute-start | bytes 737288 | tf_op jit(solution)/shard_map/ppermute | solution.py:89
  62.6 13.2 %collective-permute-start.12 = (bf16[64,1792]{1,0:T(8,128)(2,1)S(1)}, bf16[64,1792]{1,0:T(8,128)(2,1)S(1)}, u32[]{:S(2)}, u32[]{:S(2)}) collective-permute-start(bf16[64,1792]{1,0:T(8,128)(2,1)S(1)} %fusion.49), channel_id=1, source_target_pairs={{0,56},{4,12},{8,16},{12,4},{16,8},{20,28},{24,32},{28,20},{32,24}... | collective-permute-start | bytes 688136 | tf_op jit(solution)/shard_map/ppermute | solution.py:89
  67.8 15.3 %collective-permute-start.15 = (bf16[64,1792]{1,0:T(8,128)(2,1)S(1)}, bf16[64,1792]{1,0:T(8,128)(2,1)S(1)}, u32[]{:S(2)}, u32[]{:S(2)}) collective-permute-start(bf16[64,1792]{1,0:T(8,128)(2,1)S(1)} %fusion.46), channel_id=1, source_target_pairs={{0,56},{4,12},{8,16},{12,4},{16,8},{20,28},{24,32},{28,20},{32,24}... | collective-permute-start | bytes 688136 | tf_op jit(solution)/shard_map/ppermute | solution.py:89
  69.8 8.1 %collective-permute-start.7 = (bf16[64,1920]{1,0:T(8,128)(2,1)S(1)}, bf16[64,1920]{1,0:T(8,128)(2,1)S(1)}, u32[]{:S(2)}, u32[]{:S(2)}) collective-permute-start(bf16[64,1920]{1,0:T(8,128)(2,1)S(1)} %fusion.40), channel_id=1, source_target_pairs={{0,8},{4,60},{8,0},{12,20},{16,24},{20,12},{24,16},{28,36},{32,40}... | collective-permute-start | bytes 737288 | tf_op jit(solution)/shard_map/ppermute | solution.py:89
  71.8 13.9 %collective-permute-start.6 = (bf16[64,1920]{1,0:T(8,128)(2,1)S(1)}, bf16[64,1920]{1,0:T(8,128)(2,1)S(1)}, u32[]{:S(2)}, u32[]{:S(2)}) collective-permute-start(bf16[64,1920]{1,0:T(8,128)(2,1)S(1)} %fusion.43), channel_id=1, source_target_pairs={{0,8},{4,60},{8,0},{12,20},{16,24},{20,12},{24,16},{28,36},{32,40}... | collective-permute-start | bytes 737288 | tf_op jit(solution)/shard_map/ppermute | solution.py:89
  75.8 9.8 %collective-permute-start.14 = (bf16[64,1792]{1,0:T(8,128)(2,1)S(1)}, bf16[64,1792]{1,0:T(8,128)(2,1)S(1)}, u32[]{:S(2)}, u32[]{:S(2)}) collective-permute-start(bf16[64,1792]{1,0:T(8,128)(2,1)S(1)} %fusion.50), channel_id=1, source_target_pairs={{0,8},{4,60},{8,0},{12,20},{16,24},{20,12},{24,16},{28,36},{32,40}... | collective-permute-start | bytes 688136 | tf_op jit(solution)/shard_map/ppermute | solution.py:89
  78.0 9.3 %collective-permute-start.8 = (bf16[64,1920]{1,0:T(8,128)(2,1)S(1)}, bf16[64,1920]{1,0:T(8,128)(2,1)S(1)}, u32[]{:S(2)}, u32[]{:S(2)}) collective-permute-start(bf16[64,1920]{1,0:T(8,128)(2,1)S(1)} %fusion.39), channel_id=1, source_target_pairs={{0,56},{4,12},{8,16},{12,4},{16,8},{20,28},{24,32},{28,20},{32,24}... | collective-permute-start | bytes 737288 | tf_op jit(solution)/shard_map/ppermute | solution.py:89

commit v10 on v9

--- a/solution.py
+++ b/solution.py
@@ -7,15 +7,16 @@
 SWAP = [(0, 1), (1, 0)]
 
 
-def in_owner_order(out_grad, inner, outer):
+def in_owner_order(out_grad, far, near, outer):
     columns = out_grad.shape[1]
-    rows = columns // (inner * outer * 2)
+    rows = columns // (far * near * outer * 2)
     new = lax.broadcasted_iota(jnp.int32, (columns, columns), 1)
     old = lax.broadcasted_iota(jnp.int32, (columns, columns), 0)
     row, rest = new % rows, new // rows
-    i, rest = rest % inner, rest // inner
+    f, rest = rest % far, rest // far
+    n, rest = rest % near, rest // near
     y, core = rest % outer, rest // outer
-    source = ((i * outer + y) * 2 + core) * rows + row
+    source = (((f * near + n) * outer + y) * 2 + core) * rows + row
     one_hot = (source == old).astype(out_grad.dtype)
     moved = lax.dot_general(
         out_grad, one_hot, (((1,), (0,)), ((), ())), preferred_element_type=jnp.float32
@@ -24,10 +25,11 @@
 
 
 def on_device(activations, out_grad):
-    inner, outer = lax.axis_size("inner"), lax.axis_size("y")
-    core, me = lax.axis_index("core"), lax.axis_index("y")
+    far_z, near_z, outer = (lax.axis_size(name) for name in ("far", "near", "y"))
+    core, me, near = (lax.axis_index(name) for name in ("core", "y", "near"))
+    inner = far_z * near_z
     width = activations.shape[1]
-    ordered = in_owner_order(out_grad, inner, outer)
+    ordered = in_owner_order(out_grad, far_z, near_z, outer)
     columns = ordered.shape[1] // 2
 
     def half_of(owner):
@@ -87,24 +89,40 @@
                 block, before[1 - piece] = lax.optimization_barrier((block, before[1 - piece]))
         before[piece] = block
         arrived[distance, piece, swap] = lax.ppermute(block, ("y", "core"), swaps[swap])
+    z_pairings = (
+        [i ^ 1 for i in range(inner)],
+        [(((i + inner - 1) ^ 1) + 1) % inner for i in range(inner)],
+    )
+    z_swap = [(2 * i + c, 2 * z_pairings[c][i] + c) for i in range(inner) for c in (0, 1)]
+    half = columns // outer // near_z
     sums = []
     for piece in (0, 1):
         come = (arrived[1, piece, 0], arrived[1, piece, 1])
         total = own(piece, 0, 0) + come[0].astype(jnp.float32) + come[1].astype(jnp.float32)
-        sums.append(total.astype(jnp.bfloat16))
+        total = total.astype(jnp.bfloat16)
+
+        def rows_of(parity):
+            return lax.dynamic_slice_in_dim(
+                total, parity * half, half, 0, allow_negative_indices=False
+            )
+
+        theirs = lax.ppermute(rows_of(1 - near), ("far", "near", "core"), z_swap)
+        mine = rows_of(near).astype(jnp.float32) + theirs.astype(jnp.float32)
+        sums.append(mine.astype(jnp.bfloat16))
     first = jnp.concatenate(sums, axis=1)
-    first = first.reshape(inner, columns // outer // inner, width)
-    blocks = lax.all_to_all(first, "inner", split_axis=0, concat_axis=0, tiled=True)
+    first = first.reshape(far_z, half // far_z, width)
+    blocks = lax.all_to_all(first, "far", split_axis=0, concat_axis=0, tiled=True)
     return jnp.sum(blocks, axis=0, dtype=jnp.float32)
 
 
 def solution(mesh):
     inner, outer, tensor = (mesh.shape[name] for name in ("inner", "outer", "tensor"))
     fine = Mesh(
-        mesh.devices.reshape(inner, outer // 2, 2, tensor), ("inner", "y", "core", "x")
+        mesh.devices.reshape(inner // 2, 2, outer // 2, 2, tensor),
+        ("far", "near", "y", "core", "x"),
     )
-    in_specs = (P(("inner", "y", "core"), "x"), P(("inner", "y", "core", "x"), None))
-    out_specs = P(("inner", "y", "core"), "x")
+    groups = ("far", "near", "y", "core")
+    in_specs = (P(groups, "x"), P(groups + ("x",), None))
     return jax.shard_map(
-        on_device, mesh=fine, in_specs=in_specs, out_specs=out_specs, check_vma=False
+        on_device, mesh=fine, in_specs=in_specs, out_specs=P(groups, "x"), check_vma=False
     )

time: 125 us -> 127 us (1.016)
  starting transfers between devices: 47.1 us -> 53 us
  blocking collectives: 59.7 us -> 54.1 us
    ppermute x0 -> x2, starting transfers between devices: none -> 5.84 us  [on_device(): theirs = lax.ppermute(rows_of(1 - near), ('far', 'near', 'core'), z_swap)]
    all_to_all x1, blocking collectives: 35.5 us -> 30 us  [on_device(): lax.all_to_all(first, 'far', split_axis=0, concat_axis=0, tiled=True)]
    ppermute x0 -> x2, waiting for transfers between devices: none -> 2.81 us  [on_device(): theirs = lax.ppermute(rows_of(1 - near), ('far', 'near', 'core'), z_swap)]
    ppermute x14, waiting for transfers between devices: 6.07 us -> 4.53 us  [on_device(): lax.ppermute(block, ('y', 'core'), swaps[swap])]
  transfers between devices with their start and end apart: 16 -> 18, of which waited for: 6 -> 7; matrix products, arithmetic and copies ran while one was open for 1% -> 1% of each run, Pallas kernels for 0% -> 0%
where the time goes in v10:
time: 127 us; the launch traced here: 126 us
  blocking collectives  54.1 us (43%)
  starting transfers between devices  53 us (42%)
  waiting for transfers between devices  8.61 us (7%)
  matrix products  6.56 us (5%)
  other arithmetic  1.65 us (1%)
    ppermute x14, starting transfers between devices, on_device(): lax.ppermute(block, ('y', 'core'), swaps[swap])  43.2 us
    all_to_all x1, blocking collectives, on_device(): lax.all_to_all(first, 'far', split_axis=0, concat_axis=0, tiled=True)  30 us
    all_gather x1, blocking collectives, on_device(): grads = lax.all_gather(grads, 'x', axis=1, tiled=True)  24.1 us
    ppermute x2, starting transfers between devices, on_device(): theirs = lax.ppermute(rows_of(1 - near), ('far', 'near', 'core'), z_swap)  5.84 us
    dot_general x1, matrix products, on_device(): lax.dot_general(grads.reshape(tokens.shape[0], columns), tokens, (((0,),...  5.1 us
    ppermute x14, waiting for transfers between devices, on_device(): lax.ppermute(block, ('y', 'core'), swaps[swap])  4.53 us
    ppermute x2, waiting for transfers between devices, on_device(): theirs = lax.ppermute(rows_of(1 - near), ('far', 'near', 'core'), z_swap)  2.81 us
  transfers between devices with their start and end apart: 18, of which 7 were waited for; matrix products, arithmetic and copies ran while one was open for 1% of the time, Pallas kernels for 0%

profile of v10, /device:TPU:6, one launch (start us, length us, event | category | flops | bytes accessed | tf_op | source)
XLA Modules:
  0.0 125.5 jit_solution(7167406380242348567)
XLA Ops:
  0.0 0.9 copy-done
  0.9 1.5 %fusion.38 = bf16[1024,96]{0,1:T(8,128)(2,1)S(1)} fusion(bf16[96,1024]{1,0:T(8,128)(2,1)S(1)} %copy-done, s32[1024]{0:T(1024)S(1)} %get-tuple-element.40, s32[1024]{0:T(1024)S(1)} %get-tuple-element.41, s32[1024]{0:T(1024)S(1)} %get-tuple-element.39, s32[1024]{0:T(1024)S(1)} %get-tuple-element.42, pred[1024]{0:T(1024)(128)(4,1)S(1)} %get-tuple-element.37, ...), kind=kOutput, calls=%fused_computation.58 | convolution fusion | flops 272728064 | bytes 411648 | tf_op jit(solution)/shard_map/dot_general | solution.py:21
  2.4 1.9 %collective-permute-start = (bf16[96,512]{1,0:T(8,128)(2,1)S(1)}, bf16[96,512]{1,0:T(8,128)(2,1)S(1)}, u32[]{:S(2)}, u32[]{:S(2)}) collective-permute-start(bf16[96,512]{1,0:T(8,128)(2,1)S(1)} %get-tuple-element.36), channel_id=1, source_target_pairs={{0,4},{4,0},{1,5},{5,1},{2,6},{6,2},{3,7},{7,3},{8,12},{12,8},{9,1... | collective-permute-start | bytes 294920 | tf_op jit(solution)/shard_map/ppermute | solution.py:40
  4.4 1.3 %collective-permute-done = bf16[96,512]{1,0:T(8,128)(2,1)S(1)} collective-permute-done((bf16[96,512]{1,0:T(8,128)(2,1)S(1)}, bf16[96,512]{1,0:T(8,128)(2,1)S(1)}, u32[]{:S(2)}, u32[]{:S(2)}) %collective-permute-start) | collective-permute-done | bytes 98336 | tf_op jit(solution)/shard_map/ppermute | solution.py:40
  5.6 2.1 %collective-permute-start.1 = (bf16[384,3712]{1,0:T(8,128)(2,1)S(1)}, bf16[384,3712]{1,0:T(8,128)(2,1)}, u32[]{:S(2)}, u32[]{:S(2)}) collective-permute-start(bf16[384,3712]{1,0:T(8,128)(2,1)S(1)} %copy-done.1), channel_id=1, source_target_pairs={{0,4},{4,0},{1,5},{5,1},{2,6},{6,2},{3,7},{7,3},{8,12},{12,8},{9,1... | collective-permute-start | bytes 8552456 | tf_op jit(solution)/shard_map/ppermute | solution.py:42
  7.8 24.1 %all_gather.3 = bf16[2,384,512]{2,1,0:T(8,128)(2,1)S(1)} all-gather(bf16[2,96,512]{2,1,0:T(8,128)(2,1)S(1)} %pad_maximum_fusion.1), channel_id=1, replica_groups=mesh['far'=8,'near'=2,'y'=8,'core'=2,'x'=4] {'x'}, dimensions={1}, use_global_device_ids=true | all-gather | bytes 983040 | tf_op jit(solution)/shard_map/all_gather | solution.py:44
  31.9 0.0 collective-permute-done.1
  31.9 5.1 %convolution_convert_fusion = bf16[512,3712]{1,0:T(8,128)(2,1)S(1)} fusion(bf16[768,512]{1,0:T(8,128)(2,1)S(1)} %bitcast.69, bf16[384,3712]{1,0:T(8,128)(2,1)} %collective-permute-done.1, bf16[384,3712]{1,0:T(8,128)(2,1)S(1)} %copy-done.1), kind=kOutput, calls=%fused_computation.18 | convolution fusion | flops 2932539392 | bytes 10289152 | tf_op jit(solution)/shard_map/dot_general | solution.py:46
  37.1 1.9 %collective-permute-start.10 = (bf16[64,1792]{1,0:T(8,128)(2,1)S(1)}, bf16[64,1792]{1,0:T(8,128)(2,1)S(1)}, u32[]{:S(2)}, u32[]{:S(2)}) collective-permute-start(bf16[64,1792]{1,0:T(8,128)(2,1)S(1)} %get-tuple-element.33), channel_id=1, source_target_pairs={{0,56},{4,12},{8,16},{12,4},{16,8},{20,28},{24,32},{28,20},{32,24}... | collective-permute-start | bytes 688136 | tf_op jit(solution)/shard_map/ppermute | solution.py:91
  39.0 1.9 %collective-permute-start.2 = (bf16[64,1920]{1,0:T(8,128)(2,1)S(1)}, bf16[64,1920]{1,0:T(8,128)(2,1)S(1)}, u32[]{:S(2)}, u32[]{:S(2)}) collective-permute-start(bf16[64,1920]{1,0:T(8,128)(2,1)S(1)} %get-tuple-element.20), channel_id=1, source_target_pairs={{0,8},{4,60},{8,0},{12,20},{16,24},{20,12},{24,16},{28,36},{32,40}... | collective-permute-start | bytes 737288 | tf_op jit(solution)/shard_map/ppermute | solution.py:91
  41.0 5.1 %collective-permute-start.12 = (bf16[64,1792]{1,0:T(8,128)(2,1)S(1)}, bf16[64,1792]{1,0:T(8,128)(2,1)S(1)}, u32[]{:S(2)}, u32[]{:S(2)}) collective-permute-start(bf16[64,1792]{1,0:T(8,128)(2,1)S(1)} %get-tuple-element.25), channel_id=1, source_target_pairs={{0,56},{4,12},{8,16},{12,4},{16,8},{20,28},{24,32},{28,20},{32,24}... | collective-permute-start | bytes 688136 | tf_op jit(solution)/shard_map/ppermute | solution.py:91
  46.1 1.9 %collective-permute-start.3 = (bf16[64,1920]{1,0:T(8,128)(2,1)S(1)}, bf16[64,1920]{1,0:T(8,128)(2,1)S(1)}, u32[]{:S(2)}, u32[]{:S(2)}) collective-permute-start(bf16[64,1920]{1,0:T(8,128)(2,1)S(1)} %get-tuple-element.31), channel_id=1, source_target_pairs={{0,8},{4,60},{8,0},{12,20},{16,24},{20,12},{24,16},{28,36},{32,40}... | collective-permute-start | bytes 737288 | tf_op jit(solution)/shard_map/ppermute | solution.py:91
  48.0 0.6 collective-permute-done.10
  48.6 0.1 fusion.50
  48.7 3.3 %collective-permute-start.11 = (bf16[64,1792]{1,0:T(8,128)(2,1)S(1)}, bf16[64,1792]{1,0:T(8,128)(2,1)S(1)}, u32[]{:S(2)}, u32[]{:S(2)}) collective-permute-start(bf16[64,1792]{1,0:T(8,128)(2,1)S(1)} %fusion.50), channel_id=1, source_target_pairs={{0,8},{4,60},{8,0},{12,20},{16,24},{20,12},{24,16},{28,36},{32,40}... | collective-permute-start | bytes 688136 | tf_op jit(solution)/shard_map/ppermute | solution.py:91
  52.1 1.3 %collective-permute-done.12 = bf16[64,1792]{1,0:T(8,128)(2,1)S(1)} collective-permute-done((bf16[64,1792]{1,0:T(8,128)(2,1)S(1)}, bf16[64,1792]{1,0:T(8,128)(2,1)S(1)}, u32[]{:S(2)}, u32[]{:S(2)}) %collective-permute-start.12) | collective-permute-done | bytes 229408 | tf_op jit(solution)/shard_map/ppermute | solution.py:91
  53.3 0.1 fusion.49
  53.4 1.9 %collective-permute-start.14 = (bf16[64,1792]{1,0:T(8,128)(2,1)S(1)}, bf16[64,1792]{1,0:T(8,128)(2,1)S(1)}, u32[]{:S(2)}, u32[]{:S(2)}) collective-permute-start(bf16[64,1792]{1,0:T(8,128)(2,1)S(1)} %fusion.49), channel_id=1, source_target_pairs={{0,8},{4,60},{8,0},{12,20},{16,24},{20,12},{24,16},{28,36},{32,40}... | collective-permute-start | bytes 688136 | tf_op jit(solution)/shard_map/ppermute | solution.py:91
  55.3 0.0 collective-permute-done.3
  55.3 0.1 fusion.43
  55.4 5.1 %collective-permute-start.5 = (bf16[64,1920]{1,0:T(8,128)(2,1)S(1)}, bf16[64,1920]{1,0:T(8,128)(2,1)S(1)}, u32[]{:S(2)}, u32[]{:S(2)}) collective-permute-start(bf16[64,1920]{1,0:T(8,128)(2,1)S(1)} %fusion.43), channel_id=1, source_target_pairs={{0,56},{4,12},{8,16},{12,4},{16,8},{20,28},{24,32},{28,20},{32,24}... | collective-permute-start | bytes 737288 | tf_op jit(solution)/shard_map/ppermute | solution.py:91
  60.5 0.0 collective-permute-done.2
  60.5 0.1 fusion.44
  60.6 1.9 %collective-permute-start.4 = (bf16[64,1920]{1,0:T(8,128)(2,1)S(1)}, bf16[64,1920]{1,0:T(8,128)(2,1)S(1)}, u32[]{:S(2)}, u32[]{:S(2)}) collective-permute-start(bf16[64,1920]{1,0:T(8,128)(2,1)S(1)} %fusion.44), channel_id=1, source_target_pairs={{0,56},{4,12},{8,16},{12,4},{16,8},{20,28},{24,32},{28,20},{32,24}... | collective-permute-start | bytes 737288 | tf_op jit(solution)/shard_map/ppermute | solution.py:91
  62.5 0.0 collective-permute-done.11
  62.6 0.1 fusion.51
  62.6 5.1 %collective-permute-start.13 = (bf16[64,1792]{1,0:T(8,128)(2,1)S(1)}, bf16[64,1792]{1,0:T(8,128)(2,1)S(1)}, u32[]{:S(2)}, u32[]{:S(2)}) collective-permute-start(bf16[64,1792]{1,0:T(8,128)(2,1)S(1)} %fusion.51), channel_id=1, source_target_pairs={{0,56},{4,12},{8,16},{12,4},{16,8},{20,28},{24,32},{28,20},{32,24}... | collective-permute-start | bytes 688136 | tf_op jit(solution)/shard_map/ppermute | solution.py:91
  67.8 0.1 fusion.48
  67.8 1.9 %collective-permute-start.16 = (bf16[64,1792]{1,0:T(8,128)(2,1)S(1)}, bf16[64,1792]{1,0:T(8,128)(2,1)S(1)}, u32[]{:S(2)}, u32[]{:S(2)}) collective-permute-start(bf16[64,1792]{1,0:T(8,128)(2,1)S(1)} %fusion.48), channel_id=1, source_target_pairs={{0,56},{4,12},{8,16},{12,4},{16,8},{20,28},{24,32},{28,20},{32,24}... | collective-permute-start | bytes 688136 | tf_op jit(solution)/shard_map/ppermute | solution.py:91
  69.8 0.1 fusion.42
  69.9 1.9 %collective-permute-start.7 = (bf16[64,1920]{1,0:T(8,128)(2,1)S(1)}, bf16[64,1920]{1,0:T(8,128)(2,1)S(1)}, u32[]{:S(2)}, u32[]{:S(2)}) collective-permute-start(bf16[64,1920]{1,0:T(8,128)(2,1)S(1)} %fusion.42), channel_id=1, source_target_pairs={{0,8},{4,60},{8,0},{12,20},{16,24},{20,12},{24,16},{28,36},{32,40}... | collective-permute-start | bytes 737288 | tf_op jit(solution)/shard_map/ppermute | solution.py:91
  71.8 0.1 fusion.45
  71.9 3.9 %collective-permute-start.6 = (bf16[64,1920]{1,0:T(8,128)(2,1)S(1)}, bf16[64,1920]{1,0:T(8,128)(2,1)S(1)}, u32[]{:S(2)}, u32[]{:S(2)}) collective-permute-start(bf16[64,1920]{1,0:T(8,128)(2,1)S(1)} %fusion.45), channel_id=1, source_target_pairs={{0,8},{4,60},{8,0},{12,20},{16,24},{20,12},{24,16},{28,36},{32,40}... | collective-permute-start | bytes 737288 | tf_op jit(solution)/shard_map/ppermute | solution.py:91
  75.8 0.1 fusion.52
  75.9 1.9 %collective-permute-start.15 = (bf16[64,1792]{1,0:T(8,128)(2,1)S(1)}, bf16[64,1792]{1,0:T(8,128)(2,1)S(1)}, u32[]{:S(2)}, u32[]{:S(2)}) collective-permute-start(bf16[64,1792]{1,0:T(8,128)(2,1)S(1)} %fusion.52), channel_id=1, source_target_pairs={{0,8},{4,60},{8,0},{12,20},{16,24},{20,12},{24,16},{28,36},{32,40}... | collective-permute-start | bytes 688136 | tf_op jit(solution)/shard_map/ppermute | solution.py:91
  77.8 0.1 collective-permute-done.7
  77.9 0.1 fusion.41
  78.0 5.1 %collective-permute-start.8 = (bf16[64,1920]{1,0:T(8,128)(2,1)S(1)}, bf16[64,1920]{1,0:T(8,128)(2,1)S(1)}, u32[]{:S(2)}, u32[]{:S(2)}) collective-permute-start(bf16[64,1920]{1,0:T(8,128)(2,1)S(1)} %fusion.41), channel_id=1, source_target_pairs={{0,56},{4,12},{8,16},{12,4},{16,8},{20,28},{24,32},{28,20},{32,24}... | collective-permute-start | bytes 737288 | tf_op jit(solution)/shard_map/ppermute | solution.py:91
  83.2 2.5 %collective-permute-done.15 = bf16[64,1792]{1,0:T(8,128)(2,1)S(1)} collective-permute-done((bf16[64,1792]{1,0:T(8,128)(2,1)S(1)}, bf16[64,1792]{1,0:T(8,128)(2,1)S(1)}, u32[]{:S(2)}, u32[]{:S(2)}) %collective-permute-start.15) | collective-permute-done | bytes 229408 | tf_op jit(solution)/shard_map/ppermute | solution.py:91
  85.7 0.1 fusion.54
  85.8 1.9 %collective-permute-start.17 = (bf16[32,1792]{1,0:T(8,128)(2,1)S(1)}, bf16[32,1792]{1,0:T(8,128)(2,1)S(1)}, u32[]{:S(2)}, u32[]{:S(2)}) collective-permute-start(bf16[32,1792]{1,0:T(8,128)(2,1)S(1)} %constant_dynamic-slice_fusion), channel_id=1, source_target_pairs={{0,64},{4,964},{64,0},{68,132},{128,192},{132,68},{192,128},{196,2... | collective-permute-start | bytes 344072 | tf_op jit(solution)/shard_map/ppermute | solution.py:109
  87.7 0.1 fusion.47
  87.9 3.9 %collective-permute-start.9 = (bf16[32,1920]{1,0:T(8,128)(2,1)S(1)}, bf16[32,1920]{1,0:T(8,128)(2,1)S(1)}, u32[]{:S(2)}, u32[]{:S(2)}) collective-permute-start(bf16[32,1920]{1,0:T(8,128)(2,1)S(1)} %constant_dynamic-slice_fusion.1), channel_id=1, source_target_pairs={{0,64},{4,964},{64,0},{68,132},{128,192},{132,68},{192,128},{196,2... | collective-permute-start | bytes 368648 | tf_op jit(solution)/shard_map/ppermute | solution.py:109
  91.8 0.7 collective-permute-done.17
  92.5 2.1 %collective-permute-done.9 = bf16[32,1920]{1,0:T(8,128)(2,1)S(1)} collective-permute-done((bf16[32,1920]{1,0:T(8,128)(2,1)S(1)}, bf16[32,1920]{1,0:T(8,128)(2,1)S(1)}, u32[]{:S(2)}, u32[]{:S(2)}) %collective-permute-start.9) | collective-permute-done | bytes 122912 | tf_op jit(solution)/shard_map/ppermute | solution.py:109
  94.7 0.1 reshape.35
  94.8 30.0 %all_to_all.5 = bf16[8,4,3712]{2,1,0:T(4,128)(2,1)S(1)} all-to-all(bf16[8,4,3712]{2,1,0:T(4,128)(2,1)S(1)} %reshape.35), channel_id=1, replica_groups=mesh['far'=8,'near'=2,'y'=8,'core'=2,'x'=4] {'far'}, dimensions={0} | all-to-all | bytes 475136 | tf_op jit(solution)/shard_map/all_to_all | solution.py:114
  124.8 0.7 convert_reduce_fusion
  (22 shorter events, 0.3 us)
Async XLA Ops:
  0.0 0.9 copy-start
  0.9 4.7 %copy-start.1 = (bf16[384,3712]{1,0:T(8,128)(2,1)S(1)}, bf16[384,3712]{1,0:T(8,128)(2,1)}, u32[]{:S(2)}) copy-start(bf16[384,3712]{1,0:T(8,128)(2,1)} %param.2) | copy-start | bytes 8552452
  2.4 3.2 %collective-permute-start = (bf16[96,512]{1,0:T(8,128)(2,1)S(1)}, bf16[96,512]{1,0:T(8,128)(2,1)S(1)}, u32[]{:S(2)}, u32[]{:S(2)}) collective-permute-start(bf16[96,512]{1,0:T(8,128)(2,1)S(1)} %get-tuple-element.36), channel_id=1, source_target_pairs={{0,4},{4,0},{1,5},{5,1},{2,6},{6,2},{3,7},{7,3},{8,12},{12,8},{9,1... | collective-permute-start | bytes 294920 | tf_op jit(solution)/shard_map/ppermute | solution.py:40
  5.6 26.3 %collective-permute-start.1 = (bf16[384,3712]{1,0:T(8,128)(2,1)S(1)}, bf16[384,3712]{1,0:T(8,128)(2,1)}, u32[]{:S(2)}, u32[]{:S(2)}) collective-permute-start(bf16[384,3712]{1,0:T(8,128)(2,1)S(1)} %copy-done.1), channel_id=1, source_target_pairs={{0,4},{4,0},{1,5},{5,1},{2,6},{6,2},{3,7},{7,3},{8,12},{12,8},{9,1... | collective-permute-start | bytes 8552456 | tf_op jit(solution)/shard_map/ppermute | solution.py:42
  37.1 11.6 %collective-permute-start.10 = (bf16[64,1792]{1,0:T(8,128)(2,1)S(1)}, bf16[64,1792]{1,0:T(8,128)(2,1)S(1)}, u32[]{:S(2)}, u32[]{:S(2)}) collective-permute-start(bf16[64,1792]{1,0:T(8,128)(2,1)S(1)} %get-tuple-element.33), channel_id=1, source_target_pairs={{0,56},{4,12},{8,16},{12,4},{16,8},{20,28},{24,32},{28,20},{32,24}... | collective-permute-start | bytes 688136 | tf_op jit(solution)/shard_map/ppermute | solution.py:91
  39.0 21.5 %collective-permute-start.2 = (bf16[64,1920]{1,0:T(8,128)(2,1)S(1)}, bf16[64,1920]{1,0:T(8,128)(2,1)S(1)}, u32[]{:S(2)}, u32[]{:S(2)}) collective-permute-start(bf16[64,1920]{1,0:T(8,128)(2,1)S(1)} %get-tuple-element.20), channel_id=1, source_target_pairs={{0,8},{4,60},{8,0},{12,20},{16,24},{20,12},{24,16},{28,36},{32,40}... | collective-permute-start | bytes 737288 | tf_op jit(solution)/shard_map/ppermute | solution.py:91
  41.0 12.3 %collective-permute-start.12 = (bf16[64,1792]{1,0:T(8,128)(2,1)S(1)}, bf16[64,1792]{1,0:T(8,128)(2,1)S(1)}, u32[]{:S(2)}, u32[]{:S(2)}) collective-permute-start(bf16[64,1792]{1,0:T(8,128)(2,1)S(1)} %get-tuple-element.25), channel_id=1, source_target_pairs={{0,56},{4,12},{8,16},{12,4},{16,8},{20,28},{24,32},{28,20},{32,24}... | collective-permute-start | bytes 688136 | tf_op jit(solution)/shard_map/ppermute | solution.py:91
  46.1 9.2 %collective-permute-start.3 = (bf16[64,1920]{1,0:T(8,128)(2,1)S(1)}, bf16[64,1920]{1,0:T(8,128)(2,1)S(1)}, u32[]{:S(2)}, u32[]{:S(2)}) collective-permute-start(bf16[64,1920]{1,0:T(8,128)(2,1)S(1)} %get-tuple-element.31), channel_id=1, source_target_pairs={{0,8},{4,60},{8,0},{12,20},{16,24},{20,12},{24,16},{28,36},{32,40}... | collective-permute-start | bytes 737288 | tf_op jit(solution)/shard_map/ppermute | solution.py:91
  48.7 13.8 %collective-permute-start.11 = (bf16[64,1792]{1,0:T(8,128)(2,1)S(1)}, bf16[64,1792]{1,0:T(8,128)(2,1)S(1)}, u32[]{:S(2)}, u32[]{:S(2)}) collective-permute-start(bf16[64,1792]{1,0:T(8,128)(2,1)S(1)} %fusion.50), channel_id=1, source_target_pairs={{0,8},{4,60},{8,0},{12,20},{16,24},{20,12},{24,16},{28,36},{32,40}... | collective-permute-start | bytes 688136 | tf_op jit(solution)/shard_map/ppermute | solution.py:91
  53.4 14.4 %collective-permute-start.14 = (bf16[64,1792]{1,0:T(8,128)(2,1)S(1)}, bf16[64,1792]{1,0:T(8,128)(2,1)S(1)}, u32[]{:S(2)}, u32[]{:S(2)}) collective-permute-start(bf16[64,1792]{1,0:T(8,128)(2,1)S(1)} %fusion.49), channel_id=1, source_target_pairs={{0,8},{4,60},{8,0},{12,20},{16,24},{20,12},{24,16},{28,36},{32,40}... | collective-permute-start | bytes 688136 | tf_op jit(solution)/shard_map/ppermute | solution.py:91
  55.4 14.4 %collective-permute-start.5 = (bf16[64,1920]{1,0:T(8,128)(2,1)S(1)}, bf16[64,1920]{1,0:T(8,128)(2,1)S(1)}, u32[]{:S(2)}, u32[]{:S(2)}) collective-permute-start(bf16[64,1920]{1,0:T(8,128)(2,1)S(1)} %fusion.43), channel_id=1, source_target_pairs={{0,56},{4,12},{8,16},{12,4},{16,8},{20,28},{24,32},{28,20},{32,24}... | collective-permute-start | bytes 737288 | tf_op jit(solution)/shard_map/ppermute | solution.py:91
  60.6 11.2 %collective-permute-start.4 = (bf16[64,1920]{1,0:T(8,128)(2,1)S(1)}, bf16[64,1920]{1,0:T(8,128)(2,1)S(1)}, u32[]{:S(2)}, u32[]{:S(2)}) collective-permute-start(bf16[64,1920]{1,0:T(8,128)(2,1)S(1)} %fusion.44), channel_id=1, source_target_pairs={{0,56},{4,12},{8,16},{12,4},{16,8},{20,28},{24,32},{28,20},{32,24}... | collective-permute-start | bytes 737288 | tf_op jit(solution)/shard_map/ppermute | solution.py:91
  62.6 13.2 %collective-permute-start.13 = (bf16[64,1792]{1,0:T(8,128)(2,1)S(1)}, bf16[64,1792]{1,0:T(8,128)(2,1)S(1)}, u32[]{:S(2)}, u32[]{:S(2)}) collective-permute-start(bf16[64,1792]{1,0:T(8,128)(2,1)S(1)} %fusion.51), channel_id=1, source_target_pairs={{0,56},{4,12},{8,16},{12,4},{16,8},{20,28},{24,32},{28,20},{32,24}... | collective-permute-start | bytes 688136 | tf_op jit(solution)/shard_map/ppermute | solution.py:91
  67.8 15.3 %collective-permute-start.16 = (bf16[64,1792]{1,0:T(8,128)(2,1)S(1)}, bf16[64,1792]{1,0:T(8,128)(2,1)S(1)}, u32[]{:S(2)}, u32[]{:S(2)}) collective-permute-start(bf16[64,1792]{1,0:T(8,128)(2,1)S(1)} %fusion.48), channel_id=1, source_target_pairs={{0,56},{4,12},{8,16},{12,4},{16,8},{20,28},{24,32},{28,20},{32,24}... | collective-permute-start | bytes 688136 | tf_op jit(solution)/shard_map/ppermute | solution.py:91
  69.9 8.1 %collective-permute-start.7 = (bf16[64,1920]{1,0:T(8,128)(2,1)S(1)}, bf16[64,1920]{1,0:T(8,128)(2,1)S(1)}, u32[]{:S(2)}, u32[]{:S(2)}) collective-permute-start(bf16[64,1920]{1,0:T(8,128)(2,1)S(1)} %fusion.42), channel_id=1, source_target_pairs={{0,8},{4,60},{8,0},{12,20},{16,24},{20,12},{24,16},{28,36},{32,40}... | collective-permute-start | bytes 737288 | tf_op jit(solution)/shard_map/ppermute | solution.py:91
  71.9 15.8 %collective-permute-start.6 = (bf16[64,1920]{1,0:T(8,128)(2,1)S(1)}, bf16[64,1920]{1,0:T(8,128)(2,1)S(1)}, u32[]{:S(2)}, u32[]{:S(2)}) collective-permute-start(bf16[64,1920]{1,0:T(8,128)(2,1)S(1)} %fusion.45), channel_id=1, source_target_pairs={{0,8},{4,60},{8,0},{12,20},{16,24},{20,12},{24,16},{28,36},{32,40}... | collective-permute-start | bytes 737288 | tf_op jit(solution)/shard_map/ppermute | solution.py:91
  75.9 9.8 %collective-permute-start.15 = (bf16[64,1792]{1,0:T(8,128)(2,1)S(1)}, bf16[64,1792]{1,0:T(8,128)(2,1)S(1)}, u32[]{:S(2)}, u32[]{:S(2)}) collective-permute-start(bf16[64,1792]{1,0:T(8,128)(2,1)S(1)} %fusion.52), channel_id=1, source_target_pairs={{0,8},{4,60},{8,0},{12,20},{16,24},{20,12},{24,16},{28,36},{32,40}... | collective-permute-start | bytes 688136 | tf_op jit(solution)/shard_map/ppermute | solution.py:91
  78.0 9.7 %collective-permute-start.8 = (bf16[64,1920]{1,0:T(8,128)(2,1)S(1)}, bf16[64,1920]{1,0:T(8,128)(2,1)S(1)}, u32[]{:S(2)}, u32[]{:S(2)}) collective-permute-start(bf16[64,1920]{1,0:T(8,128)(2,1)S(1)} %fusion.41), channel_id=1, source_target_pairs={{0,56},{4,12},{8,16},{12,4},{16,8},{20,28},{24,32},{28,20},{32,24}... | collective-permute-start | bytes 737288 | tf_op jit(solution)/shard_map/ppermute | solution.py:91
  85.8 6.7 %collective-permute-start.17 = (bf16[32,1792]{1,0:T(8,128)(2,1)S(1)}, bf16[32,1792]{1,0:T(8,128)(2,1)S(1)}, u32[]{:S(2)}, u32[]{:S(2)}) collective-permute-start(bf16[32,1792]{1,0:T(8,128)(2,1)S(1)} %constant_dynamic-slice_fusion), channel_id=1, source_target_pairs={{0,64},{4,964},{64,0},{68,132},{128,192},{132,68},{192,128},{196,2... | collective-permute-start | bytes 344072 | tf_op jit(solution)/shard_map/ppermute | solution.py:109
  87.9 6.8 %collective-permute-start.9 = (bf16[32,1920]{1,0:T(8,128)(2,1)S(1)}, bf16[32,1920]{1,0:T(8,128)(2,1)S(1)}, u32[]{:S(2)}, u32[]{:S(2)}) collective-permute-start(bf16[32,1920]{1,0:T(8,128)(2,1)S(1)} %constant_dynamic-slice_fusion.1), channel_id=1, source_target_pairs={{0,64},{4,964},{64,0},{68,132},{128,192},{132,68},{192,128},{196,2... | collective-permute-start | bytes 368648 | tf_op jit(solution)/shard_map/ppermute | solution.py:109
